TPU v7x, 32 devices: a whole 2x2x4 slice. The times are simulated.
32 devices in a mesh: dp: 4 (over x, core), section: 2 (over y), mp: 4 (over z).
Axes of the slice: x: 2, y: 2, z: 4, core: 2. Of those that a mesh axis runs over, the one named last changes fastest.
Arguments:
- inputs: bfloat16 [2, 2048, 1024], P(None, ('dp', 'mp')), may hold values from -6 to 6
- cotangent: bfloat16 [2, 2048, 1024], P(None, ('dp', 'mp')), may hold values from -6 to 6
- doc_ids: int32 [2, 4, 512], P(None, 'dp'), may hold values from 0 to 7, never falling along the last dimension, each value on 1 to 256 neighbouring positions
- w_query: bfloat16 [2, 1024, 1024], P('section', None, 'mp'), may hold values from -0.1875 to 0.1875
- b_query: bfloat16 [2, 1024], P('section', 'mp'), may hold values from -3 to 3
- w_key: bfloat16 [2, 1024, 1024], P('section', None, 'mp'), may hold values from -0.1875 to 0.1875
- w_value: bfloat16 [2, 1024, 1024], P('section', None, 'mp'), may hold values from -0.1875 to 0.1875
- b_value: bfloat16 [2, 1024], P('section', 'mp'), may hold values from -3 to 3
- w_out: bfloat16 [2, 1024, 1024], P('section', 'mp'), may hold values from -0.5 to 0.5
- b_out: bfloat16 [2, 1024], P('section'), may hold values from -2 to 2
- gain_one: bfloat16 [2, 1024], P('section'), may hold values from 0.5 to 1.5
- shift_one: bfloat16 [2, 1024], P('section'), may hold values from -2 to 2
- w_up: bfloat16 [2, 1024, 4096], P('section', None, 'mp'), may hold values from -0.1875 to 0.1875
- b_up: bfloat16 [2, 4096], P('section', 'mp'), may hold values from -3 to 3
- w_down: bfloat16 [2, 4096, 1024], P('section', 'mp'), may hold values from -0.09375 to 0.09375
- b_down: bfloat16 [2, 1024], P('section'), may hold values from -2 to 2
- gain_two: bfloat16 [2, 1024], P('section'), may hold values from 0.5 to 1.5
- shift_two: bfloat16 [2, 1024], P('section'), may hold values from -2 to 2
Outputs:
- section_outputs: bfloat16 [2, 2, 2048, 1024], P('section', None, ('dp', 'mp'))
- section_input_grads: float32 [2, 2, 2048, 1024], P('section', None, ('dp', 'mp'))
- grad_w_query: float32 [2, 1024, 1024], P('section', None, 'mp')
- grad_b_query: float32 [2, 1024], P('section', 'mp')
- grad_w_key: float32 [2, 1024, 1024], P('section', None, 'mp')
- grad_w_value: float32 [2, 1024, 1024], P('section', None, 'mp')
- grad_b_value: float32 [2, 1024], P('section', 'mp')
- grad_w_out: float32 [2, 1024, 1024], P('section', 'mp')
- grad_b_out: float32 [2, 1024], P('section')
- grad_gain_one: float32 [2, 1024], P('section')
- grad_shift_one: float32 [2, 1024], P('section')
- grad_w_up: float32 [2, 1024, 4096], P('section', None, 'mp')
- grad_b_up: float32 [2, 4096], P('section', 'mp')
- grad_w_down: float32 [2, 4096, 1024], P('section', 'mp')
- grad_b_down: float32 [2, 1024], P('section')
- grad_gain_two: float32 [2, 1024], P('section')
- grad_shift_two: float32 [2, 1024], P('section')
Inputs may be any that keep to these rules, and one draw needn't show every extreme that they name: `doc_ids`: within each row of 512 tokens the ids never fall.
All inputs are finite; a program needn't handle non-finite values.
Results may differ from a plain program's by a relative error of at most 0.03.
Values may be sent and summed in bfloat16 or wider, within the bound.
No kernel may reach another device: no remote copies, remote signals or barrier semaphores. Data moves between devices by JAX's collectives and lax.ppermute only.
A program may use at most 128 MiB of HBM per device.

v0:
```python
from functools import partial

import jax
import jax.numpy as jnp
from jax import lax
from jax.sharding import PartitionSpec as P

HD = 64
SEQ = 512
MICRO = 2


EPSILON = 1e-05
NEGATIVE = -1e30


def from_behind(shard, axis, by):
    peers = lax.axis_size(axis)
    pairs = [(i, i + by) for i in range(peers) if 0 <= i + by < peers]
    return lax.ppermute(shard, axis, pairs)


def for_sending(shard):
    return jax.tree.map(lambda a: a.astype(jnp.bfloat16) if a.dtype == jnp.float32 else a, shard)


def norm_forward(hidden, gain, offset):
    centre = jnp.mean(hidden, -1, keepdims=True)
    centred = hidden - centre
    variance = jnp.mean(centred * centred, -1, keepdims=True)
    inverse = lax.rsqrt(variance + EPSILON)
    normed = centred * inverse
    return (normed * gain + offset, normed, inverse)


def norm_backward(upstream, normed, inverse, gain):
    scaled = upstream * gain
    return inverse * (
        scaled
        - jnp.mean(scaled, -1, keepdims=True)
        - normed * jnp.mean(scaled * normed, -1, keepdims=True)
    )


def split_heads(values, batch_rows):
    return values.reshape(batch_rows, SEQ, -1, HD)


def layer_forward(share_rows, weights, allowed):
    (
        w_query,
        b_query,
        w_key,
        w_value,
        b_value,
        w_out,
        b_out,
        gain_one,
        shift_one,
        w_up,
        b_up,
        w_down,
        b_down,
        gain_two,
        shift_two,
    ) = weights
    whole = lax.all_gather(share_rows, "mp", axis=0, tiled=True)
    batch_rows = whole.shape[0] // SEQ
    query_rows = (jnp.dot(whole, w_query, preferred_element_type=jnp.float32) + b_query).astype(
        jnp.bfloat16
    )
    key_rows = jnp.dot(whole, w_key, preferred_element_type=jnp.float32).astype(jnp.bfloat16)
    value_rows = (jnp.dot(whole, w_value, preferred_element_type=jnp.float32) + b_value).astype(
        jnp.bfloat16
    )
    scores = jnp.einsum(
        "rqhd,rkhd->rhqk",
        split_heads(query_rows, batch_rows),
        split_heads(key_rows, batch_rows),
        preferred_element_type=jnp.float32,
    ) * HD ** (-0.5)
    scores = jnp.where(allowed[:, None], scores, NEGATIVE)
    highest = jnp.max(scores, -1, keepdims=True)
    exponent = jnp.exp(scores - highest)
    probs = exponent / jnp.sum(exponent, -1, keepdims=True)
    probs_low = probs.astype(jnp.bfloat16)
    mixed = (
        jnp.einsum(
            "rhqk,rkhd->rqhd",
            probs_low,
            split_heads(value_rows, batch_rows),
            preferred_element_type=jnp.float32,
        )
        .reshape(whole.shape[0], -1)
        .astype(jnp.bfloat16)
    )
    attended = lax.psum_scatter(
        jnp.dot(mixed, w_out, preferred_element_type=jnp.float32).astype(jnp.bfloat16),
        "mp",
        scatter_dimension=0,
        tiled=True,
    ).astype(jnp.float32)
    middle, normed_one, inverse_one = norm_forward(
        share_rows.astype(jnp.float32) + attended + b_out, gain_one, shift_one
    )
    spread = lax.all_gather(middle.astype(jnp.bfloat16), "mp", axis=0, tiled=True)
    hidden_up = jnp.dot(spread, w_up, preferred_element_type=jnp.float32) + b_up
    activated = jax.nn.gelu(hidden_up, approximate=False).astype(jnp.bfloat16)
    lowered = lax.psum_scatter(
        jnp.dot(activated, w_down, preferred_element_type=jnp.float32).astype(jnp.bfloat16),
        "mp",
        scatter_dimension=0,
        tiled=True,
    ).astype(jnp.float32)
    result, normed_two, inverse_two = norm_forward(middle + lowered + b_down, gain_two, shift_two)
    kept = (
        whole,
        query_rows,
        key_rows,
        value_rows,
        probs,
        probs_low,
        mixed,
        normed_one,
        inverse_one,
        spread,
        hidden_up,
        activated,
        normed_two,
        inverse_two,
    )
    return (result, kept)


def layer_backward(upstream, weights, kept):
    (
        w_query,
        b_query,
        w_key,
        w_value,
        b_value,
        w_out,
        b_out,
        gain_one,
        shift_one,
        w_up,
        b_up,
        w_down,
        b_down,
        gain_two,
        shift_two,
    ) = weights
    (
        whole,
        query_rows,
        key_rows,
        value_rows,
        probs,
        probs_low,
        mixed,
        normed_one,
        inverse_one,
        spread,
        hidden_up,
        activated,
        normed_two,
        inverse_two,
    ) = kept
    batch_rows = whole.shape[0] // SEQ
    grad_gain_two = jnp.sum(upstream * normed_two, 0)
    grad_shift_two = jnp.sum(upstream, 0)
    grad_sum_two = norm_backward(upstream, normed_two, inverse_two, gain_two)
    grad_lowered = lax.all_gather(grad_sum_two.astype(jnp.bfloat16), "mp", axis=0, tiled=True)
    grad_b_down = jnp.sum(grad_lowered.astype(jnp.float32), 0)
    grad_w_down = jnp.einsum(
        "tf,td->fd", activated, grad_lowered, preferred_element_type=jnp.float32
    )
    grad_activated = jnp.einsum(
        "td,fd->tf", grad_lowered, w_down, preferred_element_type=jnp.float32
    )
    unused, gelu_pull = jax.vjp(partial(jax.nn.gelu, approximate=False), hidden_up)
    grad_up = gelu_pull(grad_activated)[0].astype(jnp.bfloat16)
    grad_b_up = jnp.sum(grad_up.astype(jnp.float32), 0)
    grad_w_up = jnp.einsum("td,tf->df", spread, grad_up, preferred_element_type=jnp.float32)
    grad_middle = grad_sum_two + lax.psum_scatter(
        jnp.einsum("tf,df->td", grad_up, w_up, preferred_element_type=jnp.float32).astype(
            jnp.bfloat16
        ),
        "mp",
        scatter_dimension=0,
        tiled=True,
    ).astype(jnp.float32)
    grad_gain_one = jnp.sum(grad_middle * normed_one, 0)
    grad_shift_one = jnp.sum(grad_middle, 0)
    grad_sum_one = norm_backward(grad_middle, normed_one, inverse_one, gain_one)
    grad_attended = lax.all_gather(grad_sum_one.astype(jnp.bfloat16), "mp", axis=0, tiled=True)
    grad_b_out = jnp.sum(grad_attended.astype(jnp.float32), 0)
    grad_w_out = jnp.einsum("te,td->ed", mixed, grad_attended, preferred_element_type=jnp.float32)
    grad_mixed = jnp.einsum(
        "td,ed->te", grad_attended, w_out, preferred_element_type=jnp.float32
    ).astype(jnp.bfloat16)
    mixed_heads = split_heads(grad_mixed, batch_rows)
    query_heads = split_heads(query_rows, batch_rows)
    key_heads = split_heads(key_rows, batch_rows)
    value_heads = split_heads(value_rows, batch_rows)
    grad_probs = jnp.einsum(
        "rqhd,rkhd->rhqk", mixed_heads, value_heads, preferred_element_type=jnp.float32
    )
    grad_scores = (probs * (grad_probs - jnp.sum(probs * grad_probs, -1, keepdims=True))).astype(
        jnp.bfloat16
    )
    scale = HD ** (-0.5)
    token_count = whole.shape[0]
    grad_query = (
        (
            jnp.einsum(
                "rhqk,rkhd->rqhd", grad_scores, key_heads, preferred_element_type=jnp.float32
            )
            * scale
        )
        .reshape(token_count, -1)
        .astype(jnp.bfloat16)
    )
    grad_key = (
        (
            jnp.einsum(
                "rhqk,rqhd->rkhd", grad_scores, query_heads, preferred_element_type=jnp.float32
            )
            * scale
        )
        .reshape(token_count, -1)
        .astype(jnp.bfloat16)
    )
    grad_value = (
        jnp.einsum("rhqk,rqhd->rkhd", probs_low, mixed_heads, preferred_element_type=jnp.float32)
        .reshape(token_count, -1)
        .astype(jnp.bfloat16)
    )
    grad_w_query = jnp.einsum("td,te->de", whole, grad_query, preferred_element_type=jnp.float32)
    grad_w_key = jnp.einsum("td,te->de", whole, grad_key, preferred_element_type=jnp.float32)
    grad_w_value = jnp.einsum("td,te->de", whole, grad_value, preferred_element_type=jnp.float32)
    grad_b_query = jnp.sum(grad_query.astype(jnp.float32), 0)
    grad_b_value = jnp.sum(grad_value.astype(jnp.float32), 0)
    total = jnp.einsum("te,de->td", grad_query, w_query, preferred_element_type=jnp.float32)
    total = total + jnp.einsum("te,de->td", grad_key, w_key, preferred_element_type=jnp.float32)
    grad_input = grad_sum_one + lax.psum_scatter(
        (
            total + jnp.einsum("te,de->td", grad_value, w_value, preferred_element_type=jnp.float32)
        ).astype(jnp.bfloat16),
        "mp",
        scatter_dimension=0,
        tiled=True,
    ).astype(jnp.float32)
    big_grads = (
        grad_w_query,
        grad_b_query,
        grad_w_key,
        grad_w_value,
        grad_b_value,
        grad_w_out,
        grad_b_out,
        grad_w_up,
        grad_b_up,
        grad_w_down,
        grad_b_down,
    )
    small_grads = (grad_gain_one, grad_shift_one, grad_gain_two, grad_shift_two)
    return (big_grads, small_grads, grad_input)


def per_device(
    inputs,
    cotangent,
    doc_ids,
    w_query,
    b_query,
    w_key,
    w_value,
    b_value,
    w_out,
    b_out,
    gain_one,
    shift_one,
    w_up,
    b_up,
    w_down,
    b_down,
    gain_two,
    shift_two,
):
    weights = tuple(
        (
            w[0]
            for w in (
                w_query,
                b_query,
                w_key,
                w_value,
                b_value,
                w_out,
                b_out,
                gain_one,
                shift_one,
                w_up,
                b_up,
                w_down,
                b_down,
                gain_two,
                shift_two,
            )
        )
    )
    first_section = lax.axis_index("section") == 0
    allowed_all = [
        doc_ids[index][:, :, None] == doc_ids[index][:, None, :] for index in range(MICRO)
    ]
    received = jnp.zeros_like(inputs[0])
    kept_in = []
    kept_allowed = []
    kept_out = []
    for moment in range(MICRO + 1):
        own_rows = inputs[min(moment, MICRO - 1)]
        share_rows = jnp.where(first_section, own_rows, received)
        allowed = jnp.where(
            first_section, allowed_all[min(moment, MICRO - 1)], allowed_all[max(moment - 1, 0)]
        )
        result, kept = layer_forward(share_rows, weights, allowed)
        layer_out = result.astype(jnp.bfloat16)
        kept_in.append(share_rows)
        kept_allowed.append(allowed)
        kept_out.append(layer_out)
        if moment < MICRO:
            received = from_behind(layer_out, "section", 1)
    big_index = (0, 1, 2, 3, 4, 5, 6, 9, 10, 11, 12)
    small_index = (7, 8, 13, 14)
    big_total = tuple((jnp.zeros(weights[index].shape, jnp.float32) for index in big_index))
    small_total = tuple((jnp.zeros(weights[index].shape, jnp.float32) for index in small_index))
    returned = jnp.zeros_like(inputs[0])
    grads_in = []
    for moment in range(MICRO + 1):
        index_first = max(moment - 1, 0)
        index_second = min(moment + 1, MICRO)
        share_rows = jnp.where(first_section, kept_in[index_first], kept_in[index_second])
        allowed = jnp.where(first_section, kept_allowed[index_first], kept_allowed[index_second])
        kept = layer_forward(share_rows, weights, allowed)[1]
        if moment < MICRO:
            own_grad = cotangent[moment].astype(jnp.float32)
        else:
            own_grad = jnp.zeros(cotangent[0].shape, jnp.float32)
        upstream = jnp.where(first_section, returned.astype(jnp.float32), own_grad)
        big_grads, small_grads, grad_input = layer_backward(upstream, weights, kept)
        big_total = jax.tree.map(jnp.add, big_total, big_grads)
        small_total = jax.tree.map(jnp.add, small_total, small_grads)
        grads_in.append(grad_input)
        if moment < MICRO:
            returned = from_behind(grad_input.astype(jnp.bfloat16), "section", -1)
    big_sum = jax.tree.map(
        lambda part: part.astype(jnp.float32), lax.psum(for_sending(big_total), "dp")
    )
    small_sum = lax.psum(small_total, ("dp", "mp"))
    section_outputs = jnp.stack(
        [jnp.where(first_section, kept_out[index], kept_out[index + 1]) for index in range(MICRO)]
    )[None]
    section_input_grads = jnp.stack(
        [jnp.where(first_section, grads_in[index + 1], grads_in[index]) for index in range(MICRO)]
    )[None]
    return (
        section_outputs,
        section_input_grads,
        big_sum[0][None],
        big_sum[1][None],
        big_sum[2][None],
        big_sum[3][None],
        big_sum[4][None],
        big_sum[5][None],
        big_sum[6][None],
        small_sum[0][None],
        small_sum[1][None],
        big_sum[7][None],
        big_sum[8][None],
        big_sum[9][None],
        big_sum[10][None],
        small_sum[2][None],
        small_sum[3][None],
    )


def solution(mesh):
    return jax.shard_map(
        per_device,
        mesh=mesh,
        in_specs=(
            P(None, ("dp", "mp"), None),
            P(None, ("dp", "mp"), None),
            P(None, "dp", None),
            P("section", None, "mp"),
            P("section", "mp"),
            P("section", None, "mp"),
            P("section", None, "mp"),
            P("section", "mp"),
            P("section", "mp", None),
            P("section", None),
            P("section", None),
            P("section", None),
            P("section", None, "mp"),
            P("section", "mp"),
            P("section", "mp", None),
            P("section", None),
            P("section", None),
            P("section", None),
        ),
        out_specs=(
            P("section", None, ("dp", "mp"), None),
            P("section", None, ("dp", "mp"), None),
            P("section", None, "mp"),
            P("section", "mp"),
            P("section", None, "mp"),
            P("section", None, "mp"),
            P("section", "mp"),
            P("section", "mp", None),
            P("section", None),
            P("section", None),
            P("section", None),
            P("section", None, "mp"),
            P("section", "mp"),
            P("section", "mp", None),
            P("section", None),
            P("section", None),
            P("section", None),
        ),
        check_vma=False,
    )
```

profile of v0, /device:TPU:0, one launch (start us, length us, event | category | flops | bytes accessed | tf_op | source)
XLA Modules:
  0.0 1336.8 jit_solution(7459970369877476238)
XLA Ops:
  13.2 27.7 %all-gather.54.cloned.1.call-done = bf16[1,512,1024]{2,1,0:T(8,128)(2,1)} async-done(((bf16[1,128,1024]{2,1,0:T(8,128)(2,1)}), bf16[1,512,1024]{2,1,0:T(8,128)(2,1)}) %all-gather.54.cloned.1.call-update) | async-done | bytes 1048592 | tf_op jit(solution)/shard_map/all_gather | solution.py:67
  55.9 26.7 %reduce-scatter.19.cloned.1.call-done = bf16[128,1024]{1,0:T(8,128)(2,1)} async-done(((bf16[512,1024]{1,0:T(8,128)(2,1)}), bf16[128,1024]{1,0:T(8,128)(2,1)}) %reduce-scatter.19.cloned.1.call-update) | async-done | bytes 262160 | tf_op jit(solution)/shard_map/reduce_scatter | solution.py:97
  87.1 26.7 %all-gather.20.cloned.1.call-done = bf16[512,1024]{1,0:T(8,128)(2,1)} async-done(((bf16[128,1024]{1,0:T(8,128)(2,1)}), bf16[512,1024]{1,0:T(8,128)(2,1)}) %all-gather.20.cloned.1.call-update) | async-done | bytes 1048592 | tf_op jit(solution)/shard_map/all_gather | solution.py:106
  123.4 26.5 %reduce-scatter.21.cloned.1.call-done = bf16[128,1024]{1,0:T(8,128)(2,1)} async-done(((bf16[512,1024]{1,0:T(8,128)(2,1)}), bf16[128,1024]{1,0:T(8,128)(2,1)}) %reduce-scatter.21.cloned.1.call-update) | async-done | bytes 262160 | tf_op jit(solution)/shard_map/reduce_scatter | solution.py:109
  161.4 27.9 %all-gather.34.cloned.1.call-done = bf16[512,1024]{1,0:T(8,128)(2,1)} async-done(((bf16[128,1024]{1,0:T(8,128)(2,1)}), bf16[512,1024]{1,0:T(8,128)(2,1)}) %all-gather.34.cloned.1.call-update) | async-done | bytes 1048592 | tf_op jit(solution)/shard_map/all_gather | solution.py:67
  205.3 26.7 %reduce-scatter.35.cloned.1.call-done = bf16[128,1024]{1,0:T(8,128)(2,1)} async-done(((bf16[512,1024]{1,0:T(8,128)(2,1)}), bf16[128,1024]{1,0:T(8,128)(2,1)}) %reduce-scatter.35.cloned.1.call-update) | async-done | bytes 262160 | tf_op jit(solution)/shard_map/reduce_scatter | solution.py:97
  237.0 25.9 %all-gather.36.cloned.1.call-done = bf16[512,1024]{1,0:T(8,128)(2,1)} async-done(((bf16[128,1024]{1,0:T(8,128)(2,1)}), bf16[512,1024]{1,0:T(8,128)(2,1)}) %all-gather.36.cloned.1.call-update) | async-done | bytes 1048592 | tf_op jit(solution)/shard_map/all_gather | solution.py:106
  294.6 27.1 %reduce-scatter.37.cloned.1.call-done = bf16[128,1024]{1,0:T(8,128)(2,1)} async-done(((bf16[512,1024]{1,0:T(8,128)(2,1)}), bf16[128,1024]{1,0:T(8,128)(2,1)}) %reduce-scatter.37.cloned.1.call-update) | async-done | bytes 262160 | tf_op jit(solution)/shard_map/reduce_scatter | solution.py:109
  382.5 28.7 %reduce-scatter.39.cloned.1.call-done = bf16[128,1024]{1,0:T(8,128)(2,1)} async-done(((bf16[512,1024]{1,0:T(8,128)(2,1)}), bf16[128,1024]{1,0:T(8,128)(2,1)}) %reduce-scatter.39.cloned.1.call-update) | async-done | bytes 262160 | tf_op jit(solution)/shard_map/reduce_scatter | solution.py:185
  416.3 26.3 %all-gather.24.cloned.1.call-done = bf16[512,1024]{1,0:T(8,128)(2,1)} async-done(((bf16[128,1024]{1,0:T(8,128)(2,1)}), bf16[512,1024]{1,0:T(8,128)(2,1)}) %all-gather.24.cloned.1.call-update) | async-done | bytes 1048592 | tf_op jit(solution)/shard_map/all_gather | solution.py:106
  451.8 26.7 %reduce-scatter.25.cloned.1.call-done = bf16[128,1024]{1,0:T(8,128)(2,1)} async-done(((bf16[512,1024]{1,0:T(8,128)(2,1)}), bf16[128,1024]{1,0:T(8,128)(2,1)}) %reduce-scatter.25.cloned.1.call-update) | async-done | bytes 262160 | tf_op jit(solution)/shard_map/reduce_scatter | solution.py:109
  492.6 27.9 %all-gather.30.cloned.1.call-done = bf16[512,1024]{1,0:T(8,128)(2,1)} async-done(((bf16[128,1024]{1,0:T(8,128)(2,1)}), bf16[512,1024]{1,0:T(8,128)(2,1)}) %all-gather.30.cloned.1.call-update) | async-done | bytes 1048592 | tf_op jit(solution)/shard_map/all_gather | solution.py:67
  537.1 26.7 %reduce-scatter.31.cloned.1.call-done = bf16[128,1024]{1,0:T(8,128)(2,1)} async-done(((bf16[512,1024]{1,0:T(8,128)(2,1)}), bf16[128,1024]{1,0:T(8,128)(2,1)}) %reduce-scatter.31.cloned.1.call-update) | async-done | bytes 262160 | tf_op jit(solution)/shard_map/reduce_scatter | solution.py:97
  568.2 26.5 %all-gather.32.cloned.1.call-done = bf16[512,1024]{1,0:T(8,128)(2,1)} async-done(((bf16[128,1024]{1,0:T(8,128)(2,1)}), bf16[512,1024]{1,0:T(8,128)(2,1)}) %all-gather.32.cloned.1.call-update) | async-done | bytes 1048592 | tf_op jit(solution)/shard_map/all_gather | solution.py:106
  606.4 26.7 %reduce-scatter.33.cloned.1.call-done = bf16[128,1024]{1,0:T(8,128)(2,1)} async-done(((bf16[512,1024]{1,0:T(8,128)(2,1)}), bf16[128,1024]{1,0:T(8,128)(2,1)}) %reduce-scatter.33.cloned.1.call-update) | async-done | bytes 262160 | tf_op jit(solution)/shard_map/reduce_scatter | solution.py:109
  636.7 26.1 %all-gather.40.cloned.1.call-done = bf16[512,1024]{1,0:T(8,128)(2,1)} async-done(((bf16[128,1024]{1,0:T(8,128)(2,1)}), bf16[512,1024]{1,0:T(8,128)(2,1)}) %all-gather.40.cloned.1.call-update) | async-done | bytes 1048592 | tf_op jit(solution)/shard_map/all_gather | solution.py:196
  694.5 26.9 %reduce-scatter.41.cloned.1.call-done = bf16[128,1024]{1,0:T(8,128)(2,1)} async-done(((bf16[512,1024]{1,0:T(8,128)(2,1)}), bf16[128,1024]{1,0:T(8,128)(2,1)}) %reduce-scatter.41.cloned.1.call-update) | async-done | bytes 262160 | tf_op jit(solution)/shard_map/reduce_scatter | solution.py:246
  790.6 28.6 %reduce-scatter.43.cloned.1.call-done = bf16[128,1024]{1,0:T(8,128)(2,1)} async-done(((bf16[512,1024]{1,0:T(8,128)(2,1)}), bf16[128,1024]{1,0:T(8,128)(2,1)}) %reduce-scatter.43.cloned.1.call-update) | async-done | bytes 262160 | tf_op jit(solution)/shard_map/reduce_scatter | solution.py:185
  823.2 26.7 %all-gather.48.cloned.1.call-done = bf16[512,1024]{1,0:T(8,128)(2,1)} async-done(((bf16[128,1024]{1,0:T(8,128)(2,1)}), bf16[512,1024]{1,0:T(8,128)(2,1)}) %all-gather.48.cloned.1.call-update) | async-done | bytes 1048592 | tf_op jit(solution)/shard_map/all_gather | solution.py:106
  861.6 26.7 %reduce-scatter.49.cloned.1.call-done = bf16[128,1024]{1,0:T(8,128)(2,1)} async-done(((bf16[512,1024]{1,0:T(8,128)(2,1)}), bf16[128,1024]{1,0:T(8,128)(2,1)}) %reduce-scatter.49.cloned.1.call-update) | async-done | bytes 262160 | tf_op jit(solution)/shard_map/reduce_scatter | solution.py:109
  949.7 27.1 %reduce-scatter.45.cloned.1.call-done = bf16[128,1024]{1,0:T(8,128)(2,1)} async-done(((bf16[512,1024]{1,0:T(8,128)(2,1)}), bf16[128,1024]{1,0:T(8,128)(2,1)}) %reduce-scatter.45.cloned.1.call-update) | async-done | bytes 262160 | tf_op jit(solution)/shard_map/reduce_scatter | solution.py:246
  1045.9 28.8 %reduce-scatter.51.cloned.1.call-done = bf16[128,1024]{1,0:T(8,128)(2,1)} async-done(((bf16[512,1024]{1,0:T(8,128)(2,1)}), bf16[128,1024]{1,0:T(8,128)(2,1)}) %reduce-scatter.51.cloned.1.call-update) | async-done | bytes 262160 | tf_op jit(solution)/shard_map/reduce_scatter | solution.py:185
  1159.7 61.9 %all-reduce = (f32[1,1024]{1,0:T(1,128)}, f32[1,1024]{1,0:T(1,128)}, f32[1,1024]{1,0:T(1,128)}, f32[1,1024]{1,0:T(1,128)}) all-reduce(f32[1,1024]{1,0:T(1,128)S(1)} %bitcast.593, f32[1,1024]{1,0:T(1,128)S(1)} %bitcast.594, f32[1,1024]{1,0:T(1,128)S(1)} %bitcast.591, ...), channel_id=1, replica_groups=mesh['dp'=4,'section'=2,'mp'=4] {'dp','mp'}, use_global_device_ids=true, to_apply=%region_88.89 | all-reduce | flops 4096 | bytes 32768 | tf_op jit(solution)/shard_map/psum | solution.py:360
  1245.2 72.9 %all-reduce.5.cloned.1.call-done = (bf16[1,1024,256]{2,1,0:T(8,128)(2,1)}, bf16[1,1024,256]{2,1,0:T(8,128)(2,1)}, bf16[1,1024,256]{2,1,0:T(8,128)(2,1)}, bf16[1,...) async-done(((bf16[1,1024,256]{2,1,0:T(8,128)(2,1)}, bf16[1,1024,256]{2,1,0:T(8,128)(2,1)}, bf16[1,1024,256]{2,1,0:T(8,128)(2,1)}, ...) | async-done | bytes 6291472 | tf_op jit(solution)/shard_map/psum | solution.py:358
  (559 shorter events, 589.9 us)
Async XLA Ops:
  9.1 73.5 %reduce-scatter.19.cloned.1.call-start = ((), (), s32[]{:S(2)}) async-start(), calls=%async_computation.18 | async-start | bytes 1310720 | tf_op jit(solution)/shard_map/reduce_scatter | solution.py:97
  87.0 62.8 %reduce-scatter.21.cloned.1.call-start = ((), (), s32[]{:S(2)}) async-start(), calls=%async_computation.20 | async-start | bytes 1310720 | tf_op jit(solution)/shard_map/reduce_scatter | solution.py:109
  123.1 66.2 %all-gather.34.cloned.1.call-start = ((), (), s32[]{:S(2)}) async-start(), calls=%async_computation.33 | async-start | bytes 1310720 | tf_op jit(solution)/shard_map/all_gather | solution.py:67
  161.3 70.7 %reduce-scatter.35.cloned.1.call-start = ((), (), s32[]{:S(2)}) async-start(), calls=%async_computation.34 | async-start | bytes 1310720 | tf_op jit(solution)/shard_map/reduce_scatter | solution.py:97
  236.9 84.7 %reduce-scatter.37.cloned.1.call-start = ((), (), s32[]{:S(2)}) async-start(), calls=%async_computation.36 | async-start | bytes 1310720 | tf_op jit(solution)/shard_map/reduce_scatter | solution.py:109
  274.5 78.5 %all-gather.38.cloned.1.call-start = ((), (), s32[]{:S(2)}) async-start(), calls=%async_computation.37 | async-start | bytes 1310720 | tf_op jit(solution)/shard_map/all_gather | solution.py:173
  340.6 70.6 %reduce-scatter.39.cloned.1.call-start = ((), (), s32[]{:S(2)}) async-start(), calls=%async_computation.38 | async-start | bytes 1310720 | tf_op jit(solution)/shard_map/reduce_scatter | solution.py:185
  362.0 80.6 %all-gather.24.cloned.1.call-start = ((), (), s32[]{:S(2)}) async-start(), calls=%async_computation.23 | async-start | bytes 1310720 | tf_op jit(solution)/shard_map/all_gather | solution.py:106
  415.8 62.7 %reduce-scatter.25.cloned.1.call-start = ((), (), s32[]{:S(2)}) async-start(), calls=%async_computation.24 | async-start | bytes 1310720 | tf_op jit(solution)/shard_map/reduce_scatter | solution.py:109
  451.7 68.7 %all-gather.30.cloned.1.call-start = ((), (), s32[]{:S(2)}) async-start(), calls=%async_computation.29 | async-start | bytes 1310720 | tf_op jit(solution)/shard_map/all_gather | solution.py:67
  492.5 71.3 %reduce-scatter.31.cloned.1.call-start = ((), (), s32[]{:S(2)}) async-start(), calls=%async_computation.30 | async-start | bytes 1310720 | tf_op jit(solution)/shard_map/reduce_scatter | solution.py:97
  568.0 65.1 %reduce-scatter.33.cloned.1.call-start = ((), (), s32[]{:S(2)}) async-start(), calls=%async_computation.32 | async-start | bytes 1310720 | tf_op jit(solution)/shard_map/reduce_scatter | solution.py:109
  636.6 84.7 %reduce-scatter.41.cloned.1.call-start = ((), (), s32[]{:S(2)}) async-start(), calls=%async_computation.40 | async-start | bytes 1310720 | tf_op jit(solution)/shard_map/reduce_scatter | solution.py:246
  675.3 85.7 %all-gather.42.cloned.1.call-start = ((), (), s32[]{:S(2)}) async-start(), calls=%async_computation.41 | async-start | bytes 1310720 | tf_op jit(solution)/shard_map/all_gather | solution.py:173
  749.4 69.8 %reduce-scatter.43.cloned.1.call-start = ((), (), s32[]{:S(2)}) async-start(), calls=%async_computation.42 | async-start | bytes 1310720 | tf_op jit(solution)/shard_map/reduce_scatter | solution.py:185
  769.5 80.5 %all-gather.48.cloned.1.call-start = ((), (), s32[]{:S(2)}) async-start(), calls=%async_computation.47 | async-start | bytes 1310720 | tf_op jit(solution)/shard_map/all_gather | solution.py:106
  823.2 65.2 %reduce-scatter.49.cloned.1.call-start = ((), (), s32[]{:S(2)}) async-start(), calls=%async_computation.48 | async-start | bytes 1310720 | tf_op jit(solution)/shard_map/reduce_scatter | solution.py:109
  892.0 84.8 %reduce-scatter.45.cloned.1.call-start = ((), (), s32[]{:S(2)}) async-start(), calls=%async_computation.44 | async-start | bytes 1310720 | tf_op jit(solution)/shard_map/reduce_scatter | solution.py:246
  930.4 85.9 %all-gather.50.cloned.1.call-start = ((), (), s32[]{:S(2)}) async-start(), calls=%async_computation.49 | async-start | bytes 1310720 | tf_op jit(solution)/shard_map/all_gather | solution.py:173
  1004.4 70.2 %reduce-scatter.51.cloned.1.call-start = ((), (), s32[]{:S(2)}) async-start(), calls=%async_computation.50 | async-start | bytes 1310720 | tf_op jit(solution)/shard_map/reduce_scatter | solution.py:185
  1024.8 81.3 %all-gather.28.cloned.1.call-start = ((), (), s32[]{:S(2)}) async-start(), calls=%async_computation.27 | async-start | bytes 1310720 | tf_op jit(solution)/shard_map/all_gather | solution.py:106
  1090.3 147.9 %reduce-scatter.29.cloned.1.call-start = ((), (), s32[]{:S(2)}) async-start(), calls=%async_computation.28 | async-start | bytes 1310720 | tf_op jit(solution)/shard_map/reduce_scatter | solution.py:109
  1115.3 126.5 %reduce-scatter.53.cloned.1.call-start = ((), (), s32[]{:S(2)}) async-start(), calls=%async_computation.52 | async-start | bytes 1310720 | tf_op jit(solution)/shard_map/reduce_scatter | solution.py:246
  1147.3 170.7 %all-reduce.5.cloned.1.call-start = ((), (), s32[]{:S(2)}) async-start(), calls=%async_computation.54 | async-start | bytes 12582912 | tf_op jit(solution)/shard_map/psum | solution.py:358
  (137 other events, 2318.8 us)
Sparse Core Ops, SparseCore 0:
  10.2 30.6 all-gather.53
  55.9 26.6 reduce-scatter.18
  123.2 26.6 reduce-scatter.20
  161.5 27.7 all-gather.33
  205.4 26.6 reduce-scatter.34
  264.5 27.4 all-gather.21
  295.0 26.6 reduce-scatter.36
  326.4 26.5 all-gather.37
  355.9 26.6 reduce-scatter.22
  451.9 26.6 reduce-scatter.24
  492.6 27.7 all-gather.29
  537.2 26.6 reduce-scatter.30
  606.4 26.6 reduce-scatter.32
  664.3 27.5 all-gather.45
  763.9 26.6 reduce-scatter.46
  823.3 26.5 all-gather.47
  861.7 26.6 reduce-scatter.48
  919.7 27.4 all-gather.25
  950.1 26.6 reduce-scatter.44
  1019.2 26.6 reduce-scatter.26
  1079.5 26.5 all-gather.27
  1108.3 27.4 all-gather.51
  1138.6 26.6 reduce-scatter.28
  1198.3 119.7 all-reduce.4
  (13 shorter events, 340.6 us)
where the time goes:
time: 1350 us; the launch traced here: 1340 us
  waiting for transfers between devices  881 us (65%)
  matrix products  247 us (18%)
  other arithmetic  88.8 us (7%)
  blocking collectives  74 us (5%)
  between operations  16.5 us (1%)
  local copies, waits for them, and re-layouts  16.3 us (1%)
    all_gather x6, waiting for transfers between devices, layer_forward(): lax.all_gather(middle.astype(jnp.bfloat16), 'mp', axis=0, tiled=True)  148 us
    reduce_scatter x6, waiting for transfers between devices, layer_forward(): lax.psum_scatter(jnp.dot(activated, w_down, preferred_element_type=jnp.fl...  134 us
    all_gather x6, waiting for transfers between devices, layer_forward(): whole = lax.all_gather(share_rows, 'mp', axis=0, tiled=True)  133 us
    reduce_scatter x6, waiting for transfers between devices, layer_forward(): lax.psum_scatter(jnp.dot(mixed, w_out, preferred_element_type=jnp.float32...  127 us
    reduce_scatter x3, waiting for transfers between devices, layer_backward(): lax.psum_scatter(jnp.einsum('tf,df->td', grad_up, w_up, preferred_element...  86 us
    psum x1, waiting for transfers between devices, per_device(): lax.psum(for_sending(big_total), 'dp')  72.9 us
    all_gather x3, waiting for transfers between devices, layer_backward(): lax.all_gather(grad_sum_one.astype(jnp.bfloat16), 'mp', axis=0, tiled=True)  71.7 us
    psum x1, blocking collectives, per_device(): small_sum = lax.psum(small_total, ('dp', 'mp'))  61.9 us
  transfers between devices with their start and end apart: 41, of which 39 were waited for; matrix products, arithmetic and copies ran while one was open for 14% of the time, Pallas kernels for 0%

commit v1 on v0

v1 whole, which is shorter than its diff:
```python
from functools import partial

import jax
import jax.numpy as jnp
from jax import lax
from jax.sharding import PartitionSpec as P

HD = 64
SEQ = 512
SHARE = 128
AXES = ("dp", "section", "mp")
EPSILON = 1e-05
NEGATIVE = -1e30
F32 = jnp.float32
BF16 = jnp.bfloat16


def dot_nt(left, right):
    return lax.dot_general(left, right, (((1,), (1,)), ((), ())), preferred_element_type=F32)


def dot_nn(left, right):
    return lax.dot_general(left, right, (((1,), (0,)), ((), ())), preferred_element_type=F32)


def dot_tn(left, right):
    return lax.dot_general(left, right, (((0,), (0,)), ((), ())), preferred_element_type=F32)


def mover(sizes, target, takes=None):
    replicas, sections, shards = sizes
    pairs = []
    for d in range(replicas):
        for s in range(sections):
            for z in range(shards):
                if takes is None or takes(d, s, z):
                    nd, ns, nz = target(d, s, z)
                    pairs.append(
                        ((d * sections + s) * shards + z, (nd * sections + ns) * shards + nz)
                    )

    def move(values):
        return lax.ppermute(values, AXES, pairs)

    return move


def norm_forward(hidden, gain, offset):
    centre = jnp.mean(hidden, -1, keepdims=True)
    centred = hidden - centre
    variance = jnp.mean(centred * centred, -1, keepdims=True)
    inverse = lax.rsqrt(variance + EPSILON)
    normed = centred * inverse
    return (normed * gain + offset, normed, inverse)


def norm_backward(upstream, normed, inverse, gain):
    scaled = upstream * gain
    return inverse * (
        scaled
        - jnp.mean(scaled, -1, keepdims=True)
        - normed * jnp.mean(scaled * normed, -1, keepdims=True)
    )


def layer_forward(share, weights, allowed, gather, scatter):
    wide = share.astype(F32)
    low = share.astype(BF16)
    whole = gather(low)
    rows = jnp.einsum("td,zaed->azte", whole, weights["qkv"], preferred_element_type=F32)
    rows = (rows + weights["b_qkv"][:, :, None, :]).astype(BF16)
    query, key, value = rows[0], rows[1], rows[2]
    scores = jnp.einsum("zqe,zke->zqk", query, key, preferred_element_type=F32) * HD ** (-0.5)
    scores = jnp.where(allowed[None], scores, NEGATIVE)
    exponent = jnp.exp(scores - jnp.max(scores, -1, keepdims=True))
    probs = exponent / jnp.sum(exponent, -1, keepdims=True)
    probs_low = probs.astype(BF16)
    mixed = jnp.einsum("zqk,zke->zqe", probs_low, value, preferred_element_type=F32).astype(BF16)
    attended = scatter(
        jnp.einsum("zte,zed->td", mixed, weights["out"], preferred_element_type=F32)
    )
    middle, normed_one, inverse_one = norm_forward(
        wide + attended + weights["b_out"], weights["gain_one"], weights["shift_one"]
    )
    spread = gather(middle.astype(BF16))
    hidden = [dot_nt(spread, up) + bias for up, bias in zip(weights["up"], weights["b_up"])]
    active = [jax.nn.gelu(h, approximate=False).astype(BF16) for h in hidden]
    lowered = scatter(
        dot_nn(active[0], weights["down"][0]) + dot_nn(active[1], weights["down"][1])
    )
    result, normed_two, inverse_two = norm_forward(
        middle + lowered + weights["b_down"], weights["gain_two"], weights["shift_two"]
    )
    kept = (
        whole,
        query,
        key,
        value,
        probs,
        mixed,
        normed_one,
        inverse_one,
        spread,
        hidden,
        active,
        normed_two,
        inverse_two,
    )
    return (result, kept)


def layer_backward(upstream, weights, kept, gather, scatter):
    (
        whole,
        query,
        key,
        value,
        probs,
        mixed,
        normed_one,
        inverse_one,
        spread,
        hidden,
        active,
        normed_two,
        inverse_two,
    ) = kept
    d_gain_two = jnp.sum(upstream * normed_two, 0)
    d_shift_two = jnp.sum(upstream, 0)
    d_sum_two = norm_backward(upstream, normed_two, inverse_two, weights["gain_two"])
    low_two = d_sum_two.astype(BF16)
    d_b_down = jnp.sum(low_two.astype(F32), 0)
    d_lowered = gather(low_two)
    d_hidden, d_down, d_up, d_b_up = [], [], [], []
    for h in range(2):
        d_active = dot_nt(d_lowered, weights["down"][h])
        pull = jax.vjp(partial(jax.nn.gelu, approximate=False), hidden[h])[1]
        d_hidden.append(pull(d_active)[0].astype(BF16))
        d_down.append(dot_tn(active[h], d_lowered))
        d_up.append(dot_tn(d_hidden[h], spread))
        d_b_up.append(jnp.sum(d_hidden[h].astype(F32), 0))
    d_middle = d_sum_two + scatter(
        dot_nn(d_hidden[0], weights["up"][0]) + dot_nn(d_hidden[1], weights["up"][1])
    )
    d_gain_one = jnp.sum(d_middle * normed_one, 0)
    d_shift_one = jnp.sum(d_middle, 0)
    d_sum_one = norm_backward(d_middle, normed_one, inverse_one, weights["gain_one"])
    low_one = d_sum_one.astype(BF16)
    d_b_out = jnp.sum(low_one.astype(F32), 0)
    d_attended = gather(low_one)
    d_out = jnp.einsum("zte,td->zed", mixed, d_attended, preferred_element_type=F32)
    d_mixed = jnp.einsum(
        "td,zed->zte", d_attended, weights["out"], preferred_element_type=F32
    ).astype(BF16)
    d_probs = jnp.einsum("zqe,zke->zqk", d_mixed, value, preferred_element_type=F32)
    d_scores = (probs * (d_probs - jnp.sum(probs * d_probs, -1, keepdims=True))).astype(BF16)
    scale = HD ** (-0.5)
    d_query = jnp.einsum("zqk,zke->zqe", d_scores, key, preferred_element_type=F32) * scale
    d_key = jnp.einsum("zqk,zqe->zke", d_scores, query, preferred_element_type=F32) * scale
    d_value = jnp.einsum(
        "zqk,zqe->zke", probs.astype(BF16), d_mixed, preferred_element_type=F32
    )
    d_rows = jnp.stack([d_query, d_key, d_value]).astype(BF16)
    d_qkv = jnp.einsum("azte,td->zaed", d_rows, whole, preferred_element_type=F32)
    d_b_qkv = jnp.sum(d_rows.astype(F32), 2)
    d_input = d_sum_one + scatter(
        jnp.einsum("azte,zaed->td", d_rows, weights["qkv"], preferred_element_type=F32)
    )
    vectors = jnp.stack([d_b_out, d_gain_one, d_shift_one, d_b_down, d_gain_two, d_shift_two])
    return (d_input, d_qkv, d_b_qkv, d_out, d_up, d_b_up, d_down, vectors)


def solution(mesh):
    replicas, sections, shards = (mesh.shape[name] for name in AXES)
    sizes = (replicas, sections, shards)

    def quarter_of(d, s):
        return 2 * ((d >> 1) & 1) + s

    swap_y = mover(sizes, lambda d, s, z: (d, s ^ 1, z))
    swap_x = mover(sizes, lambda d, s, z: (d ^ 2, s, z))
    swap_xy = mover(sizes, lambda d, s, z: (d ^ 2, s ^ 1, z))
    swap_core = mover(sizes, lambda d, s, z: (d ^ 1, s, z))
    swap_z = [mover(sizes, lambda d, s, z, r=r: (d, s, z ^ r)) for r in range(1, 4)]
    place_in = mover(
        sizes,
        lambda d, s, z: (
            (d & ~2) | ((z >> 1) << 1),
            z & 1,
            2 * (s ^ (z & 1)) + ((d >> 1) & 1),
        ),
    )
    place_out = [
        mover(
            sizes,
            lambda d, s, z, r=r: (
                (d & ~2) | ((z & 1) << 1),
                (z >> 1) ^ r,
                quarter_of(d, s),
            ),
        )
        for r in range(2)
    ]

    def gather(share):
        return jnp.concatenate([share, swap_y(share), swap_x(share), swap_xy(share)])

    def scatter(part):
        low = part.astype(BF16).reshape(4, SHARE, -1)
        own = part[:SHARE]
        return (
            own
            + swap_y(low[1]).astype(F32)
            + swap_x(low[2]).astype(F32)
            + swap_xy(low[3]).astype(F32)
        )

    def gather_z(piece):
        return jnp.stack([piece] + [move(piece) for move in swap_z])

    def scatter_z(pieces):
        total = pieces[0].astype(F32)
        for r in range(1, 4):
            total = total + swap_z[r - 1](pieces[r]).astype(F32)
        return total

    def to_layers(first, second, section):
        pick = (lax.axis_index("mp") >> 1) == 0
        moved_a = place_out[0](jnp.where(pick, first, second))
        moved_b = place_out[1](jnp.where(pick, second, first))
        is_first = section == 0
        return jnp.stack(
            [jnp.where(is_first, moved_a, moved_b), jnp.where(is_first, moved_b, moved_a)]
        )

    def per_device(
        inputs,
        cotangent,
        doc_ids,
        w_query,
        b_query,
        w_key,
        w_value,
        b_value,
        w_out,
        b_out,
        gain_one,
        shift_one,
        w_up,
        b_up,
        w_down,
        b_down,
        gain_two,
        shift_two,
    ):
        replica = lax.axis_index("dp")
        section = lax.axis_index("section")
        shard = lax.axis_index("mp")
        core = replica & 1
        quarter = quarter_of(replica, section)

        which = (section ^ shard) & 1
        share_in = place_in(lax.dynamic_index_in_dim(inputs, which, 0, False))
        share_grad = place_in(lax.dynamic_index_in_dim(cotangent, which, 0, False))
        other_ids = swap_x(doc_ids)
        mine = ((replica >> 1) & 1) == (shard & 1)
        ids = jnp.where(mine, doc_ids, other_ids)
        ids = lax.dynamic_index_in_dim(ids, shard >> 1, 0, False).reshape(4, SHARE)
        ids = jnp.concatenate(
            [lax.dynamic_index_in_dim(ids, quarter ^ r, 0, False) for r in range(4)]
        )
        allowed = ids[:, None] == ids[None, :]

        layer_vectors = jnp.concatenate(
            [b_out, gain_one, shift_one, b_down, gain_two, shift_two]
        )

        def attn_pack(block):
            head = block * HD + core * 32
            columns = [
                lax.dynamic_slice_in_dim(w[0], head, 32, 1).T for w in (w_query, w_key, w_value)
            ]
            small = jnp.concatenate(
                [
                    lax.dynamic_slice_in_dim(b_query[0], head, 32),
                    lax.dynamic_slice_in_dim(b_value[0], head, 32),
                    lax.dynamic_slice_in_dim(b_up[0], block * 256 + core * 128, 128),
                    jnp.zeros((1024 - 192,), BF16),
                ]
            )[None]
            return jnp.concatenate(
                columns
                + [
                    lax.dynamic_slice_in_dim(w_out[0], head, 32, 0),
                    small,
                    layer_vectors,
                    jnp.zeros((9, 1024), BF16),
                ]
            )

        def ffn_pack(block):
            unit = block * 256 + core * 128
            return jnp.concatenate(
                [
                    lax.dynamic_slice_in_dim(w_up[0], unit, 128, 1).T,
                    lax.dynamic_slice_in_dim(w_down[0], unit, 128, 0),
                ]
            )

        packs = []
        for make in (attn_pack, ffn_pack):
            own = make(quarter)
            received = swap_y(make(quarter ^ 1))
            packs.append((own, received))
        layers = []
        for layer in range(2):
            attn, ffn = (jnp.where(section == layer, own, other) for own, other in packs)
            vectors = attn[129:135].astype(F32)
            attn_own = gather_z(attn[:144])
            attn_other = swap_core(attn_own)
            ffn_own = gather_z(ffn)
            ffn_other = swap_core(ffn_own)
            heads = jnp.concatenate(
                [attn_own[:, :128].reshape(4, 4, 32, 1024), attn_other[:, :128].reshape(4, 4, 32, 1024)],
                2,
            )
            biases = [a[:, 128].astype(F32) for a in (attn_own, attn_other)]
            zero = jnp.zeros((4, HD), F32)
            layers.append(
                dict(
                    qkv=heads[:, :3],
                    out=heads[:, 3],
                    b_qkv=jnp.stack(
                        [
                            jnp.concatenate([b[:, :32] for b in biases], 1),
                            zero,
                            jnp.concatenate([b[:, 32:64] for b in biases], 1),
                        ]
                    ),
                    up=[f[:, :128].reshape(512, 1024) for f in (ffn_own, ffn_other)],
                    down=[f[:, 128:].reshape(512, 1024) for f in (ffn_own, ffn_other)],
                    b_up=[b[:, 64:192].reshape(512) for b in biases],
                    b_out=vectors[0],
                    gain_one=vectors[1],
                    shift_one=vectors[2],
                    b_down=vectors[3],
                    gain_two=vectors[4],
                    shift_two=vectors[5],
                )
            )

        first, kept_first = layer_forward(share_in, layers[0], allowed, gather, scatter)
        first = first.astype(BF16)
        second, kept_second = layer_forward(first, layers[1], allowed, gather, scatter)
        second = second.astype(BF16)
        section_outputs = to_layers(first, second, section)[None]

        upstream = share_grad.astype(F32)
        reduced = [None, None]
        all_vectors = [None, None]
        grads_in = [None, None]
        for layer, kept in ((1, kept_second), (0, kept_first)):
            d_input, d_qkv, d_b_qkv, d_out, d_up, d_b_up, d_down, vectors = layer_backward(
                upstream, layers[layer], kept, gather, scatter
            )
            grads_in[layer] = d_input.astype(BF16)
            upstream = grads_in[layer].astype(F32)
            all_vectors[layer] = vectors
            heads = jnp.concatenate([d_qkv, d_out[:, None]], 1).reshape(4, 4, 2, 32, 1024)
            halves = []
            for half in range(2):
                small = jnp.concatenate(
                    [
                        d_b_qkv[0][:, 32 * half : 32 * half + 32],
                        d_b_qkv[2][:, 32 * half : 32 * half + 32],
                        d_b_up[half].reshape(4, 128),
                        jnp.zeros((4, 1024 - 192), F32),
                    ],
                    1,
                )[:, None]
                halves.append(
                    jnp.concatenate(
                        [
                            heads[:, :, half].reshape(4, 128, 1024),
                            small,
                            jnp.zeros((4, 15, 1024), F32),
                            d_up[half].reshape(4, 128, 1024),
                            d_down[half].reshape(4, 128, 1024),
                        ],
                        1,
                    )
                )
            half_sum = (halves[0] + swap_core(halves[1].astype(BF16)).astype(F32)).astype(BF16)
            reduced[layer] = scatter_z(half_sum).astype(BF16)

        if replicas > 4:
            groups = [[low + 4 * high for high in range(replicas // 4)] for low in range(4)]
            reduced = [
                lax.psum(part, "dp", axis_index_groups=groups).astype(BF16) for part in reduced
            ]
        mine = jnp.where(section == 0, reduced[0], reduced[1])
        theirs = jnp.where(section == 0, reduced[1], reduced[0])
        pieces = jnp.stack([mine, swap_y(theirs), swap_x(mine), swap_xy(theirs)])
        pieces = jnp.stack([pieces, swap_core(pieces)])
        pieces = lax.dynamic_index_in_dim(
            jnp.stack([pieces, pieces[::-1]]), core, 0, False
        )
        ordered = jnp.stack(
            [lax.dynamic_index_in_dim(pieces, quarter ^ r, 1, False) for r in range(4)]
        ).astype(F32)
        heads = ordered[:, :, :128].reshape(4, 2, 4, 32, 1024).transpose(2, 0, 1, 3, 4)
        heads = heads.reshape(4, 256, 1024)
        small = ordered[:, :, 128]
        g_up = ordered[:, :, 144:272].reshape(1024, 1024).T
        g_down = ordered[:, :, 272:400].reshape(1024, 1024)
        vectors = lax.psum(jnp.stack(all_vectors), AXES)
        vectors = lax.dynamic_index_in_dim(vectors, section, 0, True)
        section_input_grads = to_layers(grads_in[0], grads_in[1], section)[None].astype(F32)
        return (
            section_outputs,
            section_input_grads,
            heads[0].T[None],
            small[:, :, :32].reshape(1, 256),
            heads[1].T[None],
            heads[2].T[None],
            small[:, :, 32:64].reshape(1, 256),
            heads[3][None],
            vectors[:, 0],
            vectors[:, 1],
            vectors[:, 2],
            g_up[None],
            small[:, :, 64:192].reshape(1, 1024),
            g_down[None],
            vectors[:, 3],
            vectors[:, 4],
            vectors[:, 5],
        )

    vector = P("section", None)
    columns = P("section", None, "mp")
    rows = P("section", "mp", None)
    spread = P("section", "mp")
    tokens = P(None, ("dp", "mp"), None)
    layer_tokens = P("section", None, ("dp", "mp"), None)
    return jax.shard_map(
        per_device,
        mesh=mesh,
        in_specs=(
            tokens,
            tokens,
            P(None, "dp", None),
            columns,
            spread,
            columns,
            columns,
            spread,
            rows,
            vector,
            vector,
            vector,
            columns,
            spread,
            rows,
            vector,
            vector,
            vector,
        ),
        out_specs=(
            layer_tokens,
            layer_tokens,
            columns,
            spread,
            columns,
            columns,
            spread,
            rows,
            vector,
            vector,
            vector,
            columns,
            spread,
            rows,
            vector,
            vector,
            vector,
        ),
        check_vma=False,
    )
```

time: 1350 us -> 907 us (0.67)
  waiting for transfers between devices: 881 us -> 321 us
  starting transfers between devices: 13.1 us -> 180 us
  local copies, waits for them, and re-layouts: 16.3 us -> 180 us
  matrix products: 247 us -> 88.7 us
  other arithmetic: 88.8 us -> 61.6 us
    reduce_scatter x18 -> x0, waiting for transfers between devices: 401 us -> none  [the longest x6 134 us: layer_forward(): lax.psum_scatter(jnp.dot(activated, w_down, preferred_element_type=jnp.fl...]
    all_gather x18 -> x0, waiting for transfers between devices: 378 us -> none  [the longest x6 148 us: layer_forward(): lax.all_gather(middle.astype(jnp.bfloat16), 'mp', axis=0, tiled=True)]
    ppermute x4 -> x85, waiting for transfers between devices: 26.2 us -> 321 us  [move(): return lax.ppermute(values, AXES, pairs)]
    ppermute x4 -> x85, starting transfers between devices: 9.36 us -> 180 us  [move(): return lax.ppermute(values, AXES, pairs)]
    dot_general x87 -> x46, matrix products: 219 us -> 79.3 us  [the longest x8 25 us: dot_nt(): lax.dot_general(left, right, (((1,), (1,)), ((), ())), preferred_element_...]
    concatenate x0 -> x7, local copies, waits for them, and re-layouts: none -> 78.8 us  [the longest x4 73.1 us: per_device(): jnp.concatenate([heads[:, :, half].reshape(4, 128, 1024), small, jnp.zero...]
    psum x1 -> x0, waiting for transfers between devices: 72.9 us -> none  [per_device(): lax.psum(for_sending(big_total), 'dp')]
    slice x1 -> x47, local copies, waits for them, and re-layouts: 0.7 us -> 52.5 us  [the longest x8 31.8 us: per_device(): f[:, 128:].reshape(512, 1024)]
  transfers between devices with their start and end apart: 41 -> 85, of which waited for: 39 -> 42; matrix products, arithmetic and copies ran while one was open for 14% -> 20% of each run, Pallas kernels for 0% -> 0%
where the time goes in v1:
time: 907 us; the launch traced here: 898 us
  waiting for transfers between devices  321 us (35%)
  local copies, waits for them, and re-layouts  180 us (20%)
  starting transfers between devices  180 us (20%)
  matrix products  88.7 us (10%)
  blocking collectives  62.5 us (7%)
  other arithmetic  61.6 us (7%)
    ppermute x85, waiting for transfers between devices, move(): return lax.ppermute(values, AXES, pairs)  321 us
    ppermute x85, starting transfers between devices, move(): return lax.ppermute(values, AXES, pairs)  180 us
    concatenate x4, local copies, waits for them, and re-layouts, per_device(): jnp.concatenate([heads[:, :, half].reshape(4, 128, 1024), small, jnp.zero...  73.1 us
    psum x1, blocking collectives, per_device(): vectors = lax.psum(jnp.stack(all_vectors), AXES)  62.5 us
    slice x8, local copies, waits for them, and re-layouts, per_device(): f[:, 128:].reshape(512, 1024)  31.8 us
    dot_general x8, matrix products, dot_nt(): lax.dot_general(left, right, (((1,), (1,)), ((), ())), preferred_element_...  25 us
    unnamed x349, local copies, waits for them, and re-layouts  22.9 us
    dot_general x8, matrix products, dot_tn(): lax.dot_general(left, right, (((0,), (0,)), ((), ())), preferred_element_...  21.3 us
  transfers between devices with their start and end apart: 85, of which 42 were waited for; matrix products, arithmetic and copies ran while one was open for 20% of the time, Pallas kernels for 0%

profile of v1, /device:TPU:0, one launch (start us, length us, event | category | flops | bytes accessed | tf_op | source)
XLA Modules:
  0.0 897.9 jit_solution(4652204312166342008)
XLA Ops:
  22.6 10.1 %collective-permute-start.9 = (bf16[128,1024]{1,0:T(8,128)(2,1)S(1)}, bf16[128,1024]{1,0:T(8,128)(2,1)S(1)}, u32[]{:S(2)}, u32[]{:S(2)}) collective-permute-start(bf16[128,1024]{1,0:T(8,128)(2,1)S(1)} %collective-permute-done), channel_id=1, source_target_pairs={{0,20},{1,21},{2,22},{3,23},{4,16},{5,17},{6,18},{7,19},{8,28},{9,... | collective-permute-start | bytes 786440 | tf_op jit(solution)/shard_map/ppermute | solution.py:43
  34.3 12.4 %collective-permute-start.26 = (bf16[144,1024]{1,0:T(8,128)(2,1)S(1)}, bf16[144,1024]{1,0:T(8,128)(2,1)S(1)}, u32[]{:S(2)}, u32[]{:S(2)}) collective-permute-start(bf16[144,1024]{1,0:T(8,128)(2,1)S(1)} %get-tuple-element.212), channel_id=1, source_target_pairs={{0,3},{1,2},{2,1},{3,0},{4,7},{5,6},{6,5},{7,4},{8,11},{9,10},{10,... | collective-permute-start | bytes 884744 | tf_op jit(solution)/shard_map/ppermute | solution.py:43
  48.3 6.4 collective-permute-done.26
  58.5 8.9 collective-permute-done.25
  67.4 12.5 %collective-permute-start.3 = (bf16[144,1024]{1,0:T(8,128)(2,1)S(1)}, bf16[144,1024]{1,0:T(8,128)(2,1)S(1)}, u32[]{:S(2)}, u32[]{:S(2)}) collective-permute-start(bf16[144,1024]{1,0:T(8,128)(2,1)S(1)} %get-tuple-element.213), channel_id=1, source_target_pairs={{0,1},{1,0},{2,3},{3,2},{4,5},{5,4},{6,7},{7,6},{8,9},{9,8},{10,11... | collective-permute-start | bytes 884744 | tf_op jit(solution)/shard_map/ppermute | solution.py:43
  83.6 7.0 collective-permute-done.4
  119.3 24.3 %collective-permute-done.18 = bf16[256,1024]{0,1:T(8,128)(2,1)} collective-permute-done((bf16[256,1024]{0,1:T(8,128)(2,1)S(1)}, bf16[256,1024]{0,1:T(8,128)(2,1)}, u32[]{:S(2)}, u32[]{:S(2)}) %collective-permute-start.18) | collective-permute-done | bytes 524320 | tf_op jit(solution)/shard_map/ppermute | solution.py:43
  176.0 14.2 %copy.257 = bf16[4,128,1024]{2,1,0:T(8,128)(2,1)} copy(bf16[4,128,1024]{1,2,0:T(8,128)(2,1)} %get-tuple-element.176) | data formatting | bytes 2097152 | tf_op jit(solution)/shard_map/slice | solution.py:341
  219.4 26.0 %collective-permute-done.38 = bf16[256,1024]{0,1:T(8,128)(2,1)S(1)} collective-permute-done((bf16[256,1024]{0,1:T(8,128)(2,1)S(1)}, bf16[256,1024]{0,1:T(8,128)(2,1)S(1)}, u32[]{:S(2)}, u32[]{:S(2)}) %collective-permute-start.38) | collective-permute-done | bytes 524320 | tf_op jit(solution)/shard_map/ppermute | solution.py:43
  311.3 8.3 collective-permute-done.43
  460.2 16.4 %concatenate.144 = bf16[4,400,1024]{2,1,0:T(8,128)(2,1)} concatenate(bf16[4,128,1024]{2,1,0:T(8,128)(2,1)S(1)} %bitcast.468, bf16[4,1,1024]{2,1,0:T(2,128)(2,1)S(1)} %copy.277, bf16[4,15,1024]{2,1,0:T(8,128)(2,1)S(1)} %broadcast.316, bf16[4,128,1024]{2,1,0:T(8,128)(2,1)} %bitcast.507, bf16[4,128,1024]{2,1,0:T(8,128)(2,1)} %bitcast.508), dimensions={1} | concatenate | bytes 6553600 | tf_op jit(solution)/shard_map/concatenate | solution.py:382
  483.4 16.2 %concatenate.151 = bf16[4,400,1024]{2,1,0:T(8,128)(2,1)} concatenate(bf16[4,128,1024]{2,1,0:T(8,128)(2,1)S(1)} %bitcast.469, bf16[4,1,1024]{2,1,0:T(2,128)(2,1)S(1)} %copy.280, bf16[4,15,1024]{2,1,0:T(8,128)(2,1)S(1)} %broadcast.316, bf16[4,128,1024]{2,1,0:T(8,128)(2,1)} %bitcast.506, bf16[4,128,1024]{2,1,0:T(8,128)(2,1)} %bitcast.509), dimensions={1} | concatenate | bytes 6553600 | tf_op jit(solution)/shard_map/concatenate | solution.py:382
  516.9 20.2 %concatenate.142 = f32[4,400,1024]{2,1,0:T(8,128)} concatenate(f32[4,128,1024]{2,1,0:T(8,128)} %bitcast.458, f32[4,1,1024]{2,1,0:T(1,128)S(1)} %copy.276, f32[4,15,1024]{2,1,0:T(8,128)S(1)} %broadcast.314, f32[4,128,1024]{2,1,0:T(8,128)} %bitcast.500, f32[4,128,1024]{2,1,0:T(8,128)} %bitcast.501), dimensions={1} | concatenate | bytes 13107200 | tf_op jit(solution)/shard_map/concatenate | solution.py:382
  537.2 20.2 %concatenate.149 = f32[4,400,1024]{2,1,0:T(8,128)} concatenate(f32[4,128,1024]{2,1,0:T(8,128)} %bitcast.457, f32[4,1,1024]{2,1,0:T(1,128)S(1)} %broadcast_in_dim.47, f32[4,15,1024]{2,1,0:T(8,128)S(1)} %broadcast.314, f32[4,128,1024]{2,1,0:T(8,128)} %bitcast.498, f32[4,128,1024]{2,1,0:T(8,128)} %bitcast.499), dimensions={1} | concatenate | bytes 13107200 | tf_op jit(solution)/shard_map/concatenate | solution.py:382
  576.5 11.2 %collective-permute-done.76 = bf16[400,1024]{1,0:T(8,128)(2,1)S(1)} collective-permute-done((bf16[400,1024]{1,0:T(8,128)(2,1)S(1)}, bf16[400,1024]{1,0:T(8,128)(2,1)S(1)}, u32[]{:S(2)}, u32[]{:S(2)}) %collective-permute-start.76) | collective-permute-done | bytes 819232 | tf_op jit(solution)/shard_map/ppermute | solution.py:43
  587.7 33.4 %collective-permute-start.78 = (bf16[400,1024]{1,0:T(8,128)(2,1)S(1)}, bf16[400,1024]{1,0:T(8,128)(2,1)S(1)}, u32[]{:S(2)}, u32[]{:S(2)}) collective-permute-start(bf16[400,1024]{1,0:T(8,128)(2,1)S(1)} %get-tuple-element.166), channel_id=1, source_target_pairs={{0,1},{1,0},{2,3},{3,2},{4,5},{5,4},{6,7},{7,6},{8,9},{9,8},{10,11... | collective-permute-start | bytes 2457608 | tf_op jit(solution)/shard_map/ppermute | solution.py:43
  621.0 52.1 %collective-permute-done.75 = bf16[400,1024]{1,0:T(8,128)(2,1)S(1)} collective-permute-done((bf16[400,1024]{1,0:T(8,128)(2,1)S(1)}, bf16[400,1024]{1,0:T(8,128)(2,1)S(1)}, u32[]{:S(2)}, u32[]{:S(2)}) %collective-permute-start.75) | collective-permute-done | bytes 819232 | tf_op jit(solution)/shard_map/ppermute | solution.py:43
  673.2 34.3 %collective-permute-done.79 = bf16[400,1024]{1,0:T(8,128)(2,1)S(1)} collective-permute-done((bf16[400,1024]{1,0:T(8,128)(2,1)S(1)}, bf16[400,1024]{1,0:T(8,128)(2,1)S(1)}, u32[]{:S(2)}, u32[]{:S(2)}) %collective-permute-start.79) | collective-permute-done | bytes 819232 | tf_op jit(solution)/shard_map/ppermute | solution.py:43
  712.8 18.6 %collective-permute-done.83 = bf16[400,1024]{1,0:T(8,128)(2,1)S(1)} collective-permute-done((bf16[400,1024]{1,0:T(8,128)(2,1)S(1)}, bf16[400,1024]{1,0:T(8,128)(2,1)S(1)}, u32[]{:S(2)}, u32[]{:S(2)}) %collective-permute-start.83) | collective-permute-done | bytes 819232 | tf_op jit(solution)/shard_map/ppermute | solution.py:43
  731.4 15.5 %collective-permute-done.82 = bf16[400,1024]{1,0:T(8,128)(2,1)S(1)} collective-permute-done((bf16[400,1024]{1,0:T(8,128)(2,1)S(1)}, bf16[400,1024]{1,0:T(8,128)(2,1)S(1)}, u32[]{:S(2)}, u32[]{:S(2)}) %collective-permute-start.82) | collective-permute-done | bytes 819232 | tf_op jit(solution)/shard_map/ppermute | solution.py:43
  761.9 15.1 %collective-permute-start.68 = (bf16[128,1024]{1,0:T(8,128)(2,1)S(1)}, bf16[128,1024]{1,0:T(8,128)(2,1)S(1)}, u32[]{:S(2)}, u32[]{:S(2)}) collective-permute-start(bf16[128,1024]{1,0:T(8,128)(2,1)S(1)} %get-tuple-element.184), channel_id=1, source_target_pairs={{0,4},{1,5},{2,6},{3,7},{4,0},{5,1},{6,2},{7,3},{8,12},{9,13},{10,... | collective-permute-start | bytes 786440 | tf_op jit(solution)/shard_map/ppermute | solution.py:43
  780.7 8.8 collective-permute-done.69
  797.5 62.5 %psum.7 = f32[2,6,1024]{2,1,0:T(8,128)S(1)} all-reduce(f32[2,6,1024]{2,1,0:T(8,128)S(1)} %pad_maximum_fusion.18), channel_id=1, replica_groups=mesh['dp'=4,'section'=2,'mp'=4] {'dp','section','mp'}, use_global_device_ids=true, to_apply=%region_40.41 | all-reduce | flops 12288 | bytes 98304 | tf_op jit(solution)/shard_map/psum | solution.py:416
  861.8 8.6 fusion.183
  (732 shorter events, 431.2 us)
Async XLA Ops:
  17.1 63.9 %collective-permute-start.16 = (bf16[256,1024]{0,1:T(8,128)(2,1)S(1)}, bf16[256,1024]{0,1:T(8,128)(2,1)}, u32[]{:S(2)}, u32[]{:S(2)}) collective-permute-start(bf16[256,1024]{0,1:T(8,128)(2,1)S(1)} %pad_maximum_fusion.17), channel_id=1, source_target_pairs={{0,4},{1,5},{2,6},{3,7},{4,0},{5,1},{6,2},{7,3},{8,12},{9,13},{10,... | collective-permute-start | bytes 1572872 | tf_op jit(solution)/shard_map/ppermute | solution.py:43
  22.6 78.1 %collective-permute-start.9 = (bf16[128,1024]{1,0:T(8,128)(2,1)S(1)}, bf16[128,1024]{1,0:T(8,128)(2,1)S(1)}, u32[]{:S(2)}, u32[]{:S(2)}) collective-permute-start(bf16[128,1024]{1,0:T(8,128)(2,1)S(1)} %collective-permute-done), channel_id=1, source_target_pairs={{0,20},{1,21},{2,22},{3,23},{4,16},{5,17},{6,18},{7,19},{8,28},{9,... | collective-permute-start | bytes 786440 | tf_op jit(solution)/shard_map/ppermute | solution.py:43
  98.9 44.7 %collective-permute-start.18 = (bf16[256,1024]{0,1:T(8,128)(2,1)S(1)}, bf16[256,1024]{0,1:T(8,128)(2,1)}, u32[]{:S(2)}, u32[]{:S(2)}) collective-permute-start(bf16[256,1024]{0,1:T(8,128)(2,1)S(1)} %get-tuple-element.203), channel_id=1, source_target_pairs={{0,2},{1,3},{2,0},{3,1},{4,6},{5,7},{6,4},{7,5},{8,10},{9,11},{10,... | collective-permute-start | bytes 1572872 | tf_op jit(solution)/shard_map/ppermute | solution.py:43
  100.7 42.8 %collective-permute-start.17 = (bf16[256,1024]{0,1:T(8,128)(2,1)S(1)}, bf16[256,1024]{0,1:T(8,128)(2,1)}, u32[]{:S(2)}, u32[]{:S(2)}) collective-permute-start(bf16[256,1024]{0,1:T(8,128)(2,1)S(1)} %get-tuple-element.203), channel_id=1, source_target_pairs={{0,1},{1,0},{2,3},{3,2},{4,5},{5,4},{6,7},{7,6},{8,9},{9,8},{10,11... | collective-permute-start | bytes 1572872 | tf_op jit(solution)/shard_map/ppermute | solution.py:43
  114.4 32.0 %collective-permute-start.12 = (bf16[128,1024]{1,0:T(8,128)(2,1)S(1)}, bf16[128,1024]{1,0:T(8,128)(2,1)S(1)}, u32[]{:S(2)}, u32[]{:S(2)}) collective-permute-start(bf16[128,1024]{1,0:T(8,128)(2,1)S(1)} %get-tuple-element.208), channel_id=1, source_target_pairs={{0,20},{1,21},{2,22},{3,23},{4,16},{5,17},{6,18},{7,19},{8,28},{9,... | collective-permute-start | bytes 786440 | tf_op jit(solution)/shard_map/ppermute | solution.py:43
  114.8 31.7 %collective-permute-start.11 = (bf16[128,1024]{1,0:T(8,128)(2,1)S(1)}, bf16[128,1024]{1,0:T(8,128)(2,1)S(1)}, u32[]{:S(2)}, u32[]{:S(2)}) collective-permute-start(bf16[128,1024]{1,0:T(8,128)(2,1)S(1)} %get-tuple-element.209), channel_id=1, source_target_pairs={{0,16},{1,17},{2,18},{3,19},{4,20},{5,21},{6,22},{7,23},{8,24},{9,... | collective-permute-start | bytes 786440 | tf_op jit(solution)/shard_map/ppermute | solution.py:43
  202.5 42.9 %collective-permute-start.38 = (bf16[256,1024]{0,1:T(8,128)(2,1)S(1)}, bf16[256,1024]{0,1:T(8,128)(2,1)S(1)}, u32[]{:S(2)}, u32[]{:S(2)}) collective-permute-start(bf16[256,1024]{0,1:T(8,128)(2,1)S(1)} %copy-done.34), channel_id=1, source_target_pairs={{0,2},{1,3},{2,0},{3,1},{4,6},{5,7},{6,4},{7,5},{8,10},{9,11},{10,... | collective-permute-start | bytes 1572872 | tf_op jit(solution)/shard_map/ppermute | solution.py:43
  207.3 38.2 %collective-permute-start.37 = (bf16[256,1024]{0,1:T(8,128)(2,1)S(1)}, bf16[256,1024]{0,1:T(8,128)(2,1)S(1)}, u32[]{:S(2)}, u32[]{:S(2)}) collective-permute-start(bf16[256,1024]{0,1:T(8,128)(2,1)S(1)} %copy-done.34), channel_id=1, source_target_pairs={{0,1},{1,0},{2,3},{3,2},{4,5},{5,4},{6,7},{7,6},{8,9},{9,8},{10,11... | collective-permute-start | bytes 1572872 | tf_op jit(solution)/shard_map/ppermute | solution.py:43
  212.7 36.9 %collective-permute-start.30 = (bf16[128,1024]{1,0:T(8,128)(2,1)S(1)}, bf16[128,1024]{1,0:T(8,128)(2,1)S(1)}, u32[]{:S(2)}, u32[]{:S(2)}) collective-permute-start(bf16[128,1024]{1,0:T(8,128)(2,1)S(1)} %add_convert_fusion.7), channel_id=1, source_target_pairs={{0,20},{1,21},{2,22},{3,23},{4,16},{5,17},{6,18},{7,19},{8,28},{9,... | collective-permute-start | bytes 786440 | tf_op jit(solution)/shard_map/ppermute | solution.py:43
  213.1 36.4 %collective-permute-start.29 = (bf16[128,1024]{1,0:T(8,128)(2,1)S(1)}, bf16[128,1024]{1,0:T(8,128)(2,1)S(1)}, u32[]{:S(2)}, u32[]{:S(2)}) collective-permute-start(bf16[128,1024]{1,0:T(8,128)(2,1)S(1)} %add_convert_fusion.7), channel_id=1, source_target_pairs={{0,16},{1,17},{2,18},{3,19},{4,20},{5,21},{6,22},{7,23},{8,24},{9,... | collective-permute-start | bytes 786440 | tf_op jit(solution)/shard_map/ppermute | solution.py:43
  218.0 31.5 %collective-permute-start.28 = (bf16[128,1024]{1,0:T(8,128)(2,1)S(1)}, bf16[128,1024]{1,0:T(8,128)(2,1)S(1)}, u32[]{:S(2)}, u32[]{:S(2)}) collective-permute-start(bf16[128,1024]{1,0:T(8,128)(2,1)S(1)} %add_convert_fusion.7), channel_id=1, source_target_pairs={{0,4},{1,5},{2,6},{3,7},{4,0},{5,1},{6,2},{7,3},{8,12},{9,13},{10,... | collective-permute-start | bytes 786440 | tf_op jit(solution)/shard_map/ppermute | solution.py:43
  247.0 36.4 %collective-permute-start.40 = (bf16[4,256,1024]{1,2,0:T(8,128)(2,1)}, bf16[4,256,1024]{1,2,0:T(8,128)(2,1)}, u32[]{:S(2)}, u32[]{:S(2)}) collective-permute-start(bf16[4,256,1024]{1,2,0:T(8,128)(2,1)} %pad_maximum_fusion.5), channel_id=1, source_target_pairs={{0,8},{1,9},{2,10},{3,11},{4,12},{5,13},{6,14},{7,15},{8,0},{9,1},... | collective-permute-start | bytes 6291464 | tf_op jit(solution)/shard_map/ppermute | solution.py:43
  476.7 80.6 %collective-permute-start.73 = (bf16[4,400,1024]{2,1,0:T(8,128)(2,1)}, bf16[4,400,1024]{2,1,0:T(8,128)(2,1)}, u32[]{:S(2)}, u32[]{:S(2)}) collective-permute-start(bf16[4,400,1024]{2,1,0:T(8,128)(2,1)} %concatenate.144), channel_id=1, source_target_pairs={{0,8},{1,9},{2,10},{3,11},{4,12},{5,13},{6,14},{7,15},{8,0},{9,1},... | collective-permute-start | bytes 9830408 | tf_op jit(solution)/shard_map/ppermute | solution.py:43
  499.6 69.5 %collective-permute-start.77 = (bf16[4,400,1024]{2,1,0:T(8,128)(2,1)}, bf16[4,400,1024]{2,1,0:T(8,128)(2,1)}, u32[]{:S(2)}, u32[]{:S(2)}) collective-permute-start(bf16[4,400,1024]{2,1,0:T(8,128)(2,1)} %concatenate.151), channel_id=1, source_target_pairs={{0,8},{1,9},{2,10},{3,11},{4,12},{5,13},{6,14},{7,15},{8,0},{9,1},... | collective-permute-start | bytes 9830408 | tf_op jit(solution)/shard_map/ppermute | solution.py:43
  568.5 104.7 %collective-permute-start.75 = (bf16[400,1024]{1,0:T(8,128)(2,1)S(1)}, bf16[400,1024]{1,0:T(8,128)(2,1)S(1)}, u32[]{:S(2)}, u32[]{:S(2)}) collective-permute-start(bf16[400,1024]{1,0:T(8,128)(2,1)S(1)} %get-tuple-element.171), channel_id=1, source_target_pairs={{0,2},{1,3},{2,0},{3,1},{4,6},{5,7},{6,4},{7,5},{8,10},{9,11},{10,... | collective-permute-start | bytes 2457608 | tf_op jit(solution)/shard_map/ppermute | solution.py:43
  568.5 104.7 %collective-permute-start.74 = (bf16[400,1024]{1,0:T(8,128)(2,1)S(1)}, bf16[400,1024]{1,0:T(8,128)(2,1)S(1)}, u32[]{:S(2)}, u32[]{:S(2)}) collective-permute-start(bf16[400,1024]{1,0:T(8,128)(2,1)S(1)} %get-tuple-element.169), channel_id=1, source_target_pairs={{0,1},{1,0},{2,3},{3,2},{4,5},{5,4},{6,7},{7,6},{8,9},{9,8},{10,11... | collective-permute-start | bytes 2457608 | tf_op jit(solution)/shard_map/ppermute | solution.py:43
  572.7 100.5 %collective-permute-start.80 = (bf16[400,1024]{1,0:T(8,128)(2,1)S(1)}, bf16[400,1024]{1,0:T(8,128)(2,1)S(1)}, u32[]{:S(2)}, u32[]{:S(2)}) collective-permute-start(bf16[400,1024]{1,0:T(8,128)(2,1)S(1)} %get-tuple-element.167), channel_id=1, source_target_pairs={{0,3},{1,2},{2,1},{3,0},{4,7},{5,6},{6,5},{7,4},{8,11},{9,10},{10,... | collective-permute-start | bytes 2457608 | tf_op jit(solution)/shard_map/ppermute | solution.py:43
  576.5 131.0 %collective-permute-start.79 = (bf16[400,1024]{1,0:T(8,128)(2,1)S(1)}, bf16[400,1024]{1,0:T(8,128)(2,1)S(1)}, u32[]{:S(2)}, u32[]{:S(2)}) collective-permute-start(bf16[400,1024]{1,0:T(8,128)(2,1)S(1)} %get-tuple-element.168), channel_id=1, source_target_pairs={{0,2},{1,3},{2,0},{3,1},{4,6},{5,7},{6,4},{7,5},{8,10},{9,11},{10,... | collective-permute-start | bytes 2457608 | tf_op jit(solution)/shard_map/ppermute | solution.py:43
  587.7 119.8 %collective-permute-start.78 = (bf16[400,1024]{1,0:T(8,128)(2,1)S(1)}, bf16[400,1024]{1,0:T(8,128)(2,1)S(1)}, u32[]{:S(2)}, u32[]{:S(2)}) collective-permute-start(bf16[400,1024]{1,0:T(8,128)(2,1)S(1)} %get-tuple-element.166), channel_id=1, source_target_pairs={{0,1},{1,0},{2,3},{3,2},{4,5},{5,4},{6,7},{7,6},{8,9},{9,8},{10,11... | collective-permute-start | bytes 2457608 | tf_op jit(solution)/shard_map/ppermute | solution.py:43
  709.8 37.0 %collective-permute-start.82 = (bf16[400,1024]{1,0:T(8,128)(2,1)S(1)}, bf16[400,1024]{1,0:T(8,128)(2,1)S(1)}, u32[]{:S(2)}, u32[]{:S(2)}) collective-permute-start(bf16[400,1024]{1,0:T(8,128)(2,1)S(1)} %get-tuple-element.128), channel_id=1, source_target_pairs={{0,16},{1,17},{2,18},{3,19},{4,20},{5,21},{6,22},{7,23},{8,24},{9,... | collective-permute-start | bytes 2457608 | tf_op jit(solution)/shard_map/ppermute | solution.py:43
  711.6 35.6 %collective-permute-start.81 = (bf16[400,1024]{1,0:T(8,128)(2,1)S(1)}, bf16[400,1024]{1,0:T(8,128)(2,1)S(1)}, u32[]{:S(2)}, u32[]{:S(2)}) collective-permute-start(bf16[400,1024]{1,0:T(8,128)(2,1)S(1)} %broadcast_select_fusion), channel_id=1, source_target_pairs={{0,4},{1,5},{2,6},{3,7},{4,0},{5,1},{6,2},{7,3},{8,12},{9,13},{10,... | collective-permute-start | bytes 2457608 | tf_op jit(solution)/shard_map/ppermute | solution.py:43
  750.5 111.2 %collective-permute-start.84 = (bf16[4,400,1024]{2,1,0:T(8,128)(2,1)}, bf16[4,400,1024]{2,1,0:T(8,128)(2,1)}, u32[]{:S(2)}, u32[]{:S(2)}) collective-permute-start(bf16[4,400,1024]{2,1,0:T(8,128)(2,1)} %get-tuple-element.165), channel_id=1, source_target_pairs={{0,8},{1,9},{2,10},{3,11},{4,12},{5,13},{6,14},{7,15},{8,0},{9,1},... | collective-permute-start | bytes 9830408 | tf_op jit(solution)/shard_map/ppermute | solution.py:43
  791.0 69.7 %collective-permute-start.71 = (bf16[128,1024]{1,0:T(8,128)(2,1)S(1)}, bf16[128,1024]{1,0:T(8,128)(2,1)S(1)}, u32[]{:S(2)}, u32[]{:S(2)}) collective-permute-start(bf16[128,1024]{1,0:T(8,128)(2,1)S(1)} %get-tuple-element.131), channel_id=1, source_target_pairs={{0,0},{1,16},{2,4},{3,20},{4,1},{5,17},{6,5},{7,21},{8,8},{9,24},{... | collective-permute-start | bytes 786440 | tf_op jit(solution)/shard_map/ppermute | solution.py:43
  791.7 69.0 %collective-permute-start.72 = (bf16[128,1024]{1,0:T(8,128)(2,1)S(1)}, bf16[128,1024]{1,0:T(8,128)(2,1)S(1)}, u32[]{:S(2)}, u32[]{:S(2)}) collective-permute-start(bf16[128,1024]{1,0:T(8,128)(2,1)S(1)} %broadcast_select_fusion.6), channel_id=1, source_target_pairs={{0,4},{1,20},{2,0},{3,16},{4,5},{5,21},{6,1},{7,17},{8,12},{9,28},... | collective-permute-start | bytes 786440 | tf_op jit(solution)/shard_map/ppermute | solution.py:43
  (231 other events, 2771.7 us)

commit v2 on v1

v2 whole, which is shorter than its diff:
```python
from functools import partial

import jax
import jax.numpy as jnp
from jax import lax
from jax.experimental import pallas as pl
from jax.experimental.pallas import tpu as pltpu
from jax.sharding import PartitionSpec as P

HD = 64
SEQ = 512
SHARE = 128
WIDE = 1024
HEADS = 4
HALF = 32
ATTN = 144
FEED = 272
AXES = ("dp", "section", "mp")
EPSILON = 1e-05
NEGATIVE = -1e30
F32 = jnp.float32
BF16 = jnp.bfloat16
VMEM = pl.BlockSpec(memory_space=pltpu.VMEM)
ANY = pl.BlockSpec(memory_space=pl.ANY)
SMEM = pl.BlockSpec(memory_space=pltpu.SMEM)


def dot_nt(left, right):
    return lax.dot_general(left, right, (((1,), (1,)), ((), ())), preferred_element_type=F32)


def dot_nn(left, right):
    return lax.dot_general(left, right, (((1,), (0,)), ((), ())), preferred_element_type=F32)


def dot_tn(left, right):
    return lax.dot_general(left, right, (((0,), (0,)), ((), ())), preferred_element_type=F32)


def shape(dims, dtype=BF16):
    return jax.ShapeDtypeStruct(dims, dtype)


def call(kernel, name, ins, outs, scratch=(), flops=0, moved=0, limit=40):
    return pl.pallas_call(
        kernel,
        name=name,
        in_specs=ins,
        out_specs=tuple(VMEM for _ in outs),
        out_shape=tuple(outs),
        scratch_shapes=list(scratch),
        compiler_params=pltpu.CompilerParams(vmem_limit_bytes=limit << 20),
        cost_estimate=pl.CostEstimate(flops=flops, bytes_accessed=moved, transcendentals=0),
    )


def at_rows(rows, values):
    place = lax.broadcasted_iota(jnp.int32, (rows, values[0].shape[1]), 0)
    block = jnp.zeros((rows, values[0].shape[1]), F32)
    for i, value in enumerate(values):
        block = jnp.where(place == i, value, block)
    return block


def columns(i, width=256):
    return pl.ds(pl.multiple_of(i * width, width), width)


def prep_attn_kernel(place, wq, wk, wv, wo, bq, bv, v0, v1, v2, v3, v4, v5, own, peer, turned):
    core, quarter = place[0], place[1]
    for a, w in enumerate((wq, wk, wv)):
        turned[a] = w[0].T
    layer_rows = [v[...].astype(F32) for v in (v0, v1, v2, v3, v4, v5)]
    source = lax.broadcasted_iota(jnp.int32, (256, 128), 0)
    lane = lax.broadcasted_iota(jnp.int32, (256, 128), 1)
    for out, block in ((own, quarter), (peer, quarter ^ 1)):
        head = pl.multiple_of(block * HD + core * HALF, HALF)
        for a in range(3):
            out[HALF * a : HALF * a + HALF] = turned[a, pl.ds(head, HALF)]
        out[3 * HALF : 4 * HALF] = wo[0, pl.ds(head, HALF)]
        inner = lane & 63
        wanted = block * HD + (inner ^ (core * HALF))
        hit = source == wanted
        zero = jnp.zeros((256, 128), F32)
        one = jnp.ones((256, 128), F32)
        first = jnp.where(hit & (lane < 64), one, zero).astype(BF16)
        second = jnp.where(hit & (lane >= 64), one, zero).astype(BF16)
        bias = dot_nn(jnp.broadcast_to(bq[...], (16, 256)), first) + dot_nn(
            jnp.broadcast_to(bv[...], (16, 256)), second
        )
        rows = lax.broadcasted_iota(jnp.int32, (16, WIDE), 0)
        block_rows = jnp.zeros((16, WIDE), F32)
        for i, row in enumerate(layer_rows):
            block_rows = jnp.where(rows == i + 1, row, block_rows)
        out[128:144] = block_rows.astype(BF16)
        first_row = lax.broadcasted_iota(jnp.int32, (16, 128), 0) == 0
        out[128:144, 0:128] = jnp.where(first_row, bias, block_rows[:, 0:128]).astype(BF16)


def prep_feed_kernel(place, up, down, bu, own, peer, column, sems):
    core, quarter = place[0], place[1]
    copies = []
    for i, block in enumerate((quarter, quarter ^ 1)):
        unit = pl.multiple_of(block * 256 + core * 128, 128)
        copy = pltpu.make_async_copy(up.at[0, :, pl.ds(unit, 128)], column.at[i], sems.at[2 * i])
        copy.start()
        out = (own, peer)[i]
        other = pltpu.make_async_copy(
            down.at[0, pl.ds(unit, 128)], out.at[128:256], sems.at[2 * i + 1]
        )
        other.start()
        copies.append((copy, other))
    row = lax.broadcasted_iota(jnp.int32, (16, 128), 0) == 0
    for i, block in enumerate((quarter, quarter ^ 1)):
        out = (own, peer)[i]
        out[256:272] = jnp.zeros((16, WIDE), BF16)
        for h in range(2):
            unit = pl.multiple_of(block * 256 + (core ^ h) * 128, 128)
            piece = bu[:, pl.ds(unit, 128)].astype(F32)
            out[256:272, 128 * h : 128 * h + 128] = jnp.where(row, piece, 0.0).astype(BF16)
        copies[i][0].wait()
        out[0:128] = column[i].T
        copies[i][1].wait()


def layer_rows(ref, *which):
    block = ref[...].astype(F32)
    return [block[i : i + 1] for i in which]


def norm_forward(hidden, gain, offset):
    centre = jnp.mean(hidden, -1, keepdims=True)
    centred = hidden - centre
    variance = jnp.mean(centred * centred, -1, keepdims=True)
    inverse = lax.rsqrt(variance + EPSILON)
    normed = centred * inverse
    return (normed * gain + offset, normed, inverse)


def norm_backward(upstream, normed, inverse, gain):
    scaled = upstream * gain
    return inverse * (
        scaled
        - jnp.mean(scaled, -1, keepdims=True)
        - normed * jnp.mean(scaled * normed, -1, keepdims=True)
    )


def norm_kernel(first, own, r1, r2, r3, residual, vec, result, low, normed, inverse):
    bias, gain, offset = layer_rows(vec, *((1, 2, 3) if first else (4, 5, 6)))
    hidden = residual[...].astype(F32) + (
        own[...] + r1[...].astype(F32) + r2[...].astype(F32) + r3[...].astype(F32)
    ) + bias
    value, normed[...], inverse[...] = norm_forward(hidden, gain, offset)
    result[...] = value
    low[...] = value.astype(BF16)


def sums(*values):
    return at_rows(8, [jnp.sum(v, 0, keepdims=True) for v in values])


def norm_two_back_kernel(upstream, normed, inverse, vec, total, low, vectors):
    grad = upstream[...].astype(F32)
    (gain,) = layer_rows(vec, 5)
    value = norm_backward(grad, normed[...], inverse[...], gain)
    rounded = value.astype(BF16)
    total[...] = value
    low[...] = rounded
    vectors[...] = sums(rounded.astype(F32), grad * normed[...], grad)


def norm_two_back_sum_kernel(
    before, own, r1, r2, r3, normed, inverse, vec, total, low, vectors, given
):
    given[...] = (
        before[...]
        + own[...]
        + r1[...].astype(F32)
        + r2[...].astype(F32)
        + r3[...].astype(F32)
    ).astype(BF16)
    norm_two_back_kernel(given, normed, inverse, vec, total, low, vectors)


def norm_one_back_kernel(before, own, r1, r2, r3, normed, inverse, vec, total, low, vectors):
    grad = (
        before[...]
        + own[...]
        + r1[...].astype(F32)
        + r2[...].astype(F32)
        + r3[...].astype(F32)
    )
    (gain,) = layer_rows(vec, 2)
    value = norm_backward(grad, normed[...], inverse[...], gain)
    rounded = value.astype(BF16)
    total[...] = value
    low[...] = rounded
    vectors[...] = sums(rounded.astype(F32), grad * normed[...], grad)


def load_attn(own, other, weight, sems):
    copies = []
    for half, ref in enumerate((own, other)):
        for a in range(4):
            copies.append(
                pltpu.make_async_copy(
                    ref.at[:, HALF * a : HALF * a + HALF],
                    weight.at[a, :, half],
                    sems.at[half * 4 + a],
                )
            )
    return copies


def join(target, pieces):
    for i, piece in enumerate(pieces):
        target[SHARE * i : SHARE * i + SHARE] = piece[...]


def spread_out(value, where, own, parts):
    own[:, where] = value[0:SHARE]
    for i, part in enumerate(parts):
        part[:, where] = value[SHARE * (i + 1) : SHARE * (i + 2)].astype(BF16)


def attn_kernel(
    x0, x1, x2, x3, a_own, a_other, id_column, id_row,
    own, p1, p2, p3, qkv, probs, mixed,
    weight, small, x_all, sems,
):
    copies = load_attn(a_own, a_other, weight, sems)
    copies.append(pltpu.make_async_copy(a_own.at[:, 128:144], small, sems.at[8]))
    for copy in copies:
        copy.start()
    join(x_all, (x0, x1, x2, x3))
    for copy in copies:
        copy.wait()
    biases = [small[z].astype(F32)[0:1] for z in range(4)]
    bias_of = (
        jnp.concatenate([b[:, 0:64] for b in biases], 1),
        None,
        jnp.concatenate([b[:, 64:128] for b in biases], 1),
    )
    x = x_all[...]
    for a in range(3):
        rows = dot_nt(x, weight[a].reshape(256, WIDE))
        if bias_of[a] is not None:
            rows = rows + bias_of[a]
        qkv[:, 256 * a : 256 * a + 256] = rows.astype(BF16)
    for c in range(2):
        q_rows = slice(256 * c, 256 * c + 256)
        allowed = id_column[q_rows] == id_row[...]
        for h in range(HEADS):
            query = qkv[q_rows, HD * h : HD * h + HD]
            key = qkv[:, 256 + HD * h : 256 + HD * h + HD]
            value = qkv[:, 512 + HD * h : 512 + HD * h + HD]
            scores = jnp.where(allowed, dot_nt(query, key) * HD ** (-0.5), NEGATIVE)
            exponent = jnp.exp(scores - jnp.max(scores, -1, keepdims=True))
            low = (exponent / jnp.sum(exponent, -1, keepdims=True)).astype(BF16)
            probs[h, q_rows] = low
            mixed[q_rows, HD * h : HD * h + HD] = dot_nn(low, value).astype(BF16)
    out = weight[3].reshape(256, WIDE)
    for n in range(4):
        where = slice(256 * n, 256 * n + 256)
        spread_out(dot_nn(mixed[...], out[:, where]), where, own, (p1, p2, p3))


def attn_back_kernel(
    g0, g1, g2, g3, a_own, a_other, qkv, probs,
    own, p1, p2, p3, d_rows,
    weight, g_all, sems,
):
    copies = load_attn(a_own, a_other, weight, sems)
    for copy in copies:
        copy.start()
    join(g_all, (g0, g1, g2, g3))
    for copy in copies:
        copy.wait()
    d_mixed = dot_nt(g_all[...], weight[3].reshape(256, WIDE)).astype(BF16)
    scale = HD ** (-0.5)
    for h in range(HEADS):
        query = qkv[:, HD * h : HD * h + HD]
        key = qkv[:, 256 + HD * h : 256 + HD * h + HD]
        value = qkv[:, 512 + HD * h : 512 + HD * h + HD]
        grad = d_mixed[:, HD * h : HD * h + HD]
        d_key = jnp.zeros((SEQ, HD), F32)
        d_value = jnp.zeros((SEQ, HD), F32)
        for c in range(2):
            q_rows = slice(256 * c, 256 * c + 256)
            low = probs[h, q_rows]
            p = low.astype(F32)
            d_probs = dot_nt(grad[q_rows], value)
            inner = jnp.sum(p * d_probs, -1, keepdims=True)
            d_scores = (p * (d_probs - inner)).astype(BF16)
            d_rows[q_rows, HD * h : HD * h + HD] = (dot_nn(d_scores, key) * scale).astype(BF16)
            d_key = d_key + dot_tn(d_scores, query[q_rows])
            d_value = d_value + dot_tn(low, grad[q_rows])
        d_rows[:, 256 + HD * h : 256 + HD * h + HD] = (d_key * scale).astype(BF16)
        d_rows[:, 512 + HD * h : 512 + HD * h + HD] = d_value.astype(BF16)
    rows = d_rows[...]
    for n in range(4):
        where = slice(256 * n, 256 * n + 256)
        w = weight[0:3, :, :, :, where].reshape(768, 256)
        spread_out(dot_nn(rows, w), where, own, (p1, p2, p3))


def attn_weights_kernel(
    d_rows, mixed, x0, x1, x2, x3, g0, g1, g2, g3, vec_one, vec_two, own, other, x_all, g_all
):
    join(x_all, (x0, x1, x2, x3))
    join(g_all, (g0, g1, g2, g3))
    for a in range(4):
        if a < 3:
            value = dot_tn(d_rows[:, 256 * a : 256 * a + 256], x_all[...])
        else:
            value = dot_tn(mixed[...], g_all[...])
        value = value.astype(BF16).reshape(4, 2, HALF, WIDE)
        own[:, HALF * a : HALF * a + HALF] = value[:, 0]
        other[:, HALF * a : HALF * a + HALF] = value[:, 1]
    total = jnp.sum(d_rows[...].astype(F32), 0, keepdims=True)
    one, two = vec_one[...], vec_two[...]
    vectors = [one[i : i + 1] for i in range(3)] + [two[i : i + 1] for i in range(3)]
    block = at_rows(16, [jnp.zeros((1, WIDE), F32)] + vectors)
    first_row = lax.broadcasted_iota(jnp.int32, (16, 128), 0) == 0
    for half, out in enumerate((own, other)):
        for z in range(4):
            start = HD * z + HALF * half
            bias = jnp.concatenate(
                [
                    total[:, start : start + HALF],
                    total[:, 512 + start : 512 + start + HALF],
                    jnp.zeros((1, 64), F32),
                ],
                1,
            )
            out[z, 128:144] = block.astype(BF16)
            out[z, 128:144, 0:128] = jnp.where(first_row, bias, block[:, 0:128]).astype(BF16)


def load_feed(own, other, up, down, sems):
    ups, downs = [], []
    for half, ref in enumerate((own, other)):
        ups.append(
            pltpu.make_async_copy(
                ref.at[:, 0:128], up.at[4 * half : 4 * half + 4], sems.at[2 * half]
            )
        )
        downs.append(
            pltpu.make_async_copy(
                ref.at[:, 128:256], down.at[4 * half : 4 * half + 4], sems.at[2 * half + 1]
            )
        )
    return ups, downs


def feed_kernel(
    x0, x1, x2, x3, f_own, f_other,
    own, p1, p2, p3, active, slope,
    up, down, small, bias, x_all, sems,
):
    ups, downs = load_feed(f_own, f_other, up, down, sems)
    copies = [pltpu.make_async_copy(f_own.at[:, 256:272], small, sems.at[4])] + ups
    for copy in copies + downs:
        copy.start()
    join(x_all, (x0, x1, x2, x3))
    for copy in copies:
        copy.wait()
    for half in range(2):
        for z in range(4):
            unit = 512 * half + 128 * z
            bias[0:8, unit : unit + 128] = jnp.broadcast_to(
                small[z, :, 128 * half : 128 * half + 128].astype(F32)[0:1], (8, 128)
            )

    def units(i, carry):
        block = up[pl.ds(2 * i, 2)].reshape(256, WIDE)
        hidden = dot_nt(x_all[...], block) + bias[0:1, columns(i)]
        share = 0.5 * (1.0 + lax.erf(hidden * (0.5 ** 0.5)))
        density = jnp.exp(-0.5 * hidden * hidden) * 0.3989422804014327
        active[:, columns(i)] = (hidden * share).astype(BF16)
        slope[:, columns(i)] = (share + hidden * density).astype(BF16)
        return carry

    lax.fori_loop(0, 4, units, 0)
    for copy in downs:
        copy.wait()

    def features(n, carry):
        block = down[:, :, columns(n)].reshape(WIDE, 256)
        spread_out(dot_nn(active[...], block), columns(n), own, (p1, p2, p3))
        return carry

    lax.fori_loop(0, 4, features, 0)


def feed_back_kernel(
    g0, g1, g2, g3, f_own, f_other, slope,
    own, p1, p2, p3, d_hidden,
    up, down, g_all, sems,
):
    ups, downs = load_feed(f_own, f_other, up, down, sems)
    for copy in downs + ups:
        copy.start()
    join(g_all, (g0, g1, g2, g3))
    for copy in downs:
        copy.wait()

    def units(i, carry):
        block = down[pl.ds(2 * i, 2)].reshape(256, WIDE)
        value = dot_nt(g_all[...], block) * slope[:, columns(i)].astype(F32)
        d_hidden[:, columns(i)] = value.astype(BF16)
        return carry

    lax.fori_loop(0, 4, units, 0)
    for copy in ups:
        copy.wait()

    def features(n, carry):
        block = up[:, :, columns(n)].reshape(WIDE, 256)
        spread_out(dot_nn(d_hidden[...], block), columns(n), own, (p1, p2, p3))
        return carry

    lax.fori_loop(0, 4, features, 0)


def feed_weights_kernel(
    d_hidden, active, x0, x1, x2, x3, g0, g1, g2, g3, own, other, x_all, g_all
):
    join(x_all, (x0, x1, x2, x3))
    join(g_all, (g0, g1, g2, g3))
    row = lax.broadcasted_iota(jnp.int32, (16, 128), 0) == 0
    for half, out in enumerate((own, other)):

        def pair(i, carry, half=half, out=out):
            where = columns(2 * half + i)
            value = dot_tn(d_hidden[:, where], x_all[...]).astype(BF16)
            out[pl.ds(2 * i, 2), 0:128] = value.reshape(2, 128, WIDE)
            value = dot_tn(active[:, where], g_all[...]).astype(BF16)
            out[pl.ds(2 * i, 2), 128:256] = value.reshape(2, 128, WIDE)
            return carry

        lax.fori_loop(0, 2, pair, 0)
        total = jnp.sum(d_hidden[:, 512 * half : 512 * half + 512].astype(F32), 0, keepdims=True)
        for z in range(4):
            out[z, 256:272] = jnp.zeros((16, WIDE), BF16)
            out[z, 256:272, 0:128] = jnp.where(row, total[:, 128 * z : 128 * z + 128], 0.0).astype(
                BF16
            )


def finish_attn_kernel(place, pieces, gq, gk, gv, go, small, turned, extra, sems):
    copies = []
    for j in range(4):
        for h in range(2):
            index = place[2 * j + h]
            i = 2 * j + h
            copies.append(
                pltpu.make_async_copy(pieces.at[index, 128:144], extra.at[i], sems.at[4, i])
            )
            for a in range(4):
                copies.append(
                    pltpu.make_async_copy(
                        pieces.at[index, HALF * a : HALF * a + HALF],
                        turned.at[a, j, h],
                        sems.at[a, i],
                    )
                )
    for copy in copies:
        copy.start()
    for copy in copies:
        copy.wait()
    for a, out in enumerate((gq, gk, gv)):
        out[0] = turned[a].reshape(256, WIDE).astype(F32).T
    go[0] = turned[3].reshape(256, WIDE).astype(F32)
    small[...] = extra[...]


def finish_feed_kernel(place, pieces, gu, gd, small, block, sems):
    copies = []
    for i in range(8):
        index = place[i]
        copy = pltpu.make_async_copy(pieces.at[index], block.at[i], sems.at[i])
        copy.start()
        copies.append(copy)
    for i in range(8):
        copies[i].wait()
        gu[0, :, 128 * i : 128 * i + 128] = block[i, 0:128].astype(F32).T
        gd[0, 128 * i : 128 * i + 128] = block[i, 128:256].astype(F32)
        small[i] = block[i, 256:272]


MAC_FEED = 2 * SEQ * WIDE * WIDE
TOKEN = [VMEM] * 4
PARTS = [shape((SHARE, WIDE), F32)] + [shape((SHARE, WIDE))] * 3
DMA = pltpu.SemaphoreType.DMA


def scratch(dims, dtype=BF16):
    return pltpu.VMEM(dims, dtype)


prep_attn = call(
    prep_attn_kernel,
    "pack_attention",
    [SMEM] + [VMEM] * 12,
    [shape((ATTN, WIDE))] * 2,
    [scratch((3, 256, WIDE))],
    moved=4 << 20,
)
prep_feed = call(
    prep_feed_kernel,
    "pack_feed",
    [SMEM, ANY, ANY, VMEM],
    [shape((FEED, WIDE))] * 2,
    [scratch((2, WIDE, 128)), DMA((4,))],
    moved=2 << 20,
)
VEC = VMEM
NORMS = [
    shape((SHARE, WIDE), F32),
    shape((SHARE, WIDE)),
    shape((SHARE, WIDE), F32),
    shape((SHARE, 1), F32),
]
norm_one, norm_two = (
    call(partial(norm_kernel, first), name, [VMEM] * 5 + [VEC], NORMS, moved=3 << 20)
    for first, name in ((True, "norm_one"), (False, "norm_two"))
)
BACKS = [shape((SHARE, WIDE), F32), shape((SHARE, WIDE)), shape((8, WIDE), F32)]
norm_two_back = call(
    norm_two_back_kernel, "norm_two_back", [VMEM] * 3 + [VEC], BACKS, moved=3 << 20
)
norm_two_back_sum = call(
    norm_two_back_sum_kernel,
    "norm_two_back_sum",
    [VMEM] * 7 + [VEC],
    BACKS + [shape((SHARE, WIDE))],
    moved=3 << 20,
)
norm_one_back = call(
    norm_one_back_kernel, "norm_one_back", [VMEM] * 7 + [VEC], BACKS, moved=3 << 20
)
attn_forward = call(
    attn_kernel,
    "attention",
    TOKEN + [ANY, ANY, VMEM, VMEM],
    PARTS + [shape((SEQ, 768)), shape((HEADS, SEQ, SEQ)), shape((SEQ, 256))],
    [
        scratch((4, 4, 2, HALF, WIDE)),
        scratch((4, 16, WIDE)),
        scratch((SEQ, WIDE)),
        DMA((9,)),
    ],
    flops=2 * MAC_FEED,
    moved=8 << 20,
)
attn_backward = call(
    attn_back_kernel,
    "attention_back",
    TOKEN + [ANY, ANY, VMEM, VMEM],
    PARTS + [shape((SEQ, 768))],
    [scratch((4, 4, 2, HALF, WIDE)), scratch((SEQ, WIDE)), DMA((8,))],
    flops=3 * MAC_FEED,
    moved=8 << 20,
)
attn_weights = call(
    attn_weights_kernel,
    "attention_weights",
    [VMEM] * 12,
    [shape((4, ATTN, WIDE))] * 2,
    [scratch((SEQ, WIDE)), scratch((SEQ, WIDE))],
    flops=MAC_FEED,
    moved=6 << 20,
)
FEED_SCRATCH = [scratch((8, 128, WIDE)), scratch((8, 128, WIDE))]
feed_forward = call(
    feed_kernel,
    "feed",
    TOKEN + [ANY, ANY],
    PARTS + [shape((SEQ, WIDE))] * 2,
    FEED_SCRATCH
    + [scratch((4, 16, WIDE)), scratch((8, WIDE), F32), scratch((SEQ, WIDE)), DMA((5,))],
    flops=2 * MAC_FEED,
    moved=9 << 20,
)
feed_backward = call(
    feed_back_kernel,
    "feed_back",
    TOKEN + [ANY, ANY, VMEM],
    PARTS + [shape((SEQ, WIDE))],
    FEED_SCRATCH + [scratch((SEQ, WIDE)), DMA((4,))],
    flops=2 * MAC_FEED,
    moved=9 << 20,
)
feed_weights = call(
    feed_weights_kernel,
    "feed_weights",
    [VMEM] * 10,
    [shape((4, FEED, WIDE))] * 2,
    [scratch((SEQ, WIDE)), scratch((SEQ, WIDE))],
    flops=2 * MAC_FEED,
    moved=9 << 20,
)
finish_attn = call(
    finish_attn_kernel,
    "finish_attention",
    [SMEM, ANY],
    [shape((1, WIDE, 256), F32)] * 3 + [shape((1, 256, WIDE), F32), shape((8, 16, WIDE))],
    [scratch((4, 4, 2, HALF, WIDE)), scratch((8, 16, WIDE)), DMA((5, 8))],
    moved=6 << 20,
)
finish_feed = call(
    finish_feed_kernel,
    "finish_feed",
    [SMEM, ANY],
    [shape((1, WIDE, WIDE), F32)] * 2 + [shape((8, 16, WIDE))],
    [scratch((8, FEED, WIDE)), DMA((8,))],
    moved=12 << 20,
)


def mover(sizes, target, takes=None):
    replicas, sections, shards = sizes
    pairs = []
    for d in range(replicas):
        for s in range(sections):
            for z in range(shards):
                if takes is None or takes(d, s, z):
                    nd, ns, nz = target(d, s, z)
                    pairs.append(
                        ((d * sections + s) * shards + z, (nd * sections + ns) * shards + nz)
                    )

    def move(values):
        return lax.ppermute(values, AXES, pairs)

    return move


def solution(mesh):
    replicas, sections, shards = (mesh.shape[name] for name in AXES)
    sizes = (replicas, sections, shards)

    def quarter_of(d, s):
        return 2 * ((d >> 1) & 1) + s

    swap_y = mover(sizes, lambda d, s, z: (d, s ^ 1, z))
    swap_x = mover(sizes, lambda d, s, z: (d ^ 2, s, z))
    swap_xy = mover(sizes, lambda d, s, z: (d ^ 2, s ^ 1, z))
    swap_core = mover(sizes, lambda d, s, z: (d ^ 1, s, z))
    swap_z = [mover(sizes, lambda d, s, z, r=r: (d, s, z ^ r)) for r in range(1, 4)]
    place_in = mover(
        sizes,
        lambda d, s, z: (
            (d & ~2) | ((z >> 1) << 1),
            z & 1,
            2 * (s ^ (z & 1)) + ((d >> 1) & 1),
        ),
    )
    place_out = [
        mover(
            sizes,
            lambda d, s, z, r=r: (
                (d & ~2) | ((z & 1) << 1),
                (z >> 1) ^ r,
                quarter_of(d, s),
            ),
        )
        for r in range(2)
    ]

    def gather(share):
        return (share, swap_y(share), swap_x(share), swap_xy(share))

    def scatter(parts):
        own, p1, p2, p3 = parts
        return (own, swap_y(p1), swap_x(p2), swap_xy(p3))

    def gather_direct(piece):
        return jnp.stack([piece] + [move(piece) for move in swap_z])

    def scatter_direct(pieces):
        total = pieces[0].astype(F32)
        for r in range(1, 4):
            total = total + swap_z[r - 1](pieces[r]).astype(F32)
        return total.astype(BF16)

    def gather_mp(piece):
        return lax.all_gather(piece, "mp", axis=0)

    def scatter_mp(pieces):
        return lax.psum_scatter(pieces, "mp", scatter_dimension=0)

    def to_layers(first, second, section):
        pick = (lax.axis_index("mp") >> 1) == 0
        moved_a = place_out[0](jnp.where(pick, first, second))
        moved_b = place_out[1](jnp.where(pick, second, first))
        is_first = section == 0
        return jnp.stack(
            [jnp.where(is_first, moved_a, moved_b), jnp.where(is_first, moved_b, moved_a)]
        )

    def per_device(
        inputs,
        cotangent,
        doc_ids,
        w_query,
        b_query,
        w_key,
        w_value,
        b_value,
        w_out,
        b_out,
        gain_one,
        shift_one,
        w_up,
        b_up,
        w_down,
        b_down,
        gain_two,
        shift_two,
    ):
        replica = lax.axis_index("dp")
        section = lax.axis_index("section")
        shard = lax.axis_index("mp")
        core = replica & 1
        quarter = quarter_of(replica, section)
        place = jnp.stack([core, quarter]).astype(jnp.int32)

        attn_packs = prep_attn(
            place,
            w_query,
            w_key,
            w_value,
            w_out,
            b_query,
            b_value,
            b_out,
            gain_one,
            shift_one,
            b_down,
            gain_two,
            shift_two,
        )
        feed_packs = prep_feed(place, w_up, w_down, b_up)
        packs = [(own, swap_y(peer)) for own, peer in (attn_packs, feed_packs)]

        which = (section ^ shard) & 1
        share_in = place_in(lax.dynamic_index_in_dim(inputs, which, 0, False))
        share_grad = place_in(lax.dynamic_index_in_dim(cotangent, which, 0, False))
        other_ids = swap_x(doc_ids)
        mine = ((replica >> 1) & 1) == (shard & 1)
        ids = jnp.where(mine, doc_ids, other_ids)
        ids = lax.dynamic_index_in_dim(ids, shard >> 1, 0, False).reshape(4, SHARE)
        ids = jnp.concatenate(
            [lax.dynamic_index_in_dim(ids, quarter ^ r, 0, False) for r in range(4)]
        )
        id_column, id_row = ids[:, None], ids[None, :]

        layers = []
        for layer in range(2):
            attn, feed = (jnp.where(section == layer, own, other) for own, other in packs)
            attn = gather_direct(attn) if layer == 0 else gather_mp(attn)
            feed = gather_mp(feed)
            layers.append((attn, swap_core(attn), feed, swap_core(feed), attn[0, 128:144]))

        def forward(share, weights):
            attn, attn_other, feed, feed_other, vec = weights
            whole = gather(share)
            *parts, qkv, probs, mixed = attn_forward(
                *whole, attn, attn_other, id_column, id_row
            )
            middle, low, normed_one, inverse_one = norm_one(*scatter(parts), share, vec)
            spread = gather(low)
            *parts, active, slope = feed_forward(*spread, feed, feed_other)
            _, result, normed_two, inverse_two = norm_two(*scatter(parts), middle, vec)
            kept = (
                whole,
                qkv,
                probs,
                mixed,
                normed_one,
                inverse_one,
                spread,
                active,
                slope,
                normed_two,
                inverse_two,
            )
            return result, kept

        def backward(given, weights, kept, last):
            attn, attn_other, feed, feed_other, vec = weights
            (
                whole,
                qkv,
                probs,
                mixed,
                normed_one,
                inverse_one,
                spread,
                active,
                slope,
                normed_two,
                inverse_two,
            ) = kept
            grad = None
            if last:
                total, low, vec_two = norm_two_back(given, normed_two, inverse_two, vec)
            else:
                total, low, vec_two, grad = norm_two_back_sum(
                    *given, normed_two, inverse_two, vec
                )
            grads = gather(low)
            *parts, d_hidden = feed_backward(*grads, feed, feed_other, slope)
            feed_grad = feed_weights(d_hidden, active, *spread, *grads)
            total, low, vec_one = norm_one_back(
                total, *scatter(parts), normed_one, inverse_one, vec
            )
            grads = gather(low)
            *parts, d_rows = attn_backward(*grads, attn, attn_other, qkv, probs)
            attn_grad = attn_weights(d_rows, mixed, *whole, *grads, vec_one, vec_two)
            return (total, *scatter(parts)), grad, attn_grad, feed_grad

        def core_sum(halves):
            own, other = halves
            return (own.astype(F32) + swap_core(other).astype(F32)).astype(BF16)

        first, kept_first = forward(share_in, layers[0])
        second, kept_second = forward(first, layers[1])
        section_outputs = to_layers(first, second, section)[None]

        given, _, attn_one, feed_one = backward(share_grad, layers[1], kept_second, True)
        feed_one = scatter_mp(core_sum(feed_one))
        attn_one = scatter_mp(core_sum(attn_one))
        given, grad_one, attn_zero, feed_zero = backward(given, layers[0], kept_first, False)
        grad_zero = sum(part.astype(F32) for part in given).astype(BF16)
        feed_zero = scatter_mp(core_sum(feed_zero))
        attn_zero = scatter_direct(core_sum(attn_zero))

        def exchange(zero, one):
            if replicas > 4:
                groups = [[low + 4 * high for high in range(replicas // 4)] for low in range(4)]
                zero, one = lax.psum((zero, one), "dp", axis_index_groups=groups)
            mine = jnp.where(section == 0, zero, one)
            theirs = jnp.where(section == 0, one, zero)
            pieces = jnp.stack([mine, swap_y(theirs), swap_x(mine), swap_xy(theirs)])
            return jnp.concatenate([pieces, swap_core(pieces)])

        feeds = exchange(feed_zero, feed_one)
        attns = exchange(attn_zero, attn_one)
        order = jnp.stack(
            [(h ^ core) * 4 + (j ^ quarter) for j in range(4) for h in range(2)]
        ).astype(jnp.int32)
        g_up, g_down, feed_small = finish_feed(order, feeds)
        g_query, g_key, g_value, g_out, attn_small = finish_attn(order, attns)
        vectors = jnp.sum(attns[0:4, 128:144].astype(F32), 0)
        bias = attn_small[:, 0].astype(F32)
        g_b_up = feed_small[:, 0, 0:128].astype(F32).reshape(1, WIDE)
        section_input_grads = to_layers(grad_zero, grad_one, section)[None].astype(F32)
        return (
            section_outputs,
            section_input_grads,
            g_query,
            bias[:, 0:HALF].reshape(1, 256),
            g_key,
            g_value,
            bias[:, HALF : 2 * HALF].reshape(1, 256),
            g_out,
            vectors[1:2],
            vectors[2:3],
            vectors[3:4],
            g_up,
            g_b_up,
            g_down,
            vectors[4:5],
            vectors[5:6],
            vectors[6:7],
        )

    vector = P("section", None)
    by_column = P("section", None, "mp")
    by_row = P("section", "mp", None)
    spread = P("section", "mp")
    tokens = P(None, ("dp", "mp"), None)
    layer_tokens = P("section", None, ("dp", "mp"), None)
    return jax.shard_map(
        per_device,
        mesh=mesh,
        in_specs=(
            tokens,
            tokens,
            P(None, "dp", None),
            by_column,
            spread,
            by_column,
            by_column,
            spread,
            by_row,
            vector,
            vector,
            vector,
            by_column,
            spread,
            by_row,
            vector,
            vector,
            vector,
        ),
        out_specs=(
            layer_tokens,
            layer_tokens,
            by_column,
            spread,
            by_column,
            by_column,
            spread,
            by_row,
            vector,
            vector,
            vector,
            by_column,
            spread,
            by_row,
            vector,
            vector,
            vector,
        ),
        check_vma=False,
    )
```

time: 907 us -> 654 us (0.72)
  local copies, waits for them, and re-layouts: 180 us -> 35.4 us
  matrix products: 88.7 us -> 0 us
  Pallas kernels: 0 us -> 79.6 us
  blocking collectives: 62.5 us -> 0 us
  other arithmetic: 61.6 us -> 27 us
  starting transfers between devices: 180 us -> 147 us
  waiting for transfers between devices: 321 us -> 340 us
  between operations: 3.51 us -> 15.3 us
    pallas_call x0 -> x24, Pallas kernels: none -> 79.6 us  [the longest x2 13 us: forward(): attn_forward(*whole, attn, attn_other, id_column, id_row)]
    all_gather x0 -> x3, waiting for transfers between devices: none -> 79.5 us  [gather_mp(): return lax.all_gather(piece, 'mp', axis=0)]
    dot_general x46 -> x0, matrix products: 79.3 us -> none  [the longest x8 25 us: dot_nt(): lax.dot_general(left, right, (((1,), (1,)), ((), ())), preferred_element_...]
    concatenate x7 -> x2, local copies, waits for them, and re-layouts: 78.8 us -> 3.37 us  [exchange(): return jnp.concatenate([pieces, swap_core(pieces)])]
    psum x1 -> x0, blocking collectives: 62.5 us -> none  [per_device(): vectors = lax.psum(jnp.stack(all_vectors), AXES)]
    ppermute x85 -> x79, waiting for transfers between devices: 321 us -> 260 us  [move(): return lax.ppermute(values, AXES, pairs)]
    slice x47 -> x2, local copies, waits for them, and re-layouts: 52.5 us -> 0.69 us  [the longest x1 0.62 us: per_device(): vectors[6:7]]
    ppermute x85 -> x79, starting transfers between devices: 180 us -> 147 us  [move(): return lax.ppermute(values, AXES, pairs)]
  transfers between devices with their start and end apart: 85 -> 85, of which waited for: 42 -> 55; matrix products, arithmetic and copies ran while one was open for 20% -> 5% of each run, Pallas kernels for 0% -> 8%
where the time goes in v2:
time: 654 us; the launch traced here: 645 us
  waiting for transfers between devices  340 us (52%)
  starting transfers between devices  147 us (22%)
  Pallas kernels  79.6 us (12%)
  local copies, waits for them, and re-layouts  35.4 us (5%)
  other arithmetic  27 us (4%)
  between operations  15.3 us (2%)
    ppermute x79, waiting for transfers between devices, move(): return lax.ppermute(values, AXES, pairs)  260 us
    ppermute x79, starting transfers between devices, move(): return lax.ppermute(values, AXES, pairs)  147 us
    all_gather x3, waiting for transfers between devices, gather_mp(): return lax.all_gather(piece, 'mp', axis=0)  79.5 us
    unnamed x157, local copies, waits for them, and re-layouts  29 us
  transfers between devices with their start and end apart: 85, of which 55 were waited for; matrix products, arithmetic and copies ran while one was open for 5% of the time, Pallas kernels for 8%

profile of v2, /device:TPU:0, one launch (start us, length us, event | category | flops | bytes accessed | tf_op | source)
XLA Modules:
  0.0 645.0 jit_solution(9490531924914808774)
XLA Ops:
  16.3 12.9 %collective-permute-done.16 = bf16[272,1024]{1,0:T(8,128)(2,1)} collective-permute-done((bf16[272,1024]{1,0:T(8,128)(2,1)}, bf16[272,1024]{1,0:T(8,128)(2,1)}, u32[]{:S(2)}, u32[]{:S(2)}) %collective-permute-start.16) | collective-permute-done | bytes 557088 | tf_op jit(solution)/shard_map/ppermute | solution.py:636
  35.1 6.5 %collective-permute-done.4 = bf16[144,1024]{1,0:T(8,128)(2,1)S(1)} collective-permute-done((bf16[144,1024]{1,0:T(8,128)(2,1)S(1)}, bf16[144,1024]{1,0:T(8,128)(2,1)S(1)}, u32[]{:S(2)}, u32[]{:S(2)}) %collective-permute-start.4) | collective-permute-done | bytes 294944 | tf_op jit(solution)/shard_map/ppermute | solution.py:636
  46.8 59.3 %all-gather.7.cloned.1.call-done = bf16[1088,1024]{1,0:T(8,128)(2,1)} async-done(((bf16[272,1024]{1,0:T(8,128)(2,1)}), bf16[1088,1024]{1,0:T(8,128)(2,1)}) %all-gather.7.cloned.1.call-update) | async-done | bytes 2228240 | tf_op jit(solution)/shard_map/all_gather | solution.py:690
  110.4 23.4 %collective-permute-start.1 = (bf16[128,1024]{1,0:T(8,128)(2,1)S(1)}, bf16[128,1024]{1,0:T(8,128)(2,1)S(1)}, u32[]{:S(2)}, u32[]{:S(2)}) collective-permute-start(bf16[128,1024]{1,0:T(8,128)(2,1)S(1)} %collective-permute-done.x0.residual), channel_id=1, source_target_pairs={{0,4},{1,5},{2,6},{3,7},{4,0},{5,1},{6,2},{7,3},{8,12},{9,13},{10,... | collective-permute-start | bytes 786440 | tf_op jit(solution)/shard_map/ppermute | solution.py:636
  144.9 7.2 %attention.2 = (f32[128,1024]{1,0:T(8,128)S(1)}, bf16[128,1024]{1,0:T(8,128)(2,1)}, bf16[128,1024]{1,0:T(8,128)(2,1)}, bf16[128,1024]{1,0:T(8,128)(2,1)S(1)}, bf...) custom-call(bf16[128,1024]{1,0:T(8,128)(2,1)S(1)} %collective-permute-done.x0.residual, ...), custom_call_target="tpu_custom_call" | custom-call | flops 2147483648 | bytes 8388608 | tf_op jit(solution)/shard_map/attention/pallas_call | solution.py:771
  170.0 20.2 %all-gather.9.cloned.1.call-done = bf16[576,1024]{1,0:T(8,128)(2,1)} async-done(((bf16[144,1024]{1,0:T(8,128)(2,1)}), bf16[576,1024]{1,0:T(8,128)(2,1)}) %all-gather.9.cloned.1.call-update) | async-done | bytes 1179664 | tf_op jit(solution)/shard_map/all_gather | solution.py:690
  193.1 6.2 collective-permute-done.14.x2
  199.3 6.1 collective-permute-done.15.x3
  244.0 5.7 attention.3
  253.3 5.7 collective-permute-done.25.r1
  287.0 7.0 %collective-permute-done.34.r3 = bf16[128,1024]{1,0:T(8,128)(2,1)S(1)} collective-permute-done((bf16[128,1024]{1,0:T(8,128)(2,1)S(1)}, bf16[128,1024]{1,0:T(8,128)(2,1)S(1)}, u32[]{:S(2)}, u32[]{:S(2)}) %collective-permute-start.34) | collective-permute-done | bytes 262176 | tf_op jit(solution)/shard_map/ppermute | solution.py:636
  324.0 6.3 collective-permute-done.43.r3
  342.4 6.0 attention_back.2
  374.9 5.7 collective-permute-done.49.r3
  445.8 6.0 attention_back.3
  460.2 43.0 %collective-permute-done.36 = bf16[128,1024]{1,0:T(8,128)(2,1)S(1)} collective-permute-done((bf16[128,1024]{1,0:T(8,128)(2,1)}, bf16[128,1024]{1,0:T(8,128)(2,1)S(1)}, u32[]{:S(2)}, u32[]{:S(2)}) %collective-permute-start.36) | collective-permute-done | bytes 262176 | tf_op jit(solution)/shard_map/ppermute | solution.py:636
  503.3 13.2 %collective-permute-start.60 = (bf16[128,1024]{1,0:T(8,128)(2,1)S(1)}, bf16[128,1024]{1,0:T(8,128)(2,1)S(1)}, u32[]{:S(2)}, u32[]{:S(2)}) collective-permute-start(bf16[128,1024]{1,0:T(8,128)(2,1)S(1)} %get-tuple-element.172), channel_id=1, source_target_pairs={{0,16},{1,17},{2,18},{3,19},{4,20},{5,21},{6,22},{7,23},{8,24},{9,... | collective-permute-start | bytes 786440 | tf_op jit(solution)/shard_map/ppermute | solution.py:636
  532.3 12.1 %collective-permute-done.66 = bf16[144,1024]{1,0:T(8,128)(2,1)S(1)} collective-permute-done((bf16[144,1024]{1,0:T(8,128)(2,1)S(1)}, bf16[144,1024]{1,0:T(8,128)(2,1)S(1)}, u32[]{:S(2)}, u32[]{:S(2)}) %collective-permute-start.66) | collective-permute-done | bytes 294944 | tf_op jit(solution)/shard_map/ppermute | solution.py:636
  561.5 7.1 %collective-permute-done.63 = bf16[128,1024]{1,0:T(8,128)(2,1)S(1)} collective-permute-done((bf16[128,1024]{1,0:T(8,128)(2,1)}, bf16[128,1024]{1,0:T(8,128)(2,1)S(1)}, u32[]{:S(2)}, u32[]{:S(2)}) %collective-permute-start.63) | collective-permute-done | bytes 262176 | tf_op jit(solution)/shard_map/ppermute | solution.py:636
  568.6 13.1 %collective-permute-start.77 = (bf16[272,1024]{1,0:T(8,128)(2,1)S(1)}, bf16[272,1024]{1,0:T(8,128)(2,1)S(1)}, u32[]{:S(2)}, u32[]{:S(2)}) collective-permute-start(bf16[272,1024]{1,0:T(8,128)(2,1)S(1)} %get-tuple-element.214), channel_id=1, source_target_pairs={{0,20},{1,21},{2,22},{3,23},{4,16},{5,17},{6,18},{7,19},{8,28},{9,... | collective-permute-start | bytes 1671176 | tf_op jit(solution)/shard_map/ppermute | solution.py:636
  589.2 7.1 %collective-permute-done.75 = bf16[272,1024]{1,0:T(8,128)(2,1)S(1)} collective-permute-done((bf16[272,1024]{1,0:T(8,128)(2,1)S(1)}, bf16[272,1024]{1,0:T(8,128)(2,1)S(1)}, u32[]{:S(2)}, u32[]{:S(2)}) %collective-permute-start.75) | collective-permute-done | bytes 557088 | tf_op jit(solution)/shard_map/ppermute | solution.py:636
  596.3 13.6 %collective-permute-done.76 = bf16[272,1024]{1,0:T(8,128)(2,1)S(1)} collective-permute-done((bf16[272,1024]{1,0:T(8,128)(2,1)S(1)}, bf16[272,1024]{1,0:T(8,128)(2,1)S(1)}, u32[]{:S(2)}, u32[]{:S(2)}) %collective-permute-start.76) | collective-permute-done | bytes 557088 | tf_op jit(solution)/shard_map/ppermute | solution.py:636
  613.5 6.3 finish_attention.1
  631.3 6.0 finish_feed.1
  (372 shorter events, 324.1 us)
Async XLA Ops:
  7.2 98.9 %all-gather.7.cloned.1.call-start = ((), (), s32[]{:S(2)}) async-start(), calls=%async_computation.6 | async-start | bytes 2785280 | tf_op jit(solution)/shard_map/all_gather | solution.py:690
  31.3 128.0 %all-gather.11.cloned.1.call-start = ((), (), s32[]{:S(2)}) async-start(), calls=%async_computation.8 | async-start | bytes 2785280 | tf_op jit(solution)/shard_map/all_gather | solution.py:690
  32.1 158.1 %all-gather.9.cloned.1.call-start = ((), (), s32[]{:S(2)}) async-start(), calls=%async_computation.7 | async-start | bytes 1474560 | tf_op jit(solution)/shard_map/all_gather | solution.py:690
  42.4 63.8 %collective-permute-start.5 = (bf16[144,1024]{1,0:T(8,128)(2,1)S(1)}, bf16[144,1024]{1,0:T(8,128)(2,1)S(1)}, u32[]{:S(2)}, u32[]{:S(2)}) collective-permute-start(bf16[144,1024]{1,0:T(8,128)(2,1)S(1)} %get-tuple-element.218), channel_id=1, source_target_pairs={{0,1},{1,0},{2,3},{3,2},{4,5},{5,4},{6,7},{7,6},{8,9},{9,8},{10,11... | collective-permute-start | bytes 884744 | tf_op jit(solution)/shard_map/ppermute | solution.py:636
  43.8 62.3 %collective-permute-start.6 = (bf16[144,1024]{1,0:T(8,128)(2,1)S(1)}, bf16[144,1024]{1,0:T(8,128)(2,1)S(1)}, u32[]{:S(2)}, u32[]{:S(2)}) collective-permute-start(bf16[144,1024]{1,0:T(8,128)(2,1)S(1)} %get-tuple-element.218), channel_id=1, source_target_pairs={{0,2},{1,3},{2,0},{3,1},{4,6},{5,7},{6,4},{7,5},{8,10},{9,11},{10,... | collective-permute-start | bytes 884744 | tf_op jit(solution)/shard_map/ppermute | solution.py:636
  46.4 59.7 %collective-permute-start.7 = (bf16[144,1024]{1,0:T(8,128)(2,1)S(1)}, bf16[144,1024]{1,0:T(8,128)(2,1)S(1)}, u32[]{:S(2)}, u32[]{:S(2)}) collective-permute-start(bf16[144,1024]{1,0:T(8,128)(2,1)S(1)} %get-tuple-element.218), channel_id=1, source_target_pairs={{0,3},{1,2},{2,1},{3,0},{4,7},{5,6},{6,5},{7,4},{8,11},{9,10},{10,... | collective-permute-start | bytes 884744 | tf_op jit(solution)/shard_map/ppermute | solution.py:636
  46.8 497.6 %reduce-scatter.4.cloned.1.call-start = ((), (), s32[]{:S(2)}) async-start(), calls=%async_computation.3 | async-start | bytes 1474560 | tf_op jit(solution)/shard_map/reduce_scatter | solution.py:693
  106.1 99.3 %collective-permute-start.17 = (bf16[4,272,1024]{2,1,0:T(8,128)(2,1)}, bf16[4,272,1024]{2,1,0:T(8,128)(2,1)}, u32[]{:S(2)}, u32[]{:S(2)}) collective-permute-start(bf16[4,272,1024]{2,1,0:T(8,128)(2,1)} %bitcast.92), channel_id=1, source_target_pairs={{0,8},{1,9},{2,10},{3,11},{4,12},{5,13},{6,14},{7,15},{8,0},{9,1},... | collective-permute-start | bytes 6684680 | tf_op jit(solution)/shard_map/ppermute | solution.py:636
  106.3 36.2 %collective-permute-start.8 = (bf16[4,144,1024]{2,1,0:T(8,128)(2,1)S(1)}, bf16[4,144,1024]{2,1,0:T(8,128)(2,1)S(1)}, u32[]{:S(2)}, u32[]{:S(2)}) collective-permute-start(bf16[4,144,1024]{2,1,0:T(8,128)(2,1)S(1)} %pad_maximum_fusion.1.a_own), channel_id=1, source_target_pairs={{0,8},{1,9},{2,10},{3,11},{4,12},{5,13},{6,14},{7,15},{8,0},{9,1},... | collective-permute-start | bytes 3538952 | tf_op jit(solution)/shard_map/ppermute | solution.py:636
  107.6 26.2 %collective-permute-start.9 = (s32[2,1,512]{2,1,0:T(1,128)S(1)}, s32[2,1,512]{2,1,0:T(1,128)S(1)}, u32[]{:S(2)}, u32[]{:S(2)}) collective-permute-start(s32[2,1,512]{2,1,0:T(1,128)S(1)} %copy-done.74), channel_id=1, source_target_pairs={{0,16},{1,17},{2,18},{3,19},{4,20},{5,21},{6,22},{7,23},{8,24},{9,... | collective-permute-start | bytes 12296 | tf_op jit(solution)/shard_map/ppermute | solution.py:636
  110.4 28.4 %collective-permute-start.1 = (bf16[128,1024]{1,0:T(8,128)(2,1)S(1)}, bf16[128,1024]{1,0:T(8,128)(2,1)S(1)}, u32[]{:S(2)}, u32[]{:S(2)}) collective-permute-start(bf16[128,1024]{1,0:T(8,128)(2,1)S(1)} %collective-permute-done.x0.residual), channel_id=1, source_target_pairs={{0,4},{1,5},{2,6},{3,7},{4,0},{5,1},{6,2},{7,3},{8,12},{9,13},{10,... | collective-permute-start | bytes 786440 | tf_op jit(solution)/shard_map/ppermute | solution.py:636
  159.3 106.9 %collective-permute-start.31 = (bf16[4,272,1024]{2,1,0:T(8,128)(2,1)}, bf16[4,272,1024]{2,1,0:T(8,128)(2,1)}, u32[]{:S(2)}, u32[]{:S(2)}) collective-permute-start(bf16[4,272,1024]{2,1,0:T(8,128)(2,1)} %bitcast.95), channel_id=1, source_target_pairs={{0,8},{1,9},{2,10},{3,11},{4,12},{5,13},{6,14},{7,15},{8,0},{9,1},... | collective-permute-start | bytes 6684680 | tf_op jit(solution)/shard_map/ppermute | solution.py:636
  190.2 43.7 %collective-permute-start.24 = (bf16[4,144,1024]{2,1,0:T(8,128)(2,1)}, bf16[4,144,1024]{2,1,0:T(8,128)(2,1)S(1)}, u32[]{:S(2)}, u32[]{:S(2)}) collective-permute-start(bf16[4,144,1024]{2,1,0:T(8,128)(2,1)} %bitcast.88), channel_id=1, source_target_pairs={{0,8},{1,9},{2,10},{3,11},{4,12},{5,13},{6,14},{7,15},{8,0},{9,1},... | collective-permute-start | bytes 3538952 | tf_op jit(solution)/shard_map/ppermute | solution.py:636
  358.0 201.3 %reduce-scatter.8.cloned.1.call-start = ((), (), s32[]{:S(2)}) async-start(), calls=%async_computation.5 | async-start | bytes 2785280 | tf_op jit(solution)/shard_map/reduce_scatter | solution.py:693
  364.9 194.4 %reduce-scatter.6.cloned.1.call-start = ((), (), s32[]{:S(2)}) async-start(), calls=%async_computation.4 | async-start | bytes 2785280 | tf_op jit(solution)/shard_map/reduce_scatter | solution.py:693
  455.3 61.3 %collective-permute-start.64 = (bf16[4,144,1024]{2,1,0:T(8,128)(2,1)}, bf16[4,144,1024]{2,1,0:T(8,128)(2,1)}, u32[]{:S(2)}, u32[]{:S(2)}) collective-permute-start(bf16[4,144,1024]{2,1,0:T(8,128)(2,1)} %get-tuple-element.180), channel_id=1, source_target_pairs={{0,8},{1,9},{2,10},{3,11},{4,12},{5,13},{6,14},{7,15},{8,0},{9,1},... | collective-permute-start | bytes 3538952 | tf_op jit(solution)/shard_map/ppermute | solution.py:636
  457.7 45.5 %collective-permute-start.36 = (bf16[128,1024]{1,0:T(8,128)(2,1)}, bf16[128,1024]{1,0:T(8,128)(2,1)S(1)}, u32[]{:S(2)}, u32[]{:S(2)}) collective-permute-start(bf16[128,1024]{1,0:T(8,128)(2,1)} %get-tuple-element.224), channel_id=1, source_target_pairs={{0,4},{1,20},{2,0},{3,16},{4,5},{5,21},{6,1},{7,17},{8,12},{9,28},... | collective-permute-start | bytes 786440 | tf_op jit(solution)/shard_map/ppermute | solution.py:636
  518.6 25.7 %collective-permute-start.66 = (bf16[144,1024]{1,0:T(8,128)(2,1)S(1)}, bf16[144,1024]{1,0:T(8,128)(2,1)S(1)}, u32[]{:S(2)}, u32[]{:S(2)}) collective-permute-start(bf16[144,1024]{1,0:T(8,128)(2,1)S(1)} %get-tuple-element.213), channel_id=1, source_target_pairs={{0,2},{1,3},{2,0},{3,1},{4,6},{5,7},{6,4},{7,5},{8,10},{9,11},{10,... | collective-permute-start | bytes 884744 | tf_op jit(solution)/shard_map/ppermute | solution.py:636
  547.2 34.5 %collective-permute-start.70 = (bf16[144,1024]{1,0:T(8,128)(2,1)}, bf16[144,1024]{1,0:T(8,128)(2,1)S(1)}, u32[]{:S(2)}, u32[]{:S(2)}) collective-permute-start(bf16[144,1024]{1,0:T(8,128)(2,1)} %get-tuple-element.208), channel_id=1, source_target_pairs={{0,16},{1,17},{2,18},{3,19},{4,20},{5,21},{6,22},{7,23},{8,24},{9,... | collective-permute-start | bytes 884744 | tf_op jit(solution)/shard_map/ppermute | solution.py:636
  552.7 35.2 %collective-permute-start.69 = (bf16[144,1024]{1,0:T(8,128)(2,1)}, bf16[144,1024]{1,0:T(8,128)(2,1)}, u32[]{:S(2)}, u32[]{:S(2)}) collective-permute-start(bf16[144,1024]{1,0:T(8,128)(2,1)} %get-tuple-element.205), channel_id=1, source_target_pairs={{0,4},{1,5},{2,6},{3,7},{4,0},{5,1},{6,2},{7,3},{8,12},{9,13},{10,... | collective-permute-start | bytes 884744 | tf_op jit(solution)/shard_map/ppermute | solution.py:636
  556.8 31.1 %collective-permute-start.71 = (bf16[144,1024]{1,0:T(8,128)(2,1)}, bf16[144,1024]{1,0:T(8,128)(2,1)S(1)}, u32[]{:S(2)}, u32[]{:S(2)}) collective-permute-start(bf16[144,1024]{1,0:T(8,128)(2,1)} %get-tuple-element.205), channel_id=1, source_target_pairs={{0,20},{1,21},{2,22},{3,23},{4,16},{5,17},{6,18},{7,19},{8,28},{9,... | collective-permute-start | bytes 884744 | tf_op jit(solution)/shard_map/ppermute | solution.py:636
  568.6 27.7 %collective-permute-start.75 = (bf16[272,1024]{1,0:T(8,128)(2,1)S(1)}, bf16[272,1024]{1,0:T(8,128)(2,1)S(1)}, u32[]{:S(2)}, u32[]{:S(2)}) collective-permute-start(bf16[272,1024]{1,0:T(8,128)(2,1)S(1)} %get-tuple-element.214), channel_id=1, source_target_pairs={{0,4},{1,5},{2,6},{3,7},{4,0},{5,1},{6,2},{7,3},{8,12},{9,13},{10,... | collective-permute-start | bytes 1671176 | tf_op jit(solution)/shard_map/ppermute | solution.py:636
  568.6 41.3 %collective-permute-start.77 = (bf16[272,1024]{1,0:T(8,128)(2,1)S(1)}, bf16[272,1024]{1,0:T(8,128)(2,1)S(1)}, u32[]{:S(2)}, u32[]{:S(2)}) collective-permute-start(bf16[272,1024]{1,0:T(8,128)(2,1)S(1)} %get-tuple-element.214), channel_id=1, source_target_pairs={{0,20},{1,21},{2,22},{3,23},{4,16},{5,17},{6,18},{7,19},{8,28},{9,... | collective-permute-start | bytes 1671176 | tf_op jit(solution)/shard_map/ppermute | solution.py:636
  581.7 28.2 %collective-permute-start.76 = (bf16[272,1024]{1,0:T(8,128)(2,1)S(1)}, bf16[272,1024]{1,0:T(8,128)(2,1)S(1)}, u32[]{:S(2)}, u32[]{:S(2)}) collective-permute-start(bf16[272,1024]{1,0:T(8,128)(2,1)S(1)} %bitcast.101), channel_id=1, source_target_pairs={{0,16},{1,17},{2,18},{3,19},{4,20},{5,21},{6,22},{7,23},{8,24},{9,... | collective-permute-start | bytes 1671176 | tf_op jit(solution)/shard_map/ppermute | solution.py:636
  (136 other events, 1718.3 us)
Sparse Core Ops, SparseCore 0:
  31.5 74.6 all-gather.6
  108.3 47.2 all-gather.10
  157.7 32.4 all-gather.8
  358.1 28.1 reduce-scatter.3
  389.1 44.6 reduce-scatter.7
  436.5 75.0 reduce-scatter.5

commit v3 on v2

v3 whole, which is shorter than its diff:
```python
from functools import partial

import jax
import jax.numpy as jnp
from jax import lax
from jax.experimental import pallas as pl
from jax.experimental.pallas import tpu as pltpu
from jax.sharding import PartitionSpec as P

HD = 64
SEQ = 512
SHARE = 128
WIDE = 1024
HEADS = 4
HALF = 32
ATTN = 144
UP = 144
DOWN = 128
FEED = UP + DOWN
AXES = ("dp", "section", "mp")
EPSILON = 1e-05
NEGATIVE = -1e30
F32 = jnp.float32
BF16 = jnp.bfloat16
VMEM = pl.BlockSpec(memory_space=pltpu.VMEM)
ANY = pl.BlockSpec(memory_space=pl.ANY)
HBM = pl.BlockSpec(memory_space=pltpu.HBM)
SMEM = pl.BlockSpec(memory_space=pltpu.SMEM)


def dot_nt(left, right):
    return lax.dot_general(left, right, (((1,), (1,)), ((), ())), preferred_element_type=F32)


def dot_nn(left, right):
    return lax.dot_general(left, right, (((1,), (0,)), ((), ())), preferred_element_type=F32)


def dot_tn(left, right):
    return lax.dot_general(left, right, (((0,), (0,)), ((), ())), preferred_element_type=F32)


def shape(dims, dtype=BF16):
    return jax.ShapeDtypeStruct(dims, dtype)


DMA = pltpu.SemaphoreType.DMA


def scratch(dims, dtype=BF16):
    return pltpu.VMEM(dims, dtype)


def in_hbm(value):
    return pltpu.with_memory_space_constraint(value, pltpu.HBM)


class Arriving:
    def __init__(self, copies, target):
        self.copies, self.target = copies, target
        for copy in copies:
            copy.start()

    def get(self):
        for copy in self.copies:
            copy.wait()
        self.copies = []
        return self.target


class Leaving:
    def __init__(self, copies, buffer):
        self.copies, self.buffer, self.sent = copies, buffer, False

    def __setitem__(self, where, value):
        self.buffer[where] = value

    def __getitem__(self, where):
        return self.buffer[where]

    def send(self):
        for copy in self.copies:
            copy.start()
        self.sent = True


class Chunks:
    def __init__(self, rows):
        self.buffer = shape((4, rows, WIDE))
        cut = 80 if rows == ATTN else 64
        self.parts = [(z, start, end) for z in range(4) for start, end in ((0, cut), (cut, rows))]
        self.shapes = [shape((end - start, WIDE)) for _, start, end in self.parts]

    def views(self, buffer):
        return [buffer.at[z, start:end] for z, start, end in self.parts]


def call(kernel, name, ins, outs, scratches=(), limit=32):
    def arrays(item):
        return item.shapes if isinstance(item, Chunks) else [item]

    def buffer_of(item):
        held = item.buffer if isinstance(item, Chunks) else item
        return scratch(held.shape, held.dtype)

    loads = [i for i in ins if not isinstance(i, str)]
    stores = [o for where, o in outs if where == "h"]
    specs = {"v": VMEM, "s": SMEM, "r": HBM, "h": HBM, "a": ANY}
    in_specs, pinned = [], []
    for i in ins:
        count = 1 if isinstance(i, str) else len(arrays(i))
        in_specs += [specs[i] if isinstance(i, str) else HBM] * count
        pinned += [i == "r" or not isinstance(i, str)] * count
    out_specs, out_shapes = [], []
    for where, o in outs:
        for one in arrays(o):
            out_specs.append(specs[where])
            out_shapes.append(pltpu.HBM(one.shape, one.dtype) if where == "h" else one)
    n_loads = sum(len(arrays(i)) for i in loads)
    n_stores = sum(len(arrays(o)) for o in stores)

    def views(item, buffer):
        return item.views(buffer) if isinstance(item, Chunks) else [buffer]

    def body(after, *refs):
        refs = list(refs)
        in_refs = [refs.pop(0) for _ in in_specs]
        del refs[:after]
        out_refs = [refs.pop(0) for _ in out_specs]
        load_bufs = [refs.pop(0) for _ in loads]
        store_bufs = [refs.pop(0) for _ in stores]
        load_sems = refs.pop(0) if loads else None
        store_sems = refs.pop(0) if stores else None
        operands, results, n = [], [], 0
        for kind in ins:
            if isinstance(kind, str):
                operands.append(in_refs.pop(0))
                continue
            target, copies = load_bufs.pop(0), []
            for view in views(kind, target):
                copies.append(pltpu.make_async_copy(in_refs.pop(0), view, load_sems.at[n]))
                n += 1
            operands.append(Arriving(copies, target))
        n = 0
        for where, o in outs:
            if where == "v":
                results.append(out_refs.pop(0))
                continue
            buffer, copies = store_bufs.pop(0), []
            for view in views(o, buffer):
                copies.append(pltpu.make_async_copy(view, out_refs.pop(0), store_sems.at[n]))
                n += 1
            results.append(Leaving(copies, buffer))
        kernel(*operands, *results, *refs)
        for operand in operands:
            if isinstance(operand, Arriving):
                operand.get()
        leaving = [result for result in results if isinstance(result, Leaving)]
        for result in leaving:
            if not result.sent:
                result.send()
        for result in leaving:
            for copy in result.copies:
                copy.wait()

    def run(*operands):
        after = len(operands) - len(in_specs)
        operands = [
            in_hbm(operand) if pin else operand
            for pin, operand in zip(pinned + [True] * after, operands)
        ]
        return pl.pallas_call(
            partial(body, after),
            name=name,
            in_specs=in_specs + [ANY] * after,
            out_specs=tuple(out_specs),
            out_shape=tuple(out_shapes),
            scratch_shapes=[buffer_of(item) for item in loads + stores]
            + ([DMA((n_loads,))] if loads else [])
            + ([DMA((n_stores,))] if stores else [])
            + list(scratches),
            compiler_params=pltpu.CompilerParams(vmem_limit_bytes=limit << 20),
            cost_estimate=pl.CostEstimate(flops=0, bytes_accessed=0, transcendentals=0),
        )(*operands)

    return run


def hold(value, *after):
    return pl.pallas_call(
        lambda *refs: None,
        name="hold",
        in_specs=[HBM] + [ANY] * len(after),
        out_specs=HBM,
        out_shape=pltpu.HBM(value.shape, value.dtype),
        input_output_aliases={0: 0},
    )(in_hbm(value), *after)


def stamp(*values):
    def kernel(*refs):
        refs[-1][...] = jnp.zeros((8, 128), F32)

    return pl.pallas_call(
        kernel,
        name="stamp",
        in_specs=[ANY] * len(values),
        out_specs=VMEM,
        out_shape=shape((8, 128), F32),
        compiler_params=pltpu.CompilerParams(vmem_limit_bytes=16 << 20),
        cost_estimate=pl.CostEstimate(flops=0, bytes_accessed=0, transcendentals=0),
    )(*values)


def zero_after(after):
    def kernel(after, out):
        out[0] = 0

    return pl.pallas_call(
        kernel,
        name="zero",
        in_specs=[ANY],
        out_specs=SMEM,
        out_shape=shape((1,), jnp.int32),
    )(after)[0]


def at_rows(rows, values):
    place = lax.broadcasted_iota(jnp.int32, (rows, values[0].shape[1]), 0)
    block = jnp.zeros((rows, values[0].shape[1]), F32)
    for i, value in enumerate(values):
        block = jnp.where(place == i, value, block)
    return block


def columns(i, width=256):
    return pl.ds(pl.multiple_of(i * width, width), width)


def prep_attn_kernel(place, wq, wk, wv, wo, bq, bv, v0, v1, v2, v3, v4, v5, own, peer, turned):
    core, quarter = place[0], place[1]
    for a, w in enumerate((wq, wk, wv)):
        turned[a] = w.get()[0].T
    layer_rows = [v.get()[...].astype(F32) for v in (v0, v1, v2, v3, v4, v5)]
    wo, bq, bv = wo.get(), bq.get(), bv.get()
    source = lax.broadcasted_iota(jnp.int32, (256, 128), 0)
    lane = lax.broadcasted_iota(jnp.int32, (256, 128), 1)
    for out, block in ((own, quarter), (peer, quarter ^ 1)):
        head = pl.multiple_of(block * HD + core * HALF, HALF)
        for a in range(3):
            out[HALF * a : HALF * a + HALF] = turned[a, pl.ds(head, HALF)]
        out[3 * HALF : 4 * HALF] = wo[0, pl.ds(head, HALF)]
        inner = lane & 63
        wanted = block * HD + (inner ^ (core * HALF))
        hit = source == wanted
        zero = jnp.zeros((256, 128), F32)
        one = jnp.ones((256, 128), F32)
        first = jnp.where(hit & (lane < 64), one, zero).astype(BF16)
        second = jnp.where(hit & (lane >= 64), one, zero).astype(BF16)
        bias = dot_nn(jnp.broadcast_to(bq[...], (16, 256)), first) + dot_nn(
            jnp.broadcast_to(bv[...], (16, 256)), second
        )
        rows = lax.broadcasted_iota(jnp.int32, (16, WIDE), 0)
        block_rows = jnp.zeros((16, WIDE), F32)
        for i, row in enumerate(layer_rows):
            block_rows = jnp.where(rows == i + 1, row, block_rows)
        out[128:144] = block_rows.astype(BF16)
        first_row = lax.broadcasted_iota(jnp.int32, (16, 128), 0) == 0
        out[128:144, 0:128] = jnp.where(first_row, bias, block_rows[:, 0:128]).astype(BF16)


def pick_kernel(place, own, got, out):
    own, got = own.get(), got.get()
    out[...] = jnp.where(jnp.full(own.shape, place[2]) == 0, own[...], got[...])


def prep_feed_kernel(place, up, down, bu, own, peer, column, sems):
    core, quarter = place[0], place[1]
    copies = []
    outs = ((own, quarter), (peer, quarter ^ 1))
    for i, (out, block) in enumerate(outs):
        unit = pl.multiple_of(block * 256 + core * 128, 128)
        copies.append(
            pltpu.make_async_copy(up.at[0, :, pl.ds(unit, 128)], column.at[i], sems.at[2 * i])
        )
        copies.append(
            pltpu.make_async_copy(
                down.at[0, pl.ds(unit, 128)], out.buffer.at[UP:FEED], sems.at[2 * i + 1]
            )
        )
    for copy in copies:
        copy.start()
    row = lax.broadcasted_iota(jnp.int32, (16, 128), 0) == 0
    for i, (out, block) in enumerate(outs):
        out[128:144] = jnp.zeros((16, WIDE), BF16)
        for h in range(2):
            unit = pl.multiple_of(block * 256 + (core ^ h) * 128, 128)
            piece = bu[:, pl.ds(unit, 128)].astype(F32)
            out[128:144, 128 * h : 128 * h + 128] = jnp.where(row, piece, 0.0).astype(BF16)
        copies[2 * i].wait()
        out[0:128] = column[i].T
        copies[2 * i + 1].wait()
        out.send()


def rows_of(ref, *which):
    block = ref[...].astype(F32)
    return [block[i : i + 1] for i in which]


def norm_forward(hidden, gain, offset):
    centre = jnp.mean(hidden, -1, keepdims=True)
    centred = hidden - centre
    variance = jnp.mean(centred * centred, -1, keepdims=True)
    inverse = lax.rsqrt(variance + EPSILON)
    normed = centred * inverse
    return (normed * gain + offset, normed, inverse)


def norm_backward(upstream, normed, inverse, gain):
    scaled = upstream * gain
    return inverse * (
        scaled
        - jnp.mean(scaled, -1, keepdims=True)
        - normed * jnp.mean(scaled * normed, -1, keepdims=True)
    )


def received(own, r1, r2, r3):
    return own[...] + r1[...].astype(F32) + r2[...].astype(F32) + r3[...].astype(F32)


def norm_kernel(first, own, r1, r2, r3, residual, vec, value, low, normed, inverse):
    bias, gain, offset = rows_of(vec, *((1, 2, 3) if first else (4, 5, 6)))
    hidden = residual[...].astype(F32) + received(own, r1, r2, r3) + bias
    result, flat, scale = norm_forward(hidden, gain, offset)
    low[...] = result.astype(BF16)
    value[...] = result
    normed[...] = flat.astype(BF16)
    inverse[...] = scale


def sums(*values):
    return at_rows(8, [jnp.sum(v, 0, keepdims=True) for v in values])


def norm_back(grad, gain, normed, inverse, total, low, vectors):
    flat = normed.get()[...].astype(F32)
    value = norm_backward(grad, flat, inverse.get()[...], gain)
    rounded = value.astype(BF16)
    low[...] = rounded
    total[...] = value
    total.send()
    vectors[...] = sums(rounded.astype(F32), grad * flat, grad)


def norm_two_back_kernel(upstream, vec, normed, inverse, total, low, vectors):
    (gain,) = rows_of(vec, 5)
    norm_back(upstream[...].astype(F32), gain, normed, inverse, total, low, vectors)


def norm_two_back_sum_kernel(
    own, r1, r2, r3, vec, before, normed, inverse, total, low, vectors, given
):
    (gain,) = rows_of(vec, 5)
    rounded = (before.get()[...] + received(own, r1, r2, r3)).astype(BF16)
    norm_back(rounded.astype(F32), gain, normed, inverse, total, low, vectors)
    given[...] = rounded


def norm_one_back_kernel(own, r1, r2, r3, vec, before, normed, inverse, total, low, vectors):
    (gain,) = rows_of(vec, 2)
    grad = before.get()[...] + received(own, r1, r2, r3)
    norm_back(grad, gain, normed, inverse, total, low, vectors)


def last_sum_kernel(own, r1, r2, r3, before, given):
    given[...] = (before.get()[...] + received(own, r1, r2, r3)).astype(BF16)


def load_attn(own, other, weight, sems):
    return [
        pltpu.make_async_copy(
            ref.at[:, HALF * a : HALF * a + HALF], weight.at[a, :, half], sems.at[4 * half + a]
        )
        for half, ref in enumerate((own, other))
        for a in range(4)
    ]


def join(target, pieces, sems):
    copies = [
        pltpu.make_async_copy(piece, target.at[SHARE * i : SHARE * i + SHARE], sems.at[i])
        for i, piece in enumerate(pieces)
    ]
    for copy in copies:
        copy.start()
    return copies


def arrive(copies):
    for copy in copies:
        copy.wait()


def spread_out(value, where, own, parts):
    own[:, where] = value[0:SHARE]
    for i, part in enumerate(parts):
        part[:, where] = value[SHARE * (i + 1) : SHARE * (i + 2)].astype(BF16)


def by_share(left, right, own, parts):
    for i in (3, 2, 1, 0):
        value = dot_nn(left[SHARE * i : SHARE * i + SHARE], right)
        if i:
            parts[i - 1][...] = value.astype(BF16)
        else:
            own[...] = value


def attn_kernel(
    x0, x1, x2, x3, id_row, a_own, a_other,
    own, p1, p2, p3, qkv, probs, mixed, x_out, weight_out,
    small, sems, x_sems,
):
    weight, x_all = weight_out.buffer, x_out.buffer
    copies = load_attn(a_own, a_other, weight, sems)
    copies.append(pltpu.make_async_copy(a_own.at[:, 128:144], small, sems.at[8]))
    for copy in copies:
        copy.start()
    arrive(join(x_all, (x0, x1, x2, x3), x_sems))
    x_out.send()
    arrive(copies)
    weight_out.send()
    ids = id_row[...]
    id_column = jnp.broadcast_to(ids, (128, SEQ)).T[:, 0:1]
    biases = [small[z].astype(F32)[0:1] for z in range(4)]
    bias_of = (
        jnp.concatenate([b[:, 0:64] for b in biases], 1),
        None,
        jnp.concatenate([b[:, 64:128] for b in biases], 1),
    )
    x = x_all[...]
    for a in range(3):
        rows = dot_nt(x, weight[a].reshape(256, WIDE))
        if bias_of[a] is not None:
            rows = rows + bias_of[a]
        qkv[:, 256 * a : 256 * a + 256] = rows.astype(BF16)
    qkv.send()
    for c in range(2):
        q_rows = slice(256 * c, 256 * c + 256)
        allowed = id_column[q_rows] == ids
        for h in range(HEADS):
            query = qkv[q_rows, HD * h : HD * h + HD]
            key = qkv[:, 256 + HD * h : 256 + HD * h + HD]
            value = qkv[:, 512 + HD * h : 512 + HD * h + HD]
            scores = jnp.where(allowed, dot_nt(query, key) * HD ** (-0.5), NEGATIVE)
            exponent = jnp.exp(scores - jnp.max(scores, -1, keepdims=True))
            low = (exponent / jnp.sum(exponent, -1, keepdims=True)).astype(BF16)
            probs[h, q_rows] = low
            mixed[q_rows, HD * h : HD * h + HD] = dot_nn(low, value).astype(BF16)
    probs.send()
    mixed.send()
    by_share(mixed, weight[3].reshape(256, WIDE), own, (p1, p2, p3))


def attn_back_kernel(
    g0, g1, g2, g3, weight, qkv, probs, own, p1, p2, p3, d_rows, g_out, x_sems
):
    g_all = g_out.buffer
    arrive(join(g_all, (g0, g1, g2, g3), x_sems))
    g_out.send()
    weight, qkv, probs = weight.get(), qkv.get(), probs.get()
    d_mixed = dot_nt(g_all[...], weight[3].reshape(256, WIDE)).astype(BF16)
    scale = HD ** (-0.5)
    for h in range(HEADS):
        query = qkv[:, HD * h : HD * h + HD]
        key = qkv[:, 256 + HD * h : 256 + HD * h + HD]
        value = qkv[:, 512 + HD * h : 512 + HD * h + HD]
        grad = d_mixed[:, HD * h : HD * h + HD]
        d_key = jnp.zeros((SEQ, HD), F32)
        d_value = jnp.zeros((SEQ, HD), F32)
        for c in range(2):
            q_rows = slice(256 * c, 256 * c + 256)
            low = probs[h, q_rows]
            p = low.astype(F32)
            d_probs = dot_nt(grad[q_rows], value)
            inner = jnp.sum(p * d_probs, -1, keepdims=True)
            d_scores = (p * (d_probs - inner)).astype(BF16)
            d_rows[q_rows, HD * h : HD * h + HD] = (dot_nn(d_scores, key) * scale).astype(BF16)
            d_key = d_key + dot_tn(d_scores, query[q_rows])
            d_value = d_value + dot_tn(low, grad[q_rows])
        d_rows[:, 256 + HD * h : 256 + HD * h + HD] = (d_key * scale).astype(BF16)
        d_rows[:, 512 + HD * h : 512 + HD * h + HD] = d_value.astype(BF16)
    d_rows.send()
    by_share(d_rows, weight[0:3].reshape(768, WIDE), own, (p1, p2, p3))


def attn_weights_kernel(
    d_rows, mixed, x_all, g_all, vec_one, vec_two, own, other
):
    operands = (d_rows, mixed, x_all, g_all, vec_one, vec_two)
    d_rows, mixed, x_all, g_all, vec_one, vec_two = (operand.get() for operand in operands)
    for a in range(4):
        if a < 3:
            value = dot_tn(d_rows[:, 256 * a : 256 * a + 256], x_all[...])
        else:
            value = dot_tn(mixed[...], g_all[...])
        value = value.astype(BF16).reshape(4, 2, HALF, WIDE)
        own[:, HALF * a : HALF * a + HALF] = value[:, 0]
        other[:, HALF * a : HALF * a + HALF] = value[:, 1]
    total = jnp.sum(d_rows[...].astype(F32), 0, keepdims=True)
    one, two = vec_one[...], vec_two[...]
    vectors = [one[i : i + 1] for i in range(3)] + [two[i : i + 1] for i in range(3)]
    block = at_rows(16, [jnp.zeros((1, WIDE), F32)] + vectors)
    first_row = lax.broadcasted_iota(jnp.int32, (16, 128), 0) == 0
    for half, out in ((1, other), (0, own)):
        for z in range(4):
            start = HD * z + HALF * half
            bias = jnp.concatenate(
                [
                    total[:, start : start + HALF],
                    total[:, 512 + start : 512 + start + HALF],
                    jnp.zeros((1, 64), F32),
                ],
                1,
            )
            out[z, 128:144] = block.astype(BF16)
            out[z, 128:144, 0:128] = jnp.where(first_row, bias, block[:, 0:128]).astype(BF16)
        out.send()


def load_feed(ups, downs, up, down, sems):
    copies = []
    for i, (refs, target) in enumerate(((ups, up), (downs, down))):
        for half in range(2):
            copies.append(
                pltpu.make_async_copy(
                    refs[half].at[:, 0:128],
                    target.at[4 * half : 4 * half + 4],
                    sems.at[2 * i + half],
                )
            )
    return copies[:2], copies[2:]


def feed_kernel(
    x0, x1, x2, x3, up_own, up_other, down_own, down_other,
    own, p1, p2, p3, active, slope, x_out, up_out, down_out,
    small, bias, sems, x_sems,
):
    x_all, up, down = x_out.buffer, up_out.buffer, down_out.buffer
    ups, downs = load_feed((up_own, up_other), (down_own, down_other), up, down, sems)
    copies = [pltpu.make_async_copy(up_own.at[:, 128:144], small, sems.at[4])] + ups
    for copy in copies + downs:
        copy.start()
    arrive(join(x_all, (x0, x1, x2, x3), x_sems))
    x_out.send()
    arrive(copies)
    up_out.send()
    for half in range(2):
        for z in range(4):
            unit = 512 * half + 128 * z
            bias[0:8, unit : unit + 128] = jnp.broadcast_to(
                small[z, :, 128 * half : 128 * half + 128].astype(F32)[0:1], (8, 128)
            )

    def units(i, carry):
        block = up[pl.ds(2 * i, 2)].reshape(256, WIDE)
        hidden = dot_nt(x_all[...], block) + bias[0:1, columns(i)]
        share = 0.5 * (1.0 + lax.erf(hidden * (0.5 ** 0.5)))
        density = jnp.exp(-0.5 * hidden * hidden) * 0.3989422804014327
        active[:, columns(i)] = (hidden * share).astype(BF16)
        slope[:, columns(i)] = (share + hidden * density).astype(BF16)
        return carry

    lax.fori_loop(0, 4, units, 0)
    active.send()
    slope.send()
    arrive(downs)
    down_out.send()

    def features(n, carry):
        block = down[:, :, columns(n)].reshape(WIDE, 256)
        spread_out(dot_nn(active[...], block), columns(n), own, (p1, p2, p3))
        return carry

    lax.fori_loop(0, 4, features, 0)


def feed_back_kernel(
    g0, g1, g2, g3, down, slope, up, own, p1, p2, p3, d_hidden, g_out, x_sems
):
    g_all = g_out.buffer
    arrive(join(g_all, (g0, g1, g2, g3), x_sems))
    g_out.send()
    down, slope = down.get(), slope.get()

    def units(i, carry):
        block = down[pl.ds(2 * i, 2)].reshape(256, WIDE)
        value = dot_nt(g_all[...], block) * slope[:, columns(i)].astype(F32)
        d_hidden[:, columns(i)] = value.astype(BF16)
        return carry

    lax.fori_loop(0, 4, units, 0)
    d_hidden.send()
    up = up.get()

    def features(n, carry):
        block = up[:, :, columns(n)].reshape(WIDE, 256)
        spread_out(dot_nn(d_hidden[...], block), columns(n), own, (p1, p2, p3))
        return carry

    lax.fori_loop(0, 4, features, 0)


def feed_weights_kernel(
    d_hidden, active, x_all, g_all, up_own, up_other, down_own, down_other
):
    d_hidden, active, x_all, g_all = (v.get() for v in (d_hidden, active, x_all, g_all))
    row = lax.broadcasted_iota(jnp.int32, (16, 128), 0) == 0
    for half, up, down in ((1, up_other, down_other), (0, up_own, down_own)):

        def pair(i, carry, half=half, up=up, down=down):
            where = columns(2 * half + i)
            value = dot_tn(d_hidden[:, where], x_all[...]).astype(BF16)
            up[pl.ds(2 * i, 2), 0:128] = value.reshape(2, 128, WIDE)
            value = dot_tn(active[:, where], g_all[...]).astype(BF16)
            down[pl.ds(2 * i, 2)] = value.reshape(2, 128, WIDE)
            return carry

        lax.fori_loop(0, 2, pair, 0)
        total = jnp.sum(d_hidden[:, 512 * half : 512 * half + 512].astype(F32), 0, keepdims=True)
        for z in range(4):
            up[z, 128:144] = jnp.zeros((16, WIDE), BF16)
            up[z, 128:144, 0:128] = jnp.where(row, total[:, 128 * z : 128 * z + 128], 0.0).astype(
                BF16
            )
        up.send()
        down.send()


def core_sum_kernel(*refs):
    count = len(refs) // 3
    for own, received, out in zip(refs[:count], refs[count : 2 * count], refs[2 * count :]):
        out[...] = (own.get()[...].astype(F32) + received[...].astype(F32)).astype(BF16)
        out.send()


def ordered(place):
    return [
        (4 * c + r, ((r ^ place[1]) * 2 + (c ^ place[0])).astype(jnp.int32))
        for c in range(2)
        for r in range(4)
    ]


def finish_attn_kernel(place, *refs):
    pieces, refs = refs[:8], refs[8:]
    gq, gk, gv, go, small, turned, sems = refs
    copies = []
    for i, to in ordered(place):
        copies.append(
            pltpu.make_async_copy(pieces[i].at[128:144], small.buffer.at[to], sems.at[4, i])
        )
        for a in range(4):
            copies.append(
                pltpu.make_async_copy(
                    pieces[i].at[HALF * a : HALF * a + HALF], turned.at[a, to], sems.at[a, i]
                )
            )
    for copy in copies:
        copy.start()
    for copy in copies:
        copy.wait()
    for a, out in enumerate((gq, gk, gv)):
        out[0] = turned[a].reshape(256, WIDE).astype(F32).T
        out.send()
    go[0] = turned[3].reshape(256, WIDE).astype(F32)


def finish_feed_kernel(place, *refs):
    pieces, refs = refs[:8], refs[8:]
    up, down, small, block, sems = refs
    copies = []
    for i, to in ordered(place):
        copies.append(pltpu.make_async_copy(pieces[i], block.at[to], sems.at[i]))
    for copy in copies:
        copy.start()
    for copy in copies:
        copy.wait()
    for i in range(8):
        down[0, 128 * i : 128 * i + 128] = block[i, UP:FEED].astype(F32)
    down.send()
    for i in range(8):
        up[0, :, 128 * i : 128 * i + 128] = block[i, 0:128].astype(F32).T
        small[i] = block[i, 128:144]


def finish_tokens_kernel(place, a, b, out):
    is_first = place[2] == 0

    @pl.when(is_first)
    def _():
        out[0, 0] = a[...].astype(out.buffer.dtype)
        out[0, 1] = b[...].astype(out.buffer.dtype)

    @pl.when(jnp.logical_not(is_first))
    def _():
        out[0, 0] = b[...].astype(out.buffer.dtype)
        out[0, 1] = a[...].astype(out.buffer.dtype)


RAW = ["a"] * 4
WHOLE = shape((SEQ, WIDE))
BLOCKS = shape((8, 128, WIDE))
HEAD_ROWS = shape((4, 4, 2, HALF, WIDE))
TOKEN = shape((SHARE, WIDE))
WIDE_TOKEN = shape((SHARE, WIDE), F32)
ONE = shape((SHARE, 1), F32)
PARTS = [("v", WIDE_TOKEN)] + [("v", TOKEN)] * 3
ROW = shape((1, WIDE))
FOUR = DMA((4,))
MASK = shape((1, SEQ), F32)
VECTORS = shape((8, WIDE), F32)

prep_attn = call(
    prep_attn_kernel,
    "pack_attention",
    ["s"]
    + [shape((1, WIDE, 256))] * 3
    + [shape((1, 256, WIDE))]
    + [shape((1, 256))] * 2
    + [ROW] * 6,
    [("h", shape((ATTN, WIDE)))] * 2,
    [scratch((3, 256, WIDE))],
)
pick = call(
    pick_kernel,
    "pick",
    ["s"] + [shape((ATTN, WIDE))] * 2,
    [("h", shape((ATTN, WIDE)))],
)
prep_feed = call(
    prep_feed_kernel,
    "pack_feed",
    ["s", "r", "r", "v"],
    [("h", shape((FEED, WIDE)))] * 2,
    [scratch((2, WIDE, 128)), DMA((4,))],
)
norm_one, norm_two = (
    call(
        partial(norm_kernel, first),
        name,
        ["v"] * 6,
        [("v", WIDE_TOKEN), ("v", TOKEN), ("h", TOKEN), ("h", ONE)],
        )
    for first, name in ((True, "norm_one"), (False, "norm_two"))
)
BACKS = [("h", WIDE_TOKEN), ("v", TOKEN), ("h", VECTORS)]
norm_two_back = call(
    norm_two_back_kernel, "norm_two_back", ["v", "v", TOKEN, ONE], BACKS
)
norm_two_back_sum = call(
    norm_two_back_sum_kernel,
    "norm_two_back_sum",
    ["v"] * 5 + [WIDE_TOKEN, TOKEN, ONE],
    BACKS + [("h", TOKEN)],
)
norm_one_back = call(
    norm_one_back_kernel,
    "norm_one_back",
    ["v"] * 5 + [WIDE_TOKEN, TOKEN, ONE],
    BACKS,
)
last_sum = call(
    last_sum_kernel, "last_sum", ["v"] * 4 + [WIDE_TOKEN], [("h", TOKEN)]
)
attn_forward = call(
    attn_kernel,
    "attention",
    RAW + ["v", "a", "a"],
    PARTS
    + [
        ("h", shape((SEQ, 768))),
        ("h", shape((HEADS, SEQ, SEQ))),
        ("h", shape((SEQ, 256))),
        ("h", WHOLE),
        ("h", HEAD_ROWS),
    ],
    [scratch((4, 16, WIDE)), DMA((9,)), FOUR],
)
attn_backward = call(
    attn_back_kernel,
    "attention_back",
    RAW + [HEAD_ROWS, shape((SEQ, 768)), shape((HEADS, SEQ, SEQ))],
    PARTS + [("h", shape((SEQ, 768))), ("h", WHOLE)],
    [FOUR],
)
attn_weights = call(
    attn_weights_kernel,
    "attention_weights",
    [shape((SEQ, 768)), shape((SEQ, 256)), WHOLE, WHOLE] + [VECTORS] * 2,
    [("h", shape((4, ATTN, WIDE)))] * 2,
)
feed_forward = call(
    feed_kernel,
    "feed",
    RAW + ["a"] * 4,
    PARTS + [("h", WHOLE)] * 3 + [("h", BLOCKS)] * 2,
    [scratch((4, 16, WIDE)), scratch((8, WIDE), F32), DMA((5,)), FOUR],
)
feed_backward = call(
    feed_back_kernel,
    "feed_back",
    RAW + [BLOCKS, WHOLE, BLOCKS],
    PARTS + [("h", WHOLE)] * 2,
    [FOUR],
)
feed_weights = call(
    feed_weights_kernel,
    "feed_weights",
    [WHOLE] * 4,
    [("h", shape((4, UP, WIDE)))] * 2 + [("h", shape((4, DOWN, WIDE)))] * 2,
)
FEED_GRADS = [shape((4, UP, WIDE)), shape((4, DOWN, WIDE))]
core_sum_feed = call(
    core_sum_kernel,
    "core_sum_feed",
    FEED_GRADS + ["v"] * 2,
    [("h", grad) for grad in FEED_GRADS],
)
core_sum_attn = call(
    core_sum_kernel,
    "core_sum_attention",
    [shape((4, ATTN, WIDE)), "v"],
    [("h", shape((4, ATTN, WIDE)))],
)
finish_attn = call(
    finish_attn_kernel,
    "finish_attention",
    ["s"] + ["r"] * 8,
    [("h", shape((1, WIDE, 256), F32))] * 3
    + [("h", shape((1, 256, WIDE), F32)), ("h", shape((8, 16, WIDE)))],
    [scratch((4, 8, HALF, WIDE)), DMA((5, 8))],
)
finish_feed = call(
    finish_feed_kernel,
    "finish_feed",
    ["s"] + ["r"] * 8,
    [("h", shape((1, WIDE, WIDE), F32))] * 2 + [("h", shape((8, 16, WIDE)))],
    [scratch((8, FEED, WIDE)), DMA((8,))],
)
finish_tokens = {
    dtype: call(
        finish_tokens_kernel,
        "finish_tokens",
        ["s", "v", "v"],
        [("h", shape((1, 2, SHARE, WIDE), dtype))],
        )
    for dtype in (F32, BF16)
}


def mover(sizes, target, takes=None):
    replicas, sections, shards = sizes
    pairs = []
    for d in range(replicas):
        for s in range(sections):
            for z in range(shards):
                if takes is None or takes(d, s, z):
                    nd, ns, nz = target(d, s, z)
                    pairs.append(
                        ((d * sections + s) * shards + z, (nd * sections + ns) * shards + nz)
                    )

    def move(values):
        return lax.ppermute(values, AXES, pairs)

    return move


def solution(mesh):
    replicas, sections, shards = (mesh.shape[name] for name in AXES)
    sizes = (replicas, sections, shards)

    def quarter_of(d, s):
        return 2 * ((d >> 1) & 1) + s

    swap_y = mover(sizes, lambda d, s, z: (d, s ^ 1, z))
    swap_x = mover(sizes, lambda d, s, z: (d ^ 2, s, z))
    swap_xy = mover(sizes, lambda d, s, z: (d ^ 2, s ^ 1, z))
    swap_core = mover(sizes, lambda d, s, z: (d ^ 1, s, z))
    place_in = mover(
        sizes,
        lambda d, s, z: (
            (d & ~2) | ((z >> 1) << 1),
            z & 1,
            2 * (s ^ (z & 1)) + ((d >> 1) & 1),
        ),
    )
    place_out = [
        mover(
            sizes,
            lambda d, s, z, r=r: (
                (d & ~2) | ((z & 1) << 1),
                (z >> 1) ^ r,
                quarter_of(d, s),
            ),
        )
        for r in range(2)
    ]

    def gather(share):
        return (share, swap_y(share), swap_x(share), swap_xy(share))

    def scatter(parts):
        own, p1, p2, p3 = parts
        return (own, swap_y(p1), swap_x(p2), swap_xy(p3))

    def gather_mp(piece):
        return lax.all_gather(piece, "mp", axis=0)

    def scatter_mp(pieces):
        return lax.psum_scatter(pieces, "mp", scatter_dimension=0)

    def to_layers(first, second):
        is_first = (lax.axis_index("mp") >> 1) == 0
        return (
            place_out[0](jnp.where(is_first, first, second)),
            place_out[1](jnp.where(is_first, second, first)),
        )

    def per_device(
        inputs,
        cotangent,
        doc_ids,
        w_query,
        b_query,
        w_key,
        w_value,
        b_value,
        w_out,
        b_out,
        gain_one,
        shift_one,
        w_up,
        b_up,
        w_down,
        b_down,
        gain_two,
        shift_two,
    ):
        replica = lax.axis_index("dp")
        section = lax.axis_index("section")
        shard = lax.axis_index("mp")
        core = replica & 1
        quarter = quarter_of(replica, section)
        place = jnp.stack([core, quarter, section, shard]).astype(jnp.int32)

        attn_own, attn_peer = prep_attn(
            place,
            w_query,
            w_key,
            w_value,
            w_out,
            b_query,
            b_value,
            b_out,
            gain_one,
            shift_one,
            b_down,
            gain_two,
            shift_two,
        )
        attn_got = swap_y(attn_peer)
        which = (section ^ shard) & 1
        share_in = place_in(lax.dynamic_index_in_dim(inputs, which, 0, False))
        other_ids = swap_x(doc_ids)
        (attn_zero,) = pick(place, attn_own, attn_got, share_in, other_ids)
        whole_in = gather(share_in)
        feed_own, feed_peer = prep_feed(
            place, w_up, w_down, b_up, attn_zero, stamp(*whole_in[1:])
        )
        feed_got = swap_y(feed_peer)

        def of_layer(layer, own, got):
            return jnp.where(section == layer, own, got)

        attn_zero = gather_mp(attn_zero)
        attn_zero = (attn_zero, swap_core(attn_zero))
        feed_packs = [of_layer(layer, feed_own, feed_got) for layer in range(2)]
        up_zero = gather_mp(feed_packs[0][:UP])
        down_zero = gather_mp(feed_packs[0][UP:])
        attn_one = gather_mp(of_layer(1, attn_own, attn_got))
        up_one = gather_mp(feed_packs[1][:UP])
        down_one = gather_mp(feed_packs[1][UP:])

        mine = ((replica >> 1) & 1) == (shard & 1)
        ids = jnp.where(mine, doc_ids, other_ids)
        ids = lax.dynamic_index_in_dim(ids, shard >> 1, 0, False).reshape(4, SHARE)
        ids = jnp.concatenate(
            [lax.dynamic_index_in_dim(ids, quarter ^ r, 0, False) for r in range(4)]
        )
        id_row = ids.astype(F32)[None, :]

        def attn_half(share, whole, weights, vec):
            *parts, qkv, probs, mixed, whole, weights = attn_forward(*whole, id_row, *weights)
            parts = scatter(parts)
            middle, low, normed, inverse = norm_one(*parts, share, vec)
            return middle, low, (whole, qkv, probs, mixed, normed, inverse, weights)

        def feed_half(middle, spread, weights, vec):
            *parts, active, slope, spread, up, down = feed_forward(*spread, *weights)
            parts = scatter(parts)
            _, result, normed, inverse = norm_two(*parts, middle, vec)
            return result, (spread, active, slope, normed, inverse, up, down)

        vec_zero = attn_zero[0][0, 128:144]
        middle, low, kept_attn_zero = attn_half(share_in, whole_in, attn_zero, vec_zero)
        spread = gather(low)
        up_zero = hold(up_zero, low)
        down_zero = hold(down_zero, stamp(*spread[1:]))
        feed_zero = (up_zero, swap_core(up_zero), down_zero, swap_core(down_zero))
        first, kept_feed_zero = feed_half(middle, spread, feed_zero, vec_zero)

        whole = gather(first)
        attn_one = hold(attn_one, first)
        vec_one = attn_one[0, 128:144]
        attn_one = (attn_one, swap_core(attn_one))
        middle, low, kept_attn_one = attn_half(first, whole, attn_one, vec_one)
        spread = gather(low)
        up_one = hold(up_one, low)
        down_one = hold(down_one, low)
        feed_one = (up_one, swap_core(up_one), down_one, swap_core(down_one))
        grad_which = which ^ zero_after(kept_attn_zero[1])
        share_grad = place_in(lax.dynamic_index_in_dim(cotangent, grad_which, 0, False))
        second, kept_feed_one = feed_half(middle, spread, feed_one, vec_one)

        def feed_half_back(low, kept, *after):
            spread, active, slope, _, _, up, down = kept
            grads = gather(low)
            *parts, d_hidden, grads = feed_backward(*grads, down, slope, up, *after)
            parts = scatter(parts)
            return parts, feed_weights(d_hidden, active, spread, grads), d_hidden

        def attn_half_back(grads, kept, *after):
            _, qkv, probs, _, _, _, weights = kept
            *parts, d_rows, grads = attn_backward(*grads, weights, qkv, probs, *after)
            return parts, d_rows, grads

        def feed_sum(halves, start):
            up, up_other, down, down_other = halves
            received = [swap_core(hold(other, start)) for other in (up_other, down_other)]
            return core_sum_feed(up, down, *received)

        total, low, vec_two = norm_two_back(
            share_grad, vec_one, kept_feed_one[3], kept_feed_one[4]
        )
        parts, halves, _ = feed_half_back(low, kept_feed_one)
        outputs = to_layers(first, second)
        total, low, vec_first = norm_one_back(
            *parts, vec_one, total, kept_attn_one[4], kept_attn_one[5], halves[0], *outputs
        )
        (section_outputs,) = finish_tokens[BF16](place, *outputs)
        grads = gather(low)
        halves = feed_sum(halves, low)
        ready = stamp(*grads[1:], in_hbm(halves[0]))
        parts, d_rows, grads = attn_half_back(grads, kept_attn_one, ready)
        parts = scatter(parts)
        feed_grad_one = [scatter_mp(hold(part, ready)) for part in halves]
        own, other = attn_weights(
            d_rows, kept_attn_one[3], kept_attn_one[0], grads, vec_first, vec_two
        )
        total, low, vec_two, grad_one = norm_two_back_sum(
            *parts, vec_zero, total, kept_feed_zero[3], kept_feed_zero[4], own
        )
        (attn_grad_one,) = core_sum_attn(own, swap_core(hold(other, low)))
        parts, halves, d_hidden = feed_half_back(
            low, kept_feed_zero, attn_grad_one, feed_grad_one[0]
        )
        attn_grad_one = hold(attn_grad_one, d_hidden)
        total, low, vec_first = norm_one_back(
            *parts,
            vec_zero,
            total,
            kept_attn_zero[4],
            kept_attn_zero[5],
            halves[0],
            feed_grad_one[1],
        )
        grads = gather(low)
        halves = feed_sum(halves, low)
        ready = stamp(*grads[1:], in_hbm(halves[0]))
        attn_grad_one = scatter_mp(attn_grad_one)
        parts, d_rows, grads = attn_half_back(grads, kept_attn_zero, ready, attn_grad_one)
        feed_grad_zero = [scatter_mp(hold(part, ready)) for part in halves]
        own, other = attn_weights(
            d_rows, kept_attn_zero[3], kept_attn_zero[0], grads, vec_first, vec_two
        )
        (attn_grad_zero,) = core_sum_attn(own, swap_core(other))
        parts = scatter(parts[:1] + [hold(part, attn_grad_zero) for part in parts[1:]])
        attn_grad_zero = scatter_mp(attn_grad_zero)
        (grad_zero,) = last_sum(*parts, total)

        def exchange(zero, one, *after):
            if replicas > 4:
                groups = [[low + 4 * high for high in range(replicas // 4)] for low in range(4)]
                zero, one = lax.psum((zero, one), "dp", axis_index_groups=groups)
            mine = jnp.where(section == 0, zero, one)
            theirs = jnp.where(section == 0, one, zero)
            if after:
                mine, theirs = hold(mine, *after), hold(theirs, *after)
            pieces = [mine, swap_y(theirs), swap_x(mine), swap_xy(theirs)]
            return pieces + [swap_core(piece) for piece in pieces]

        moved = to_layers(grad_zero, grad_one)
        (section_input_grads,) = finish_tokens[F32](place, *moved)
        feeds = exchange(
            jnp.concatenate(feed_grad_zero), jnp.concatenate(feed_grad_one), stamp(*moved)
        )
        attns = exchange(attn_grad_zero, attn_grad_one)
        g_up, g_down, up_small = finish_feed(place, *feeds)
        g_query, g_key, g_value, g_out, attn_small = finish_attn(place, *attns)
        vectors = sum(piece[128:144].astype(F32) for piece in attns[0:4])
        bias = attn_small[:, 0].astype(F32)
        g_b_up = up_small[:, 0, 0:128].astype(F32).reshape(1, WIDE)
        return (
            section_outputs,
            section_input_grads,
            g_query,
            bias[:, 0:HALF].reshape(1, 256),
            g_key,
            g_value,
            bias[:, HALF : 2 * HALF].reshape(1, 256),
            g_out,
            vectors[1:2],
            vectors[2:3],
            vectors[3:4],
            g_up,
            g_b_up,
            g_down,
            vectors[4:5],
            vectors[5:6],
            vectors[6:7],
        )

    vector = P("section", None)
    by_column = P("section", None, "mp")
    by_row = P("section", "mp", None)
    spread = P("section", "mp")
    tokens = P(None, ("dp", "mp"), None)
    layer_tokens = P("section", None, ("dp", "mp"), None)
    return jax.shard_map(
        per_device,
        mesh=mesh,
        in_specs=(
            tokens,
            tokens,
            P(None, "dp", None),
            by_column,
            spread,
            by_column,
            by_column,
            spread,
            by_row,
            vector,
            vector,
            vector,
            by_column,
            spread,
            by_row,
            vector,
            vector,
            vector,
        ),
        out_specs=(
            layer_tokens,
            layer_tokens,
            by_column,
            spread,
            by_column,
            by_column,
            spread,
            by_row,
            vector,
            vector,
            vector,
            by_column,
            spread,
            by_row,
            vector,
            vector,
            vector,
        ),
        check_vma=False,
    )
```

time: 654 us -> 583 us (0.89)
  Pallas kernels: 79.6 us -> 133 us
  starting transfers between devices: 147 us -> 95 us
  waiting for transfers between devices: 340 us -> 295 us
  other arithmetic: 27 us -> 9.39 us
  local copies, waits for them, and re-layouts: 35.4 us -> 26.3 us
    pallas_call x24 -> x58, Pallas kernels: 79.6 us -> 133 us  [the longest x32 132 us: run(): pl.pallas_call(partial(body, after), name=name, in_specs=in_specs + [ANY]...]
    ppermute x79 -> x83, starting transfers between devices: 147 us -> 93.8 us  [move(): return lax.ppermute(values, AXES, pairs)]
    ppermute x79 -> x83, waiting for transfers between devices: 260 us -> 211 us  [move(): return lax.ppermute(values, AXES, pairs)]
    reduce_scatter x3 -> x6, waiting for transfers between devices: 0.01 us -> 48.8 us  [scatter_mp(): return lax.psum_scatter(pieces, 'mp', scatter_dimension=0)]
    all_gather x3 -> x6, waiting for transfers between devices: 79.5 us -> 33.6 us  [gather_mp(): return lax.all_gather(piece, 'mp', axis=0)]
    convert_element_type x6 -> x2, other arithmetic: 11.3 us -> 1.32 us  [the longest x1 1.31 us: per_device(): g_b_up = up_small[:, 0, 0:128].astype(F32).reshape(1, WIDE)]
    unnamed x157 -> x133, local copies, waits for them, and re-layouts: 29 us -> 19.6 us
  transfers between devices with their start and end apart: 85 -> 95, of which waited for: 55 -> 64; matrix products, arithmetic and copies ran while one was open for 5% -> 2% of each run, Pallas kernels for 8% -> 19%
where the time goes in v3:
time: 583 us; the launch traced here: 574 us
  waiting for transfers between devices  295 us (51%)
  Pallas kernels  133 us (23%)
  starting transfers between devices  95 us (16%)
  local copies, waits for them, and re-layouts  26.3 us (5%)
  between operations  16.3 us (3%)
  other arithmetic  9.39 us (2%)
    ppermute x83, waiting for transfers between devices, move(): return lax.ppermute(values, AXES, pairs)  211 us
    pallas_call x32, Pallas kernels, run(): pl.pallas_call(partial(body, after), name=name, in_specs=in_specs + [ANY]...  132 us
    ppermute x83, starting transfers between devices, move(): return lax.ppermute(values, AXES, pairs)  93.8 us
    reduce_scatter x6, waiting for transfers between devices, scatter_mp(): return lax.psum_scatter(pieces, 'mp', scatter_dimension=0)  48.8 us
    all_gather x6, waiting for transfers between devices, gather_mp(): return lax.all_gather(piece, 'mp', axis=0)  33.6 us
    unnamed x133, local copies, waits for them, and re-layouts  19.6 us
  transfers between devices with their start and end apart: 95, of which 64 were waited for; matrix products, arithmetic and copies ran while one was open for 2% of the time, Pallas kernels for 19%

profile of v3, /device:TPU:0, one launch (start us, length us, event | category | flops | bytes accessed | tf_op | source)
XLA Modules:
  0.0 574.3 jit_solution(827676687767437504)
XLA Ops:
  24.0 8.6 %collective-permute-start.1 = (bf16[128,1024]{1,0:T(8,128)(2,1)}, bf16[128,1024]{1,0:T(8,128)(2,1)S(1)}, u32[]{:S(2)}, u32[]{:S(2)}) collective-permute-start(bf16[128,1024]{1,0:T(8,128)(2,1)} %copy-done.13), channel_id=1, source_target_pairs={{0,4},{1,5},{2,6},{3,7},{4,0},{5,1},{6,2},{7,3},{8,12},{9,13},{10,... | collective-permute-start | bytes 786440 | tf_op jit(solution)/shard_map/ppermute | solution.py:878
  34.2 4.9 collective-permute-done.1.refs_1_.refs_0_
  50.1 11.1 %collective-permute-done.13 = bf16[272,1024]{1,0:T(8,128)(2,1)S(1)} collective-permute-done((bf16[272,1024]{1,0:T(8,128)(2,1)}, bf16[272,1024]{1,0:T(8,128)(2,1)S(1)}, u32[]{:S(2)}, u32[]{:S(2)}) %collective-permute-start.13) | collective-permute-done | bytes 557088 | tf_op jit(solution)/shard_map/ppermute | solution.py:878
  70.1 8.5 %attention.2 = (f32[128,1024]{1,0:T(8,128)S(1)}, bf16[128,1024]{1,0:T(8,128)(2,1)}, bf16[128,1024]{1,0:T(8,128)(2,1)}, bf16[128,1024]{1,0:T(8,128)(2,1)S(1)}, bf...) custom-call(bf16[128,1024]{1,0:T(8,128)(2,1)S(1)} %copy-done.14, ...), custom_call_target="tpu_custom_call" | custom-call | tf_op jit(solution)/shard_map/attention/pallas_call | solution.py:172
  110.7 14.4 %all-gather.17.cloned.1.call-done = bf16[512,1024]{1,0:T(8,128)(2,1)} async-done(((bf16[128,1024]{1,0:T(8,128)(2,1)}), bf16[512,1024]{1,0:T(8,128)(2,1)}) %all-gather.17.cloned.1.call-update) | async-done | bytes 1048592 | tf_op jit(solution)/shard_map/all_gather | solution.py:922
  131.1 5.0 feed.2
  162.0 5.2 collective-permute-done.19.refs_1_
  175.3 7.0 %attention.3 = (f32[128,1024]{1,0:T(8,128)S(1)}, bf16[128,1024]{1,0:T(8,128)(2,1)S(1)}, bf16[128,1024]{1,0:T(8,128)(2,1)S(1)}, bf16[128,1024]{1,0:T(8,128)(2,1)S...) custom-call(bf16[128,1024]{1,0:T(8,128)(2,1)S(1)} %copy-done.6, ...), custom_call_target="tpu_custom_call" | custom-call | tf_op jit(solution)/shard_map/attention/pallas_call | solution.py:172
  199.5 16.6 %all-gather.23.cloned.1.call-done = bf16[512,1024]{1,0:T(8,128)(2,1)} async-done(((bf16[128,1024]{1,0:T(8,128)(2,1)}), bf16[512,1024]{1,0:T(8,128)(2,1)}) %all-gather.23.cloned.1.call-update) | async-done | bytes 1048592 | tf_op jit(solution)/shard_map/all_gather | solution.py:922
  233.0 6.2 %feed.3 = (f32[128,1024]{1,0:T(8,128)S(1)}, bf16[128,1024]{1,0:T(8,128)(2,1)S(1)}, bf16[128,1024]{1,0:T(8,128)(2,1)S(1)}, bf16[128,1024]{1,0:T(8,128)(2,1)S(1)},...) custom-call(bf16[128,1024]{1,0:T(8,128)(2,1)S(1)} %copy-done.16, ...), custom_call_target="tpu_custom_call" | custom-call | tf_op jit(solution)/shard_map/feed/pallas_call | solution.py:172
  247.7 7.0 %collective-permute-done.32.refs_2_ = bf16[128,1024]{1,0:T(8,128)(2,1)S(1)} collective-permute-done((bf16[128,1024]{1,0:T(8,128)(2,1)S(1)}, bf16[128,1024]{1,0:T(8,128)(2,1)S(1)}, u32[]{:S(2)}, u32[]{:S(2)}) %collective-permute-start.32) | collective-permute-done | bytes 262176 | tf_op jit(solution)/shard_map/ppermute | solution.py:878
  274.5 8.7 %collective-permute-done.38.refs_2_ = bf16[128,1024]{1,0:T(8,128)(2,1)S(1)} collective-permute-done((bf16[128,1024]{1,0:T(8,128)(2,1)S(1)}, bf16[128,1024]{1,0:T(8,128)(2,1)S(1)}, u32[]{:S(2)}, u32[]{:S(2)}) %collective-permute-start.38) | collective-permute-done | bytes 262176 | tf_op jit(solution)/shard_map/ppermute | solution.py:878
  286.1 6.0 %feed_back.2 = (f32[128,1024]{1,0:T(8,128)S(1)}, bf16[128,1024]{1,0:T(8,128)(2,1)S(1)}, bf16[128,1024]{1,0:T(8,128)(2,1)S(1)}, bf16[128,1024]{1,0:T(8,128)(2,1)S...) custom-call(bf16[128,1024]{1,0:T(8,128)(2,1)S(1)} %get-tuple-element.161.refs_0_, ...), custom_call_target="tpu_custom_call" | custom-call | tf_op jit(solution)/shard_map/feed_back/pallas_call | solution.py:172
  296.1 6.9 %feed_weights.2 = (bf16[4,144,1024]{2,1,0:T(8,128)(2,1)}, bf16[4,144,1024]{2,1,0:T(8,128)(2,1)}, bf16[4,128,1024]{2,1,0:T(8,128)(2,1)}, bf16[4,128,1024]{2,1,0:T(8,128)(2,1)}) custom-call(bf16[512,1024]{1,0:T(8,128)(2,1)} %get-tuple-element.172.refs_0_, bf16[512,1024]{1,0:T(8,128)(2,1)} %get-tuple-element.173.refs_1_, ...), custom_call_target="tpu_custom_call" | custom-call | tf_op jit(solution)/shard_map/feed_weights/pallas_call | solution.py:172
  306.1 5.5 collective-permute-done.42.refs_3_
  326.7 5.0 collective-permute-done.45.refs_2_.refs_3_
  333.3 9.1 %attention_back.2 = (f32[128,1024]{1,0:T(8,128)S(1)}, bf16[128,1024]{1,0:T(8,128)(2,1)S(1)}, bf16[128,1024]{1,0:T(8,128)(2,1)S(1)}, bf16[128,1024]{1,0:T(8,128)(...) custom-call(bf16[128,1024]{1,0:T(8,128)(2,1)S(1)} %copy-done.12, ...), custom_call_target="tpu_custom_call" | custom-call | tf_op jit(solution)/shard_map/attention_back/pallas_call | solution.py:172
  376.1 6.1 %feed_back.3 = (f32[128,1024]{1,0:T(8,128)S(1)}, bf16[128,1024]{1,0:T(8,128)(2,1)S(1)}, bf16[128,1024]{1,0:T(8,128)(2,1)S(1)}, bf16[128,1024]{1,0:T(8,128)(2,1)S...) custom-call(bf16[128,1024]{1,0:T(8,128)(2,1)S(1)} %copy-done.29, ...), custom_call_target="tpu_custom_call" | custom-call | tf_op jit(solution)/shard_map/feed_back/pallas_call | solution.py:172
  385.8 6.8 %feed_weights.3 = (bf16[4,144,1024]{2,1,0:T(8,128)(2,1)}, bf16[4,144,1024]{2,1,0:T(8,128)(2,1)}, bf16[4,128,1024]{2,1,0:T(8,128)(2,1)}, bf16[4,128,1024]{2,1,0:T(8,128)(2,1)}) custom-call(bf16[512,1024]{1,0:T(8,128)(2,1)} %get-tuple-element.211.refs_0_.refs_1_, bf16[512,1024]{1,0:T(8,128)(2,1)} %get-tuple-element.212.refs_1_, ...), custom_call_target="tpu_custom_call" | custom-call | tf_op jit(solution)/shard_map/feed_weights/pallas_call | solution.py:172
  420.2 9.1 %attention_back.3 = (f32[128,1024]{1,0:T(8,128)S(1)}, bf16[128,1024]{1,0:T(8,128)(2,1)S(1)}, bf16[128,1024]{1,0:T(8,128)(2,1)S(1)}, bf16[128,1024]{1,0:T(8,128)(...) custom-call(bf16[128,1024]{1,0:T(8,128)(2,1)S(1)} %copy-done.10, ...), custom_call_target="tpu_custom_call" | custom-call | tf_op jit(solution)/shard_map/attention_back/pallas_call | solution.py:172
  443.5 6.8 %collective-permute-done.66.refs_3_ = bf16[128,1024]{1,0:T(8,128)(2,1)S(1)} collective-permute-done((bf16[128,1024]{1,0:T(8,128)(2,1)}, bf16[128,1024]{1,0:T(8,128)(2,1)S(1)}, u32[]{:S(2)}, u32[]{:S(2)}) %collective-permute-start.66) | collective-permute-done | bytes 262176 | tf_op jit(solution)/shard_map/ppermute | solution.py:878
  461.5 44.6 %reduce-scatter.15.cloned.1.call-done = bf16[1,144,1024]{2,1,0:T(8,128)(2,1)} async-done(((bf16[4,144,1024]{2,1,0:T(8,128)(2,1)}), bf16[1,144,1024]{2,1,0:T(8,128)(2,1)}) %reduce-scatter.15.cloned.1.call-update) | async-done | bytes 294928 | tf_op jit(solution)/shard_map/reduce_scatter | solution.py:925
  514.1 21.2 %collective-permute-done.76.refs_2_ = bf16[272,1024]{1,0:T(8,128)(2,1)S(1)} collective-permute-done((bf16[272,1024]{1,0:T(8,128)(2,1)}, bf16[272,1024]{1,0:T(8,128)(2,1)S(1)}, u32[]{:S(2)}, u32[]{:S(2)}) %collective-permute-start.76) | collective-permute-done | bytes 557088 | tf_op jit(solution)/shard_map/ppermute | solution.py:878
  547.4 7.2 %finish_feed.1 = (f32[1,1024,1024]{2,1,0:T(8,128)}, f32[1,1024,1024]{2,1,0:T(8,128)}, bf16[8,16,1024]{2,1,0:T(8,128)(2,1)}) custom-call(s32[4]{0:T(128)S(1)} %pad_add_fusion.refs_0_, bf16[272,1024]{1,0:T(8,128)(2,1)} %hold.38.refs_1_, bf16[272,1024]{1,0:T(8,128)(2,1)} %copy-done.51, bf16[272,1024]{1,0:T(8,128)(2,1)} %copy-done.53, ...), custom_call_target="tpu_custom_call" | custom-call | tf_op jit(solution)/shard_map/finish_feed/pallas_call | solution.py:172
  (394 shorter events, 320.5 us)
Async XLA Ops:
  7.2 58.4 %all-gather.13.cloned.1.call-start = ((), (), s32[]{:S(2)}) async-start(), calls=%async_computation.12 | async-start | bytes 1474560 | tf_op jit(solution)/shard_map/all_gather | solution.py:922
  24.0 75.5 %all-gather.15.cloned.1.call-start = ((), (), s32[]{:S(2)}) async-start(), calls=%async_computation.13 | async-start | bytes 1474560 | tf_op jit(solution)/shard_map/all_gather | solution.py:922
  63.9 61.2 %all-gather.17.cloned.1.call-start = ((), (), s32[]{:S(2)}) async-start(), calls=%async_computation.14 | async-start | bytes 1310720 | tf_op jit(solution)/shard_map/all_gather | solution.py:922
  64.7 91.8 %all-gather.19.cloned.1.call-start = ((), (), s32[]{:S(2)}) async-start(), calls=%async_computation.15 | async-start | bytes 1474560 | tf_op jit(solution)/shard_map/all_gather | solution.py:922
  65.6 133.9 %all-gather.21.cloned.1.call-start = ((), (), s32[]{:S(2)}) async-start(), calls=%async_computation.16 | async-start | bytes 1474560 | tf_op jit(solution)/shard_map/all_gather | solution.py:922
  82.9 133.1 %all-gather.23.cloned.1.call-start = ((), (), s32[]{:S(2)}) async-start(), calls=%async_computation.17 | async-start | bytes 1310720 | tf_op jit(solution)/shard_map/all_gather | solution.py:922
  99.4 25.7 %collective-permute-start.14 = (bf16[4,144,1024]{2,1,0:T(8,128)(2,1)}, bf16[4,144,1024]{2,1,0:T(8,128)(2,1)S(1)}, u32[]{:S(2)}, u32[]{:S(2)}) collective-permute-start(bf16[4,144,1024]{2,1,0:T(8,128)(2,1)} %hold.20.refs_4_), channel_id=1, source_target_pairs={{0,8},{1,9},{2,10},{3,11},{4,12},{5,13},{6,14},{7,15},{8,0},{9,1},... | collective-permute-start | bytes 3538952 | tf_op jit(solution)/shard_map/ppermute | solution.py:878
  158.2 217.8 %reduce-scatter.7.cloned.1.call-start = ((), (), s32[]{:S(2)}) async-start(), calls=%async_computation.6 | async-start | bytes 1474560 | tf_op jit(solution)/shard_map/reduce_scatter | solution.py:925
  199.5 32.3 %collective-permute-start.29 = (bf16[4,144,1024]{2,1,0:T(8,128)(2,1)}, bf16[4,144,1024]{2,1,0:T(8,128)(2,1)S(1)}, u32[]{:S(2)}, u32[]{:S(2)}) collective-permute-start(bf16[4,144,1024]{2,1,0:T(8,128)(2,1)} %hold.23.refs_4_), channel_id=1, source_target_pairs={{0,8},{1,9},{2,10},{3,11},{4,12},{5,13},{6,14},{7,15},{8,0},{9,1},... | collective-permute-start | bytes 3538952 | tf_op jit(solution)/shard_map/ppermute | solution.py:878
  262.1 21.2 %collective-permute-start.38 = (bf16[128,1024]{1,0:T(8,128)(2,1)S(1)}, bf16[128,1024]{1,0:T(8,128)(2,1)S(1)}, u32[]{:S(2)}, u32[]{:S(2)}) collective-permute-start(bf16[128,1024]{1,0:T(8,128)(2,1)S(1)} %get-tuple-element.161.refs_0_), channel_id=1, source_target_pairs={{0,16},{1,17},{2,18},{3,19},{4,20},{5,21},{6,22},{7,23},{8,24},{9,... | collective-permute-start | bytes 786440 | tf_op jit(solution)/shard_map/ppermute | solution.py:878
  265.5 20.6 %collective-permute-start.39 = (bf16[128,1024]{1,0:T(8,128)(2,1)S(1)}, bf16[128,1024]{1,0:T(8,128)(2,1)S(1)}, u32[]{:S(2)}, u32[]{:S(2)}) collective-permute-start(bf16[128,1024]{1,0:T(8,128)(2,1)S(1)} %get-tuple-element.161.refs_0_), channel_id=1, source_target_pairs={{0,20},{1,21},{2,22},{3,23},{4,16},{5,17},{6,18},{7,19},{8,28},{9,... | collective-permute-start | bytes 786440 | tf_op jit(solution)/shard_map/ppermute | solution.py:878
  265.5 37.5 %collective-permute-start.34 = (bf16[128,1024]{1,0:T(8,128)(2,1)S(1)}, bf16[128,1024]{1,0:T(8,128)(2,1)S(1)}, u32[]{:S(2)}, u32[]{:S(2)}) collective-permute-start(bf16[128,1024]{1,0:T(8,128)(2,1)S(1)} %get-tuple-element.256), channel_id=1, source_target_pairs={{0,0},{1,16},{2,4},{3,20},{4,1},{5,17},{6,5},{7,21},{8,8},{9,24},{... | collective-permute-start | bytes 786440 | tf_op jit(solution)/shard_map/ppermute | solution.py:878
  266.2 36.8 %collective-permute-start.35 = (bf16[128,1024]{1,0:T(8,128)(2,1)S(1)}, bf16[128,1024]{1,0:T(8,128)(2,1)S(1)}, u32[]{:S(2)}, u32[]{:S(2)}) collective-permute-start(bf16[128,1024]{1,0:T(8,128)(2,1)S(1)} %get-tuple-element.255), channel_id=1, source_target_pairs={{0,4},{1,20},{2,0},{3,16},{4,5},{5,21},{6,1},{7,17},{8,12},{9,28},... | collective-permute-start | bytes 786440 | tf_op jit(solution)/shard_map/ppermute | solution.py:878
  332.2 60.4 %reduce-scatter.9.cloned.1.call-start = ((), (), s32[]{:S(2)}) async-start(), calls=%async_computation.7 | async-start | bytes 1310720 | tf_op jit(solution)/shard_map/reduce_scatter | solution.py:925
  333.0 87.2 %reduce-scatter.11.cloned.1.call-start = ((), (), s32[]{:S(2)}) async-start(), calls=%async_computation.8 | async-start | bytes 1474560 | tf_op jit(solution)/shard_map/reduce_scatter | solution.py:925
  382.2 79.3 %reduce-scatter.17.cloned.1.call-start = ((), (), s32[]{:S(2)}) async-start(), calls=%async_computation.11 | async-start | bytes 1310720 | tf_op jit(solution)/shard_map/reduce_scatter | solution.py:925
  416.0 90.1 %reduce-scatter.15.cloned.1.call-start = ((), (), s32[]{:S(2)}) async-start(), calls=%async_computation.10 | async-start | bytes 1474560 | tf_op jit(solution)/shard_map/reduce_scatter | solution.py:925
  416.8 123.0 %reduce-scatter.13.cloned.1.call-start = ((), (), s32[]{:S(2)}) async-start(), calls=%async_computation.9 | async-start | bytes 1474560 | tf_op jit(solution)/shard_map/reduce_scatter | solution.py:925
  458.2 50.3 %collective-permute-start.67 = (bf16[128,1024]{1,0:T(8,128)(2,1)S(1)}, bf16[128,1024]{1,0:T(8,128)(2,1)S(1)}, u32[]{:S(2)}, u32[]{:S(2)}) collective-permute-start(bf16[128,1024]{1,0:T(8,128)(2,1)S(1)} %get-tuple-element.254), channel_id=1, source_target_pairs={{0,0},{1,16},{2,4},{3,20},{4,1},{5,17},{6,5},{7,21},{8,8},{9,24},{... | collective-permute-start | bytes 786440 | tf_op jit(solution)/shard_map/ppermute | solution.py:878
  458.9 49.6 %collective-permute-start.68 = (bf16[128,1024]{1,0:T(8,128)(2,1)S(1)}, bf16[128,1024]{1,0:T(8,128)(2,1)S(1)}, u32[]{:S(2)}, u32[]{:S(2)}) collective-permute-start(bf16[128,1024]{1,0:T(8,128)(2,1)S(1)} %get-tuple-element.253), channel_id=1, source_target_pairs={{0,4},{1,20},{2,0},{3,16},{4,5},{5,21},{6,1},{7,17},{8,12},{9,28},... | collective-permute-start | bytes 786440 | tf_op jit(solution)/shard_map/ppermute | solution.py:878
  509.1 26.1 %collective-permute-start.76 = (bf16[272,1024]{1,0:T(8,128)(2,1)}, bf16[272,1024]{1,0:T(8,128)(2,1)S(1)}, u32[]{:S(2)}, u32[]{:S(2)}) collective-permute-start(bf16[272,1024]{1,0:T(8,128)(2,1)} %hold.39), channel_id=1, source_target_pairs={{0,4},{1,5},{2,6},{3,7},{4,0},{5,1},{6,2},{7,3},{8,12},{9,13},{10,... | collective-permute-start | bytes 1671176 | tf_op jit(solution)/shard_map/ppermute | solution.py:878
  509.1 26.1 %collective-permute-start.78 = (bf16[272,1024]{1,0:T(8,128)(2,1)}, bf16[272,1024]{1,0:T(8,128)(2,1)S(1)}, u32[]{:S(2)}, u32[]{:S(2)}) collective-permute-start(bf16[272,1024]{1,0:T(8,128)(2,1)} %hold.39), channel_id=1, source_target_pairs={{0,20},{1,21},{2,22},{3,23},{4,16},{5,17},{6,18},{7,19},{8,28},{9,... | collective-permute-start | bytes 1671176 | tf_op jit(solution)/shard_map/ppermute | solution.py:878
  513.6 25.2 %collective-permute-start.77 = (bf16[272,1024]{1,0:T(8,128)(2,1)}, bf16[272,1024]{1,0:T(8,128)(2,1)S(1)}, u32[]{:S(2)}, u32[]{:S(2)}) collective-permute-start(bf16[272,1024]{1,0:T(8,128)(2,1)} %hold.38.refs_1_), channel_id=1, source_target_pairs={{0,16},{1,17},{2,18},{3,19},{4,20},{5,21},{6,22},{7,23},{8,24},{9,... | collective-permute-start | bytes 1671176 | tf_op jit(solution)/shard_map/ppermute | solution.py:878
  514.1 28.3 %collective-permute-start.79 = (bf16[272,1024]{1,0:T(8,128)(2,1)}, bf16[272,1024]{1,0:T(8,128)(2,1)}, u32[]{:S(2)}, u32[]{:S(2)}) collective-permute-start(bf16[272,1024]{1,0:T(8,128)(2,1)} %hold.38.refs_1_), channel_id=1, source_target_pairs={{0,8},{1,9},{2,10},{3,11},{4,12},{5,13},{6,14},{7,15},{8,0},{9,1},... | collective-permute-start | bytes 1671176 | tf_op jit(solution)/shard_map/ppermute | solution.py:878
  (137 other events, 1241.9 us)
Sparse Core Ops, SparseCore 0:
  24.1 39.8 all-gather.12
  66.1 30.2 all-gather.14
  98.0 27.0 all-gather.16
  126.5 29.9 all-gather.18
  157.9 29.5 all-gather.20
  188.9 27.0 all-gather.22
  332.4 29.3 reduce-scatter.6
  364.0 25.8 reduce-scatter.8
  392.3 27.8 reduce-scatter.10
  423.0 25.8 reduce-scatter.16
  451.2 54.8 reduce-scatter.14
  508.9 30.8 reduce-scatter.12

commit v4 on v3

--- a/solution.py
+++ b/solution.py
@@ -14,9 +14,7 @@
 HEADS = 4
 HALF = 32
 ATTN = 144
-UP = 144
-DOWN = 128
-FEED = UP + DOWN
+FEED = 128
 AXES = ("dp", "section", "mp")
 EPSILON = 1e-05
 NEGATIVE = -1e30
@@ -237,12 +235,14 @@
     return pl.ds(pl.multiple_of(i * width, width), width)
 
 
-def prep_attn_kernel(place, wq, wk, wv, wo, bq, bv, v0, v1, v2, v3, v4, v5, own, peer, turned):
+def prep_attn_kernel(
+    place, wq, wk, wv, wo, bq, bv, bu, v0, v1, v2, v3, v4, v5, own, peer, turned
+):
     core, quarter = place[0], place[1]
     for a, w in enumerate((wq, wk, wv)):
         turned[a] = w.get()[0].T
     layer_rows = [v.get()[...].astype(F32) for v in (v0, v1, v2, v3, v4, v5)]
-    wo, bq, bv = wo.get(), bq.get(), bv.get()
+    wo, bq, bv, bu = wo.get(), bq.get(), bv.get(), bu.get()
     source = lax.broadcasted_iota(jnp.int32, (256, 128), 0)
     lane = lax.broadcasted_iota(jnp.int32, (256, 128), 1)
     for out, block in ((own, quarter), (peer, quarter ^ 1)):
@@ -267,6 +267,11 @@
         out[128:144] = block_rows.astype(BF16)
         first_row = lax.broadcasted_iota(jnp.int32, (16, 128), 0) == 0
         out[128:144, 0:128] = jnp.where(first_row, bias, block_rows[:, 0:128]).astype(BF16)
+        for h in range(2):
+            unit = pl.multiple_of(block * 256 + (core ^ h) * 128, 128)
+            lanes = slice(128 * (h + 1), 128 * (h + 2))
+            piece = jnp.where(first_row, bu[:, pl.ds(unit, 128)].astype(F32), block_rows[:, lanes])
+            out[128:144, lanes] = piece.astype(BF16)
 
 
 def pick_kernel(place, own, got, out):
@@ -274,7 +279,7 @@
     out[...] = jnp.where(jnp.full(own.shape, place[2]) == 0, own[...], got[...])
 
 
-def prep_feed_kernel(place, up, down, bu, own, peer, column, sems):
+def prep_feed_kernel(place, up, down, own, peer, column, sems):
     core, quarter = place[0], place[1]
     copies = []
     outs = ((own, quarter), (peer, quarter ^ 1))
@@ -285,20 +290,16 @@
         )
         copies.append(
             pltpu.make_async_copy(
-                down.at[0, pl.ds(unit, 128)], out.buffer.at[UP:FEED], sems.at[2 * i + 1]
+                down.at[0, pl.ds(unit, 128)],
+                out.buffer.at[FEED : 2 * FEED],
+                sems.at[2 * i + 1],
             )
         )
     for copy in copies:
         copy.start()
-    row = lax.broadcasted_iota(jnp.int32, (16, 128), 0) == 0
-    for i, (out, block) in enumerate(outs):
-        out[128:144] = jnp.zeros((16, WIDE), BF16)
-        for h in range(2):
-            unit = pl.multiple_of(block * 256 + (core ^ h) * 128, 128)
-            piece = bu[:, pl.ds(unit, 128)].astype(F32)
-            out[128:144, 128 * h : 128 * h + 128] = jnp.where(row, piece, 0.0).astype(BF16)
+    for i, (out, _) in enumerate(outs):
         copies[2 * i].wait()
-        out[0:128] = column[i].T
+        out[0:FEED] = column[i].T
         copies[2 * i + 1].wait()
         out.send()
 
@@ -497,10 +498,12 @@
 
 
 def attn_weights_kernel(
-    d_rows, mixed, x_all, g_all, vec_one, vec_two, own, other
+    d_rows, mixed, x_all, g_all, vec_one, vec_two, feed_bias, own, other
 ):
-    operands = (d_rows, mixed, x_all, g_all, vec_one, vec_two)
-    d_rows, mixed, x_all, g_all, vec_one, vec_two = (operand.get() for operand in operands)
+    operands = (d_rows, mixed, x_all, g_all, vec_one, vec_two, feed_bias)
+    d_rows, mixed, x_all, g_all, vec_one, vec_two, feed_bias = (
+        operand.get() for operand in operands
+    )
     for a in range(4):
         if a < 3:
             value = dot_tn(d_rows[:, 256 * a : 256 * a + 256], x_all[...])
@@ -527,6 +530,9 @@
             )
             out[z, 128:144] = block.astype(BF16)
             out[z, 128:144, 0:128] = jnp.where(first_row, bias, block[:, 0:128]).astype(BF16)
+            unit = 512 * half + 128 * z
+            piece = jnp.where(first_row, feed_bias[0:1, unit : unit + 128], block[:, 128:256])
+            out[z, 128:144, 128:256] = piece.astype(BF16)
         out.send()
 
 
@@ -536,7 +542,7 @@
         for half in range(2):
             copies.append(
                 pltpu.make_async_copy(
-                    refs[half].at[:, 0:128],
+                    refs[half],
                     target.at[4 * half : 4 * half + 4],
                     sems.at[2 * i + half],
                 )
@@ -545,13 +551,13 @@
 
 
 def feed_kernel(
-    x0, x1, x2, x3, up_own, up_other, down_own, down_other,
+    x0, x1, x2, x3, a_own, up_own, up_other, down_own, down_other,
     own, p1, p2, p3, active, slope, x_out, up_out, down_out,
     small, bias, sems, x_sems,
 ):
     x_all, up, down = x_out.buffer, up_out.buffer, down_out.buffer
     ups, downs = load_feed((up_own, up_other), (down_own, down_other), up, down, sems)
-    copies = [pltpu.make_async_copy(up_own.at[:, 128:144], small, sems.at[4])] + ups
+    copies = [pltpu.make_async_copy(a_own.at[:, 128:144], small, sems.at[4])] + ups
     for copy in copies + downs:
         copy.start()
     arrive(join(x_all, (x0, x1, x2, x3), x_sems))
@@ -562,7 +568,7 @@
         for z in range(4):
             unit = 512 * half + 128 * z
             bias[0:8, unit : unit + 128] = jnp.broadcast_to(
-                small[z, :, 128 * half : 128 * half + 128].astype(F32)[0:1], (8, 128)
+                small[z, :, 128 * (half + 1) : 128 * (half + 2)].astype(F32)[0:1], (8, 128)
             )
 
     def units(i, carry):
@@ -615,29 +621,40 @@
 
 
 def feed_weights_kernel(
-    d_hidden, active, x_all, g_all, up_own, up_other, down_own, down_other
+    d_hidden, active, x_all, g_all, up_own, up_other, down_own, down_other, bias
 ):
     d_hidden, active, x_all, g_all = (v.get() for v in (d_hidden, active, x_all, g_all))
-    row = lax.broadcasted_iota(jnp.int32, (16, 128), 0) == 0
     for half, up, down in ((1, up_other, down_other), (0, up_own, down_own)):
 
         def pair(i, carry, half=half, up=up, down=down):
             where = columns(2 * half + i)
             value = dot_tn(d_hidden[:, where], x_all[...]).astype(BF16)
-            up[pl.ds(2 * i, 2), 0:128] = value.reshape(2, 128, WIDE)
+            up[pl.ds(2 * i, 2)] = value.reshape(2, 128, WIDE)
             value = dot_tn(active[:, where], g_all[...]).astype(BF16)
             down[pl.ds(2 * i, 2)] = value.reshape(2, 128, WIDE)
             return carry
 
         lax.fori_loop(0, 2, pair, 0)
-        total = jnp.sum(d_hidden[:, 512 * half : 512 * half + 512].astype(F32), 0, keepdims=True)
-        for z in range(4):
-            up[z, 128:144] = jnp.zeros((16, WIDE), BF16)
-            up[z, 128:144, 0:128] = jnp.where(row, total[:, 128 * z : 128 * z + 128], 0.0).astype(
-                BF16
-            )
         up.send()
         down.send()
+    bias[...] = sums(d_hidden[...].astype(F32))
+
+
+def assemble_kernel(place, x0, x1, x2, x3, out):
+    for r, piece in enumerate((x0, x1, x2, x3)):
+        out[place[3] ^ r] = piece[...]
+
+
+def core_sum_feed_kernel(place, up, down, up_got, down_got, up_out, down_out):
+    down_out[...] = (down.get()[...].astype(F32) + down_got[...].astype(F32)).astype(BF16)
+    up_out[...] = (up.get()[...].astype(F32) + up_got[...].astype(F32)).astype(BF16)
+
+
+def split_kernel(place, own, received, *outs):
+    own = own.get()
+    for r, out in enumerate(outs):
+        z = place[3] ^ r
+        out[...] = (own[z].astype(F32) + received[z].astype(F32)).astype(BF16)
 
 
 def core_sum_kernel(*refs):
@@ -655,46 +672,49 @@
     ]
 
 
+def gathered(pieces, place, target, sems):
+    copies = [
+        pltpu.make_async_copy(pieces[i], target.at[to], sems.at[i]) for i, to in ordered(place)
+    ]
+    for copy in copies:
+        copy.start()
+    arrive(copies)
+
+
 def finish_attn_kernel(place, *refs):
     pieces, refs = refs[:8], refs[8:]
-    gq, gk, gv, go, small, turned, sems = refs
-    copies = []
-    for i, to in ordered(place):
-        copies.append(
-            pltpu.make_async_copy(pieces[i].at[128:144], small.buffer.at[to], sems.at[4, i])
-        )
-        for a in range(4):
-            copies.append(
-                pltpu.make_async_copy(
-                    pieces[i].at[HALF * a : HALF * a + HALF], turned.at[a, to], sems.at[a, i]
-                )
-            )
-    for copy in copies:
-        copy.start()
-    for copy in copies:
-        copy.wait()
+    gq, gk, gv, go, bias_query, bias_value, bias_up, *vectors, block, sems = refs
+    gathered(pieces, place, block, sems)
     for a, out in enumerate((gq, gk, gv)):
-        out[0] = turned[a].reshape(256, WIDE).astype(F32).T
+        rows = block[:, HALF * a : HALF * a + HALF].reshape(256, WIDE)
+        out[0] = rows.astype(F32).T
         out.send()
-    go[0] = turned[3].reshape(256, WIDE).astype(F32)
-
-
-def finish_feed_kernel(place, *refs):
+    go[0] = block[:, 3 * HALF : 4 * HALF].reshape(256, WIDE).astype(F32)
+    go.send()
+    small = [block[i, 128:144].astype(F32) for i in range(8)]
+    bias_query[...] = jnp.concatenate([v[0:1, 0:HALF] for v in small], 1)
+    bias_value[...] = jnp.concatenate([v[0:1, HALF : 2 * HALF] for v in small], 1)
+    for i in range(8):
+        bias_up[:, 128 * i : 128 * i + 128] = small[i][0:1, 128:256]
+    total = 0.5 * sum(small[1:], small[0])
+    for i, out in enumerate(vectors):
+        out[...] = total[i + 1 : i + 2]
+
+
+def finish_up_kernel(place, *refs):
     pieces, refs = refs[:8], refs[8:]
-    up, down, small, block, sems = refs
-    copies = []
-    for i, to in ordered(place):
-        copies.append(pltpu.make_async_copy(pieces[i], block.at[to], sems.at[i]))
-    for copy in copies:
-        copy.start()
-    for copy in copies:
-        copy.wait()
+    out, block, sems = refs
+    gathered(pieces, place, block, sems)
     for i in range(8):
-        down[0, 128 * i : 128 * i + 128] = block[i, UP:FEED].astype(F32)
-    down.send()
+        out[0, :, 128 * i : 128 * i + 128] = block[i].astype(F32).T
+
+
+def finish_down_kernel(place, *refs):
+    pieces, refs = refs[:8], refs[8:]
+    out, block, sems = refs
+    gathered(pieces, place, block, sems)
     for i in range(8):
-        up[0, :, 128 * i : 128 * i + 128] = block[i, 0:128].astype(F32).T
-        small[i] = block[i, 128:144]
+        out[0, 128 * i : 128 * i + 128] = block[i].astype(F32)
 
 
 def finish_tokens_kernel(place, a, b, out):
@@ -731,7 +751,7 @@
     + [shape((1, WIDE, 256))] * 3
     + [shape((1, 256, WIDE))]
     + [shape((1, 256))] * 2
-    + [ROW] * 6,
+    + [ROW] * 7,
     [("h", shape((ATTN, WIDE)))] * 2,
     [scratch((3, 256, WIDE))],
 )
@@ -744,8 +764,8 @@
 prep_feed = call(
     prep_feed_kernel,
     "pack_feed",
-    ["s", "r", "r", "v"],
-    [("h", shape((FEED, WIDE)))] * 2,
+    ["s", "r", "r"],
+    [("h", shape((2 * FEED, WIDE)))] * 2,
     [scratch((2, WIDE, 128)), DMA((4,))],
 )
 norm_one, norm_two = (
@@ -800,13 +820,13 @@
 attn_weights = call(
     attn_weights_kernel,
     "attention_weights",
-    [shape((SEQ, 768)), shape((SEQ, 256)), WHOLE, WHOLE] + [VECTORS] * 2,
+    [shape((SEQ, 768)), shape((SEQ, 256)), WHOLE, WHOLE] + [VECTORS] * 3,
     [("h", shape((4, ATTN, WIDE)))] * 2,
 )
 feed_forward = call(
     feed_kernel,
     "feed",
-    RAW + ["a"] * 4,
+    RAW + ["a"] * 5,
     PARTS + [("h", WHOLE)] * 3 + [("h", BLOCKS)] * 2,
     [scratch((4, 16, WIDE)), scratch((8, WIDE), F32), DMA((5,)), FOUR],
 )
@@ -821,14 +841,35 @@
     feed_weights_kernel,
     "feed_weights",
     [WHOLE] * 4,
-    [("h", shape((4, UP, WIDE)))] * 2 + [("h", shape((4, DOWN, WIDE)))] * 2,
-)
-FEED_GRADS = [shape((4, UP, WIDE)), shape((4, DOWN, WIDE))]
+    [("h", shape((4, FEED, WIDE)))] * 4 + [("h", VECTORS)],
+)
+FEED_HALVES = ["s", shape((4, FEED, WIDE)), shape((4, FEED, WIDE)), "v", "v"]
 core_sum_feed = call(
+    core_sum_feed_kernel,
+    "core_sum_feed",
+    FEED_HALVES,
+    [("h", shape((4, FEED, WIDE))), ("h", shape((4, FEED, WIDE)))],
+)
+split_attn, split_down = (
+    call(
+        split_kernel,
+        "core_split",
+        ["s", shape((4, rows, WIDE)), "v"],
+        [("v", shape((rows, WIDE)))] * 4,
+    )
+    for rows in (ATTN, FEED)
+)
+core_sum_up = call(
     core_sum_kernel,
-    "core_sum_feed",
-    FEED_GRADS + ["v"] * 2,
-    [("h", grad) for grad in FEED_GRADS],
+    "core_sum_up",
+    [shape((4, FEED, WIDE)), "v"],
+    [("h", shape((4, FEED, WIDE)))],
+)
+assemble = call(
+    assemble_kernel,
+    "assemble",
+    ["s"] + ["v"] * 4,
+    [("h", shape((4, FEED, WIDE)))],
 )
 core_sum_attn = call(
     core_sum_kernel,
@@ -836,30 +877,40 @@
     [shape((4, ATTN, WIDE)), "v"],
     [("h", shape((4, ATTN, WIDE)))],
 )
+EIGHT = DMA((8,))
 finish_attn = call(
     finish_attn_kernel,
     "finish_attention",
-    ["s"] + ["r"] * 8,
+    ["s"] + ["a"] * 8,
     [("h", shape((1, WIDE, 256), F32))] * 3
-    + [("h", shape((1, 256, WIDE), F32)), ("h", shape((8, 16, WIDE)))],
-    [scratch((4, 8, HALF, WIDE)), DMA((5, 8))],
-)
-finish_feed = call(
-    finish_feed_kernel,
-    "finish_feed",
-    ["s"] + ["r"] * 8,
-    [("h", shape((1, WIDE, WIDE), F32))] * 2 + [("h", shape((8, 16, WIDE)))],
-    [scratch((8, FEED, WIDE)), DMA((8,))],
-)
-finish_tokens = {
-    dtype: call(
+    + [("h", shape((1, 256, WIDE), F32))]
+    + [("h", shape((1, 256), F32))] * 2
+    + [("h", shape((1, WIDE), F32))] * 7,
+    [scratch((8, ATTN, WIDE)), EIGHT],
+)
+finish_up = call(
+    finish_up_kernel,
+    "finish_up",
+    ["s"] + ["a"] * 8,
+    [("h", shape((1, WIDE, WIDE), F32))],
+    [scratch((8, FEED, WIDE)), EIGHT],
+)
+finish_down = call(
+    finish_down_kernel,
+    "finish_down",
+    ["s"] + ["a"] * 8,
+    [("h", shape((1, WIDE, WIDE), F32))],
+    [scratch((8, FEED, WIDE)), EIGHT],
+)
+finish_tokens, finish_grads = (
+    call(
         finish_tokens_kernel,
-        "finish_tokens",
+        name,
         ["s", "v", "v"],
         [("h", shape((1, 2, SHARE, WIDE), dtype))],
-        )
-    for dtype in (F32, BF16)
-}
+    )
+    for name, dtype in (("finish_tokens", BF16), ("finish_grads", F32))
+)
 
 
 def mover(sizes, target, takes=None):
@@ -884,28 +935,32 @@
     replicas, sections, shards = (mesh.shape[name] for name in AXES)
     sizes = (replicas, sections, shards)
 
-    def quarter_of(d, s):
+    def block_of(d, s):
         return 2 * ((d >> 1) & 1) + s
+
+    def quarter_of(d, s, z):
+        return (block_of(d, s) + z) % 4
 
     swap_y = mover(sizes, lambda d, s, z: (d, s ^ 1, z))
     swap_x = mover(sizes, lambda d, s, z: (d ^ 2, s, z))
     swap_xy = mover(sizes, lambda d, s, z: (d ^ 2, s ^ 1, z))
     swap_core = mover(sizes, lambda d, s, z: (d ^ 1, s, z))
-    place_in = mover(
-        sizes,
-        lambda d, s, z: (
-            (d & ~2) | ((z >> 1) << 1),
-            z & 1,
-            2 * (s ^ (z & 1)) + ((d >> 1) & 1),
-        ),
-    )
+    swap_z = [mover(sizes, lambda d, s, z, r=r: (d, s, z ^ r)) for r in range(1, 4)]
+    def into_place(d, s, z):
+        x = (d >> 1) & 1
+        micro = s ^ ((z - x) & 1)
+        plane = 2 * micro + x
+        block = (z - plane) % 4
+        return (d & ~2) | ((block >> 1) << 1), block & 1, plane
+
+    place_in = mover(sizes, into_place)
     place_out = [
         mover(
             sizes,
             lambda d, s, z, r=r: (
                 (d & ~2) | ((z & 1) << 1),
                 (z >> 1) ^ r,
-                quarter_of(d, s),
+                quarter_of(d, s, z),
             ),
         )
         for r in range(2)
@@ -917,6 +972,9 @@
     def scatter(parts):
         own, p1, p2, p3 = parts
         return (own, swap_y(p1), swap_x(p2), swap_xy(p3))
+
+    def gather_direct(place, piece):
+        return assemble(place, piece, *[move(piece) for move in swap_z])[0]
 
     def gather_mp(piece):
         return lax.all_gather(piece, "mp", axis=0)
@@ -955,8 +1013,8 @@
         section = lax.axis_index("section")
         shard = lax.axis_index("mp")
         core = replica & 1
-        quarter = quarter_of(replica, section)
-        place = jnp.stack([core, quarter, section, shard]).astype(jnp.int32)
+        block = block_of(replica, section)
+        place = jnp.stack([core, block, section, shard]).astype(jnp.int32)
 
         attn_own, attn_peer = prep_attn(
             place,
@@ -966,6 +1024,7 @@
             w_out,
             b_query,
             b_value,
+            b_up,
             b_out,
             gain_one,
             shift_one,
@@ -974,13 +1033,13 @@
             shift_two,
         )
         attn_got = swap_y(attn_peer)
-        which = (section ^ shard) & 1
+        which = section ^ ((shard - ((replica >> 1) & 1)) & 1)
         share_in = place_in(lax.dynamic_index_in_dim(inputs, which, 0, False))
         other_ids = swap_x(doc_ids)
         (attn_zero,) = pick(place, attn_own, attn_got, share_in, other_ids)
         whole_in = gather(share_in)
         feed_own, feed_peer = prep_feed(
-            place, w_up, w_down, b_up, attn_zero, stamp(*whole_in[1:])
+            place, w_up, w_down, attn_zero, stamp(*whole_in[1:])
         )
         feed_got = swap_y(feed_peer)
 
@@ -990,22 +1049,25 @@
         attn_zero = gather_mp(attn_zero)
         attn_zero = (attn_zero, swap_core(attn_zero))
         feed_packs = [of_layer(layer, feed_own, feed_got) for layer in range(2)]
-        up_zero = gather_mp(feed_packs[0][:UP])
-        down_zero = gather_mp(feed_packs[0][UP:])
+        up_zero = gather_mp(feed_packs[0][:FEED])
+        down_zero = gather_direct(place, feed_packs[0][FEED:])
         attn_one = gather_mp(of_layer(1, attn_own, attn_got))
-        up_one = gather_mp(feed_packs[1][:UP])
-        down_one = gather_mp(feed_packs[1][UP:])
+        up_one = gather_mp(feed_packs[1][:FEED])
+        down_one = gather_mp(feed_packs[1][FEED:])
 
         mine = ((replica >> 1) & 1) == (shard & 1)
         ids = jnp.where(mine, doc_ids, other_ids)
         ids = lax.dynamic_index_in_dim(ids, shard >> 1, 0, False).reshape(4, SHARE)
         ids = jnp.concatenate(
-            [lax.dynamic_index_in_dim(ids, quarter ^ r, 0, False) for r in range(4)]
+            [
+                lax.dynamic_index_in_dim(ids, ((block ^ r) + shard) % 4, 0, False)
+                for r in range(4)
+            ]
         )
         id_row = ids.astype(F32)[None, :]
 
-        def attn_half(share, whole, weights, vec):
-            *parts, qkv, probs, mixed, whole, weights = attn_forward(*whole, id_row, *weights)
+        def attn_half(share, whole, weights, vec, *after):
+            *parts, qkv, probs, mixed, whole, weights = attn_forward(*whole, id_row, *weights, *after)
             parts = scatter(parts)
             middle, low, normed, inverse = norm_one(*parts, share, vec)
             return middle, low, (whole, qkv, probs, mixed, normed, inverse, weights)
@@ -1021,7 +1083,7 @@
         spread = gather(low)
         up_zero = hold(up_zero, low)
         down_zero = hold(down_zero, stamp(*spread[1:]))
-        feed_zero = (up_zero, swap_core(up_zero), down_zero, swap_core(down_zero))
+        feed_zero = (attn_zero[0], up_zero, swap_core(up_zero), down_zero, swap_core(down_zero))
         first, kept_feed_zero = feed_half(middle, spread, feed_zero, vec_zero)
 
         whole = gather(first)
@@ -1032,7 +1094,7 @@
         spread = gather(low)
         up_one = hold(up_one, low)
         down_one = hold(down_one, low)
-        feed_one = (up_one, swap_core(up_one), down_one, swap_core(down_one))
+        feed_one = (attn_one[0], up_one, swap_core(up_one), down_one, swap_core(down_one))
         grad_which = which ^ zero_after(kept_attn_zero[1])
         share_grad = place_in(lax.dynamic_index_in_dim(cotangent, grad_which, 0, False))
         second, kept_feed_one = feed_half(middle, spread, feed_one, vec_one)
@@ -1049,35 +1111,36 @@
             *parts, d_rows, grads = attn_backward(*grads, weights, qkv, probs, *after)
             return parts, d_rows, grads
 
-        def feed_sum(halves, start):
-            up, up_other, down, down_other = halves
+        def feed_sum(total, halves, start, *after):
+            up, up_other, down, down_other, _ = halves
             received = [swap_core(hold(other, start)) for other in (up_other, down_other)]
-            return core_sum_feed(up, down, *received)
+            return total(place, up, down, *received, *after)
 
         total, low, vec_two = norm_two_back(
             share_grad, vec_one, kept_feed_one[3], kept_feed_one[4]
         )
         parts, halves, _ = feed_half_back(low, kept_feed_one)
+        feed_bias = halves[4]
         outputs = to_layers(first, second)
         total, low, vec_first = norm_one_back(
             *parts, vec_one, total, kept_attn_one[4], kept_attn_one[5], halves[0], *outputs
         )
-        (section_outputs,) = finish_tokens[BF16](place, *outputs)
+        (section_outputs,) = finish_tokens(place, *outputs)
         grads = gather(low)
-        halves = feed_sum(halves, low)
+        halves = feed_sum(core_sum_feed, halves, low)
         ready = stamp(*grads[1:], in_hbm(halves[0]))
         parts, d_rows, grads = attn_half_back(grads, kept_attn_one, ready)
         parts = scatter(parts)
-        feed_grad_one = [scatter_mp(hold(part, ready)) for part in halves]
+        up_grad_one, down_grad_one = [scatter_mp(hold(part, ready)) for part in halves]
         own, other = attn_weights(
-            d_rows, kept_attn_one[3], kept_attn_one[0], grads, vec_first, vec_two
+            d_rows, kept_attn_one[3], kept_attn_one[0], grads, vec_first, vec_two, feed_bias
         )
         total, low, vec_two, grad_one = norm_two_back_sum(
             *parts, vec_zero, total, kept_feed_zero[3], kept_feed_zero[4], own
         )
         (attn_grad_one,) = core_sum_attn(own, swap_core(hold(other, low)))
         parts, halves, d_hidden = feed_half_back(
-            low, kept_feed_zero, attn_grad_one, feed_grad_one[0]
+            low, kept_feed_zero, attn_grad_one, up_grad_one
         )
         attn_grad_one = hold(attn_grad_one, d_hidden)
         total, low, vec_first = norm_one_back(
@@ -1087,20 +1150,35 @@
             kept_attn_zero[4],
             kept_attn_zero[5],
             halves[0],
-            feed_grad_one[1],
+            down_grad_one,
         )
         grads = gather(low)
-        halves = feed_sum(halves, low)
-        ready = stamp(*grads[1:], in_hbm(halves[0]))
         attn_grad_one = scatter_mp(attn_grad_one)
+        up, up_other, down, down_other, feed_bias = halves
+        (up,) = core_sum_up(up, swap_core(hold(up_other, low)))
+        ready = stamp(*grads[1:], in_hbm(up))
         parts, d_rows, grads = attn_half_back(grads, kept_attn_zero, ready, attn_grad_one)
-        feed_grad_zero = [scatter_mp(hold(part, ready)) for part in halves]
+        up_grad_zero = scatter_mp(hold(up, ready))
         own, other = attn_weights(
-            d_rows, kept_attn_zero[3], kept_attn_zero[0], grads, vec_first, vec_two
-        )
-        (attn_grad_zero,) = core_sum_attn(own, swap_core(other))
-        parts = scatter(parts[:1] + [hold(part, attn_grad_zero) for part in parts[1:]])
-        attn_grad_zero = scatter_mp(attn_grad_zero)
+            d_rows,
+            kept_attn_zero[3],
+            kept_attn_zero[0],
+            grads,
+            vec_first,
+            vec_two,
+            feed_bias,
+        )
+        attn_parts = split_attn(place, own, swap_core(other))
+        down_parts = split_down(place, down, swap_core(hold(down_other, low)))
+        parts = scatter(parts[:1] + [hold(part, attn_parts[1]) for part in parts[1:]])
+
+        def scatter_direct(parts, *after):
+            moved = [move(hold(part, *after)) for move, part in zip(swap_z, parts[1:])]
+            total = sum((part.astype(F32) for part in moved), parts[0].astype(F32))
+            return total.astype(BF16), stamp(*moved)
+
+        down_grad_zero, down_there = scatter_direct(down_parts, up_grad_zero)
+        attn_grad_zero, attn_there = scatter_direct(attn_parts, down_there)
         (grad_zero,) = last_sum(*parts, total)
 
         def exchange(zero, one, *after):
@@ -1114,35 +1192,32 @@
             pieces = [mine, swap_y(theirs), swap_x(mine), swap_xy(theirs)]
             return pieces + [swap_core(piece) for piece in pieces]
 
-        moved = to_layers(grad_zero, grad_one)
-        (section_input_grads,) = finish_tokens[F32](place, *moved)
-        feeds = exchange(
-            jnp.concatenate(feed_grad_zero), jnp.concatenate(feed_grad_one), stamp(*moved)
-        )
+        moved = to_layers(hold(grad_zero, attn_there), grad_one)
+        (section_input_grads,) = finish_grads(place, *moved)
+        ups = exchange(up_grad_zero, up_grad_one, grad_zero)
+        (g_up,) = finish_up(place, *ups)
+        downs = exchange(down_grad_zero, down_grad_one)
+        (g_down,) = finish_down(place, *downs)
         attns = exchange(attn_grad_zero, attn_grad_one)
-        g_up, g_down, up_small = finish_feed(place, *feeds)
-        g_query, g_key, g_value, g_out, attn_small = finish_attn(place, *attns)
-        vectors = sum(piece[128:144].astype(F32) for piece in attns[0:4])
-        bias = attn_small[:, 0].astype(F32)
-        g_b_up = up_small[:, 0, 0:128].astype(F32).reshape(1, WIDE)
+        g_query, g_key, g_value, g_out, g_b_query, g_b_value, g_b_up, *vectors = finish_attn(place, *attns)
         return (
             section_outputs,
             section_input_grads,
             g_query,
-            bias[:, 0:HALF].reshape(1, 256),
+            g_b_query,
             g_key,
             g_value,
-            bias[:, HALF : 2 * HALF].reshape(1, 256),
+            g_b_value,
             g_out,
-            vectors[1:2],
-            vectors[2:3],
-            vectors[3:4],
+            vectors[0],
+            vectors[1],
+            vectors[2],
             g_up,
             g_b_up,
             g_down,
-            vectors[4:5],
-            vectors[5:6],
-            vectors[6:7],
+            vectors[3],
+            vectors[4],
+            vectors[5],
         )
 
     vector = P("section", None)

time: 583 us -> 552 us (0.947)
  the two profiles are of different devices: /device:TPU:0 before, /device:TPU:5 now
where the time goes in v4:
time: 552 us; the launch traced here: 543 us
  waiting for transfers between devices  223 us (40%)
  Pallas kernels  138 us (25%)
  starting transfers between devices  127 us (23%)
  local copies, waits for them, and re-layouts  31 us (6%)
  between operations  15.9 us (3%)
  other arithmetic  8.7 us (2%)
    ppermute x99, waiting for transfers between devices, move(): return lax.ppermute(values, AXES, pairs)  186 us
    pallas_call x35, Pallas kernels, run(): pl.pallas_call(partial(body, after), name=name, in_specs=in_specs + [ANY]...  137 us
    ppermute x99, starting transfers between devices, move(): return lax.ppermute(values, AXES, pairs)  126 us
    unnamed x160, local copies, waits for them, and re-layouts  29.3 us
    all_gather x5, waiting for transfers between devices, gather_mp(): return lax.all_gather(piece, 'mp', axis=0)  22.8 us
    reduce_scatter x4, waiting for transfers between devices, scatter_mp(): return lax.psum_scatter(pieces, 'mp', scatter_dimension=0)  13.8 us
  transfers between devices with their start and end apart: 108, of which 50 were waited for; matrix products, arithmetic and copies ran while one was open for 2% of the time, Pallas kernels for 22%

profile of v4, /device:TPU:5, one launch (start us, length us, event | category | flops | bytes accessed | tf_op | source)
XLA Modules:
  0.0 543.3 jit_solution(3259024884522099946)
XLA Ops:
  10.8 6.3 %collective-permute-start = (bf16[128,1024]{1,0:T(8,128)(2,1)S(1)}, bf16[128,1024]{1,0:T(8,128)(2,1)S(1)}, u32[]{:S(2)}, u32[]{:S(2)}) collective-permute-start(bf16[128,1024]{1,0:T(8,128)(2,1)S(1)} %dynamic-slice_bitcast_fusion.1), channel_id=1, source_target_pairs={{0,0},{1,22},{2,16},{3,6},{4,18},{5,4},{6,2},{7,20},{8,8},{9,30},{... | collective-permute-start | bytes 786440 | tf_op jit(solution)/shard_map/ppermute | solution.py:929
  35.3 6.4 %collective-permute-done.3.refs_3_.refs_2_ = bf16[128,1024]{1,0:T(8,128)(2,1)S(1)} collective-permute-done((bf16[128,1024]{1,0:T(8,128)(2,1)}, bf16[128,1024]{1,0:T(8,128)(2,1)S(1)}, u32[]{:S(2)}, u32[]{:S(2)}) %collective-permute-start.3) | collective-permute-done | bytes 262176 | tf_op jit(solution)/shard_map/ppermute | solution.py:929
  45.4 10.6 %collective-permute-done.13 = bf16[256,1024]{1,0:T(8,128)(2,1)S(1)} collective-permute-done((bf16[256,1024]{1,0:T(8,128)(2,1)}, bf16[256,1024]{1,0:T(8,128)(2,1)S(1)}, u32[]{:S(2)}, u32[]{:S(2)}) %collective-permute-start.13) | collective-permute-done | bytes 524320 | tf_op jit(solution)/shard_map/ppermute | solution.py:929
  69.4 8.5 %attention.2 = (f32[128,1024]{1,0:T(8,128)S(1)}, bf16[128,1024]{1,0:T(8,128)(2,1)}, bf16[128,1024]{1,0:T(8,128)(2,1)S(1)}, bf16[128,1024]{1,0:T(8,128)(2,1)S(1)}...) custom-call(bf16[128,1024]{1,0:T(8,128)(2,1)S(1)} %copy-done.22, ...), custom_call_target="tpu_custom_call" | custom-call | tf_op jit(solution)/shard_map/attention/pallas_call | solution.py:170
  101.4 7.0 %all-gather.13.cloned.1.call-done = bf16[512,1024]{1,0:T(8,128)(2,1)} async-done(((bf16[128,1024]{1,0:T(8,128)(2,1)}), bf16[512,1024]{1,0:T(8,128)(2,1)}) %all-gather.13.cloned.1.call-update) | async-done | bytes 1048592 | tf_op jit(solution)/shard_map/all_gather | solution.py:980
  115.2 6.9 %feed.2 = (f32[128,1024]{1,0:T(8,128)S(1)}, bf16[128,1024]{1,0:T(8,128)(2,1)}, bf16[128,1024]{1,0:T(8,128)(2,1)}, bf16[128,1024]{1,0:T(8,128)(2,1)}, bf16[512,10...) custom-call(bf16[128,1024]{1,0:T(8,128)(2,1)S(1)} %copy-done.29, ...), custom_call_target="tpu_custom_call" | custom-call | tf_op jit(solution)/shard_map/feed/pallas_call | solution.py:170
  130.9 6.4 %collective-permute-done.21.refs_3_ = bf16[128,1024]{1,0:T(8,128)(2,1)S(1)} collective-permute-done((bf16[128,1024]{1,0:T(8,128)(2,1)}, bf16[128,1024]{1,0:T(8,128)(2,1)S(1)}, u32[]{:S(2)}, u32[]{:S(2)}) %collective-permute-start.21) | collective-permute-done | bytes 262176 | tf_op jit(solution)/shard_map/ppermute | solution.py:929
  151.1 6.6 %collective-permute-done.24.refs_3_ = bf16[128,1024]{1,0:T(8,128)(2,1)S(1)} collective-permute-done((bf16[128,1024]{1,0:T(8,128)(2,1)S(1)}, bf16[128,1024]{1,0:T(8,128)(2,1)S(1)}, u32[]{:S(2)}, u32[]{:S(2)}) %collective-permute-start.24) | collective-permute-done | bytes 262176 | tf_op jit(solution)/shard_map/ppermute | solution.py:929
  158.9 7.0 %attention.3 = (f32[128,1024]{1,0:T(8,128)S(1)}, bf16[128,1024]{1,0:T(8,128)(2,1)S(1)}, bf16[128,1024]{1,0:T(8,128)(2,1)S(1)}, bf16[128,1024]{1,0:T(8,128)(2,1)S...) custom-call(bf16[128,1024]{1,0:T(8,128)(2,1)S(1)} %copy-done.13, ...), custom_call_target="tpu_custom_call" | custom-call | tf_op jit(solution)/shard_map/attention/pallas_call | solution.py:170
  171.8 6.1 %collective-permute-done.28.refs_3_ = bf16[128,1024]{1,0:T(8,128)(2,1)S(1)} collective-permute-done((bf16[128,1024]{1,0:T(8,128)(2,1)S(1)}, bf16[128,1024]{1,0:T(8,128)(2,1)S(1)}, u32[]{:S(2)}, u32[]{:S(2)}) %collective-permute-start.28) | collective-permute-done | bytes 262176 | tf_op jit(solution)/shard_map/ppermute | solution.py:929
  184.1 14.0 %all-gather.17.cloned.1.call-done = bf16[512,1024]{1,0:T(8,128)(2,1)} async-done(((bf16[128,1024]{1,0:T(8,128)(2,1)}), bf16[512,1024]{1,0:T(8,128)(2,1)}) %all-gather.17.cloned.1.call-update) | async-done | bytes 1048592 | tf_op jit(solution)/shard_map/all_gather | solution.py:980
  216.4 6.3 %feed.3 = (f32[128,1024]{1,0:T(8,128)S(1)}, bf16[128,1024]{1,0:T(8,128)(2,1)S(1)}, bf16[128,1024]{1,0:T(8,128)(2,1)S(1)}, bf16[128,1024]{1,0:T(8,128)(2,1)S(1)},...) custom-call(bf16[128,1024]{1,0:T(8,128)(2,1)S(1)} %copy-done.17, ...), custom_call_target="tpu_custom_call" | custom-call | tf_op jit(solution)/shard_map/feed/pallas_call | solution.py:170
  230.0 9.7 %collective-permute-done.36.refs_3_ = bf16[128,1024]{1,0:T(8,128)(2,1)S(1)} collective-permute-done((bf16[128,1024]{1,0:T(8,128)(2,1)S(1)}, bf16[128,1024]{1,0:T(8,128)(2,1)S(1)}, u32[]{:S(2)}, u32[]{:S(2)}) %collective-permute-start.36) | collective-permute-done | bytes 262176 | tf_op jit(solution)/shard_map/ppermute | solution.py:929
  255.0 11.8 %collective-permute-done.42.refs_3_ = bf16[128,1024]{1,0:T(8,128)(2,1)S(1)} collective-permute-done((bf16[128,1024]{1,0:T(8,128)(2,1)S(1)}, bf16[128,1024]{1,0:T(8,128)(2,1)S(1)}, u32[]{:S(2)}, u32[]{:S(2)}) %collective-permute-start.42) | collective-permute-done | bytes 262176 | tf_op jit(solution)/shard_map/ppermute | solution.py:929
  276.2 6.4 %feed_weights.2 = (bf16[4,128,1024]{2,1,0:T(8,128)(2,1)}, bf16[4,128,1024]{2,1,0:T(8,128)(2,1)}, bf16[4,128,1024]{2,1,0:T(8,128)(2,1)}, bf16[4,128,1024]{2,1,0:T(8,128)(2,1)}, f32[8,1024]{1,0:T(8,128)}) custom-call(bf16[512,1024]{1,0:T(8,128)(2,1)} %get-tuple-element.185.refs_0_, bf16[512,1024]{1,0:T(8,128)(2,1)} %get-tuple-element.186.refs_1_, ...), custom_call_target="tpu_custom_call" | custom-call | tf_op jit(solution)/shard_map/feed_weights/pallas_call | solution.py:170
  309.2 9.1 %attention_back.2 = (f32[128,1024]{1,0:T(8,128)S(1)}, bf16[128,1024]{1,0:T(8,128)(2,1)S(1)}, bf16[128,1024]{1,0:T(8,128)(2,1)S(1)}, bf16[128,1024]{1,0:T(8,128)(...) custom-call(bf16[128,1024]{1,0:T(8,128)(2,1)S(1)} %copy-done.15, ...), custom_call_target="tpu_custom_call" | custom-call | tf_op jit(solution)/shard_map/attention_back/pallas_call | solution.py:170
  350.8 6.0 %feed_back.3 = (f32[128,1024]{1,0:T(8,128)S(1)}, bf16[128,1024]{1,0:T(8,128)(2,1)S(1)}, bf16[128,1024]{1,0:T(8,128)(2,1)S(1)}, bf16[128,1024]{1,0:T(8,128)(2,1)S...) custom-call(bf16[128,1024]{1,0:T(8,128)(2,1)S(1)} %copy-done.33, ...), custom_call_target="tpu_custom_call" | custom-call | tf_op jit(solution)/shard_map/feed_back/pallas_call | solution.py:170
  359.8 6.3 %feed_weights.3 = (bf16[4,128,1024]{2,1,0:T(8,128)(2,1)}, bf16[4,128,1024]{2,1,0:T(8,128)(2,1)}, bf16[4,128,1024]{2,1,0:T(8,128)(2,1)}, bf16[4,128,1024]{2,1,0:T(8,128)(2,1)}, f32[8,1024]{1,0:T(8,128)}) custom-call(bf16[512,1024]{1,0:T(8,128)(2,1)} %get-tuple-element.225.refs_0_.refs_1_, bf16[512,1024]{1,0:T(8,128)(2,1)} %get-tuple-element.226.refs_1_, ...), custom_call_target="tpu_custom_call" | custom-call | tf_op jit(solution)/shard_map/feed_weights/pallas_call | solution.py:170
  395.4 9.1 %attention_back.3 = (f32[128,1024]{1,0:T(8,128)S(1)}, bf16[128,1024]{1,0:T(8,128)(2,1)S(1)}, bf16[128,1024]{1,0:T(8,128)(2,1)S(1)}, bf16[128,1024]{1,0:T(8,128)(...) custom-call(bf16[128,1024]{1,0:T(8,128)(2,1)S(1)} %copy-done.20, ...), custom_call_target="tpu_custom_call" | custom-call | tf_op jit(solution)/shard_map/attention_back/pallas_call | solution.py:170
  413.8 10.4 %reduce-scatter.11.cloned.1.call-done = bf16[1,128,1024]{2,1,0:T(8,128)(2,1)} async-done(((bf16[4,128,1024]{2,1,0:T(8,128)(2,1)}), bf16[1,128,1024]{2,1,0:T(8,128)(2,1)}) %reduce-scatter.11.cloned.1.call-update) | async-done | bytes 262160 | tf_op jit(solution)/shard_map/reduce_scatter | solution.py:983
  434.6 13.7 %collective-permute-done.71.refs_1_ = bf16[128,1024]{1,0:T(8,128)(2,1)S(1)} collective-permute-done((bf16[128,1024]{1,0:T(8,128)(2,1)}, bf16[128,1024]{1,0:T(8,128)(2,1)S(1)}, u32[]{:S(2)}, u32[]{:S(2)}) %collective-permute-start.71) | collective-permute-done | bytes 262176 | tf_op jit(solution)/shard_map/ppermute | solution.py:929
  462.2 6.7 %collective-permute-done.92.refs_2_ = bf16[128,1024]{1,0:T(8,128)(2,1)S(1)} collective-permute-done((bf16[128,1024]{1,0:T(8,128)(2,1)}, bf16[128,1024]{1,0:T(8,128)(2,1)S(1)}, u32[]{:S(2)}, u32[]{:S(2)}) %collective-permute-start.92) | collective-permute-done | bytes 262176 | tf_op jit(solution)/shard_map/ppermute | solution.py:929
  497.3 13.7 %collective-permute-done.76.refs_1_ = bf16[128,1024]{1,0:T(8,128)(2,1)S(1)} collective-permute-done((bf16[128,1024]{1,0:T(8,128)(2,1)S(1)}, bf16[128,1024]{1,0:T(8,128)(2,1)S(1)}, u32[]{:S(2)}, u32[]{:S(2)}) %collective-permute-start.76) | collective-permute-done | bytes 262176 | tf_op jit(solution)/shard_map/ppermute | solution.py:929
  514.4 6.2 %collective-permute-done.80.refs_4_ = bf16[144,1024]{1,0:T(8,128)(2,1)S(1)} collective-permute-done((bf16[144,1024]{1,0:T(8,128)(2,1)S(1)}, bf16[144,1024]{1,0:T(8,128)(2,1)S(1)}, u32[]{:S(2)}, u32[]{:S(2)}) %collective-permute-start.80) | collective-permute-done | bytes 294944 | tf_op jit(solution)/shard_map/ppermute | solution.py:929
  (448 shorter events, 326.2 us)
Async XLA Ops:
  7.2 54.7 %all-gather.11.cloned.1.call-start = ((), (), s32[]{:S(2)}) async-start(), calls=%async_computation.8 | async-start | bytes 1474560 | tf_op jit(solution)/shard_map/all_gather | solution.py:980
  28.7 79.7 %all-gather.13.cloned.1.call-start = ((), (), s32[]{:S(2)}) async-start(), calls=%async_computation.9 | async-start | bytes 1310720 | tf_op jit(solution)/shard_map/all_gather | solution.py:980
  58.9 83.9 %all-gather.15.cloned.1.call-start = ((), (), s32[]{:S(2)}) async-start(), calls=%async_computation.10 | async-start | bytes 1474560 | tf_op jit(solution)/shard_map/all_gather | solution.py:980
  60.0 120.5 %all-gather.19.cloned.1.call-start = ((), (), s32[]{:S(2)}) async-start(), calls=%async_computation.12 | async-start | bytes 1310720 | tf_op jit(solution)/shard_map/all_gather | solution.py:980
  63.7 31.4 %collective-permute-start.15 = (bf16[128,1024]{1,0:T(8,128)(2,1)}, bf16[128,1024]{1,0:T(8,128)(2,1)}, u32[]{:S(2)}, u32[]{:S(2)}) collective-permute-start(bf16[128,1024]{1,0:T(8,128)(2,1)} %get-tuple-element.287.refs_1_), channel_id=1, source_target_pairs={{0,1},{1,0},{2,3},{3,2},{4,5},{5,4},{6,7},{7,6},{8,9},{9,8},{10,11... | collective-permute-start | bytes 786440 | tf_op jit(solution)/shard_map/ppermute | solution.py:929
  63.9 32.4 %collective-permute-start.16 = (bf16[128,1024]{1,0:T(8,128)(2,1)}, bf16[128,1024]{1,0:T(8,128)(2,1)}, u32[]{:S(2)}, u32[]{:S(2)}) collective-permute-start(bf16[128,1024]{1,0:T(8,128)(2,1)} %get-tuple-element.287.refs_1_), channel_id=1, source_target_pairs={{0,2},{1,3},{2,0},{3,1},{4,6},{5,7},{6,4},{7,5},{8,10},{9,11},{10,... | collective-permute-start | bytes 786440 | tf_op jit(solution)/shard_map/ppermute | solution.py:929
  81.5 116.5 %all-gather.17.cloned.1.call-start = ((), (), s32[]{:S(2)}) async-start(), calls=%async_computation.11 | async-start | bytes 1310720 | tf_op jit(solution)/shard_map/all_gather | solution.py:980
  125.7 225.1 %reduce-scatter.5.cloned.1.call-start = ((), (), s32[]{:S(2)}) async-start(), calls=%async_computation.4 | async-start | bytes 1310720 | tf_op jit(solution)/shard_map/reduce_scatter | solution.py:983
  180.5 32.8 %collective-permute-start.33 = (bf16[4,128,1024]{2,1,0:T(8,128)(2,1)}, bf16[4,128,1024]{2,1,0:T(8,128)(2,1)}, u32[]{:S(2)}, u32[]{:S(2)}) collective-permute-start(bf16[4,128,1024]{2,1,0:T(8,128)(2,1)} %hold.30.refs_7_), channel_id=1, source_target_pairs={{0,8},{1,9},{2,10},{3,11},{4,12},{5,13},{6,14},{7,15},{8,0},{9,1},... | collective-permute-start | bytes 3145736 | tf_op jit(solution)/shard_map/ppermute | solution.py:929
  248.1 34.5 %collective-permute-start.37 = (bf16[128,1024]{1,0:T(8,128)(2,1)S(1)}, bf16[128,1024]{1,0:T(8,128)(2,1)S(1)}, u32[]{:S(2)}, u32[]{:S(2)}) collective-permute-start(bf16[128,1024]{1,0:T(8,128)(2,1)S(1)} %get-tuple-element.284), channel_id=1, source_target_pairs={{0,0},{1,17},{2,6},{3,23},{4,1},{5,18},{6,7},{7,20},{8,8},{9,25},{... | collective-permute-start | bytes 786440 | tf_op jit(solution)/shard_map/ppermute | solution.py:929
  251.5 31.1 %collective-permute-start.38 = (bf16[128,1024]{1,0:T(8,128)(2,1)S(1)}, bf16[128,1024]{1,0:T(8,128)(2,1)S(1)}, u32[]{:S(2)}, u32[]{:S(2)}) collective-permute-start(bf16[128,1024]{1,0:T(8,128)(2,1)S(1)} %get-tuple-element.283), channel_id=1, source_target_pairs={{0,4},{1,21},{2,2},{3,19},{4,5},{5,22},{6,3},{7,16},{8,12},{9,29},... | collective-permute-start | bytes 786440 | tf_op jit(solution)/shard_map/ppermute | solution.py:929
  308.0 58.1 %reduce-scatter.7.cloned.1.call-start = ((), (), s32[]{:S(2)}) async-start(), calls=%async_computation.5 | async-start | bytes 1310720 | tf_op jit(solution)/shard_map/reduce_scatter | solution.py:983
  308.8 86.6 %reduce-scatter.9.cloned.1.call-start = ((), (), s32[]{:S(2)}) async-start(), calls=%async_computation.6 | async-start | bytes 1474560 | tf_op jit(solution)/shard_map/reduce_scatter | solution.py:983
  356.8 67.3 %reduce-scatter.11.cloned.1.call-start = ((), (), s32[]{:S(2)}) async-start(), calls=%async_computation.7 | async-start | bytes 1310720 | tf_op jit(solution)/shard_map/reduce_scatter | solution.py:983
  424.7 23.5 %collective-permute-start.71 = (bf16[128,1024]{1,0:T(8,128)(2,1)}, bf16[128,1024]{1,0:T(8,128)(2,1)S(1)}, u32[]{:S(2)}, u32[]{:S(2)}) collective-permute-start(bf16[128,1024]{1,0:T(8,128)(2,1)} %hold.44), channel_id=1, source_target_pairs={{0,2},{1,3},{2,0},{3,1},{4,6},{5,7},{6,4},{7,5},{8,10},{9,11},{10,... | collective-permute-start | bytes 786440 | tf_op jit(solution)/shard_map/ppermute | solution.py:929
  425.1 23.1 %collective-permute-start.70 = (bf16[128,1024]{1,0:T(8,128)(2,1)}, bf16[128,1024]{1,0:T(8,128)(2,1)S(1)}, u32[]{:S(2)}, u32[]{:S(2)}) collective-permute-start(bf16[128,1024]{1,0:T(8,128)(2,1)} %hold.43), channel_id=1, source_target_pairs={{0,1},{1,0},{2,3},{3,2},{4,5},{5,4},{6,7},{7,6},{8,9},{9,8},{10,11... | collective-permute-start | bytes 786440 | tf_op jit(solution)/shard_map/ppermute | solution.py:929
  431.9 21.7 %collective-permute-start.68 = (bf16[128,1024]{1,0:T(8,128)(2,1)}, bf16[128,1024]{1,0:T(8,128)(2,1)S(1)}, u32[]{:S(2)}, u32[]{:S(2)}) collective-permute-start(bf16[128,1024]{1,0:T(8,128)(2,1)} %hold.40), channel_id=1, source_target_pairs={{0,20},{1,21},{2,22},{3,23},{4,16},{5,17},{6,18},{7,19},{8,28},{9,... | collective-permute-start | bytes 786440 | tf_op jit(solution)/shard_map/ppermute | solution.py:929
  433.4 22.7 %collective-permute-start.66 = (bf16[128,1024]{1,0:T(8,128)(2,1)}, bf16[128,1024]{1,0:T(8,128)(2,1)}, u32[]{:S(2)}, u32[]{:S(2)}) collective-permute-start(bf16[128,1024]{1,0:T(8,128)(2,1)} %hold.38), channel_id=1, source_target_pairs={{0,4},{1,5},{2,6},{3,7},{4,0},{5,1},{6,2},{7,3},{8,12},{9,13},{10,... | collective-permute-start | bytes 786440 | tf_op jit(solution)/shard_map/ppermute | solution.py:929
  454.4 22.7 %collective-permute-start.74 = (bf16[144,1024]{1,0:T(8,128)(2,1)}, bf16[144,1024]{1,0:T(8,128)(2,1)S(1)}, u32[]{:S(2)}, u32[]{:S(2)}) collective-permute-start(bf16[144,1024]{1,0:T(8,128)(2,1)} %hold.47), channel_id=1, source_target_pairs={{0,2},{1,3},{2,0},{3,1},{4,6},{5,7},{6,4},{7,5},{8,10},{9,11},{10,... | collective-permute-start | bytes 884744 | tf_op jit(solution)/shard_map/ppermute | solution.py:929
  455.1 22.2 %collective-permute-start.73 = (bf16[144,1024]{1,0:T(8,128)(2,1)S(1)}, bf16[144,1024]{1,0:T(8,128)(2,1)S(1)}, u32[]{:S(2)}, u32[]{:S(2)}) collective-permute-start(bf16[144,1024]{1,0:T(8,128)(2,1)S(1)} %copy-done.8), channel_id=1, source_target_pairs={{0,1},{1,0},{2,3},{3,2},{4,5},{5,4},{6,7},{7,6},{8,9},{9,8},{10,11... | collective-permute-start | bytes 884744 | tf_op jit(solution)/shard_map/ppermute | solution.py:929
  487.6 23.4 %collective-permute-start.76 = (bf16[128,1024]{1,0:T(8,128)(2,1)S(1)}, bf16[128,1024]{1,0:T(8,128)(2,1)S(1)}, u32[]{:S(2)}, u32[]{:S(2)}) collective-permute-start(bf16[128,1024]{1,0:T(8,128)(2,1)S(1)} %get-tuple-element.282), channel_id=1, source_target_pairs={{0,0},{1,17},{2,6},{3,23},{4,1},{5,18},{6,7},{7,20},{8,8},{9,25},{... | collective-permute-start | bytes 786440 | tf_op jit(solution)/shard_map/ppermute | solution.py:929
  490.2 21.6 %collective-permute-start.77 = (bf16[128,1024]{1,0:T(8,128)(2,1)S(1)}, bf16[128,1024]{1,0:T(8,128)(2,1)S(1)}, u32[]{:S(2)}, u32[]{:S(2)}) collective-permute-start(bf16[128,1024]{1,0:T(8,128)(2,1)S(1)} %get-tuple-element.281), channel_id=1, source_target_pairs={{0,4},{1,21},{2,2},{3,19},{4,5},{5,22},{6,3},{7,16},{8,12},{9,29},... | collective-permute-start | bytes 786440 | tf_op jit(solution)/shard_map/ppermute | solution.py:929
  496.8 23.8 %collective-permute-start.80 = (bf16[144,1024]{1,0:T(8,128)(2,1)S(1)}, bf16[144,1024]{1,0:T(8,128)(2,1)S(1)}, u32[]{:S(2)}, u32[]{:S(2)}) collective-permute-start(bf16[144,1024]{1,0:T(8,128)(2,1)S(1)} %copy-done.75), channel_id=1, source_target_pairs={{0,20},{1,21},{2,22},{3,23},{4,16},{5,17},{6,18},{7,19},{8,28},{9,... | collective-permute-start | bytes 884744 | tf_op jit(solution)/shard_map/ppermute | solution.py:929
  511.8 21.3 %collective-permute-start.81 = (bf16[144,1024]{1,0:T(8,128)(2,1)S(1)}, bf16[144,1024]{1,0:T(8,128)(2,1)S(1)}, u32[]{:S(2)}, u32[]{:S(2)}) collective-permute-start(bf16[144,1024]{1,0:T(8,128)(2,1)S(1)} %broadcast_select_fusion.3.refs_1_), channel_id=1, source_target_pairs={{0,8},{1,9},{2,10},{3,11},{4,12},{5,13},{6,14},{7,15},{8,0},{9,1},... | collective-permute-start | bytes 884744 | tf_op jit(solution)/shard_map/ppermute | solution.py:929
  (164 other events, 1327.0 us)
Sparse Core Ops, SparseCore 0:
  28.8 33.0 all-gather.10
  63.4 44.8 all-gather.12
  109.9 30.2 all-gather.14
  141.6 27.4 all-gather.18
  170.6 27.4 all-gather.16
  308.2 28.7 reduce-scatter.4
  339.4 25.7 reduce-scatter.6
  367.5 27.8 reduce-scatter.8
  398.2 25.8 reduce-scatter.10

commit v5 on v4

--- a/solution.py
+++ b/solution.py
@@ -165,12 +165,15 @@
         after = len(operands) - len(in_specs)
         operands = [
             in_hbm(operand) if pin else operand
-            for pin, operand in zip(pinned + [True] * after, operands)
+            for pin, operand in zip(
+                pinned + [o.size > 1 for o in operands[len(pinned) :]], operands
+            )
         ]
         return pl.pallas_call(
             partial(body, after),
             name=name,
-            in_specs=in_specs + [ANY] * after,
+            in_specs=in_specs
+            + [ANY if o.size > 1 else SMEM for o in operands[len(in_specs) :]],
             out_specs=tuple(out_specs),
             out_shape=tuple(out_shapes),
             scratch_shapes=[buffer_of(item) for item in loads + stores]
@@ -188,26 +191,26 @@
     return pl.pallas_call(
         lambda *refs: None,
         name="hold",
-        in_specs=[HBM] + [ANY] * len(after),
+        in_specs=[HBM] + [ANY if o.size > 1 else SMEM for o in after],
         out_specs=HBM,
         out_shape=pltpu.HBM(value.shape, value.dtype),
         input_output_aliases={0: 0},
     )(in_hbm(value), *after)
 
 
-def stamp(*values):
+def stamp(*values, kept=()):
     def kernel(*refs):
-        refs[-1][...] = jnp.zeros((8, 128), F32)
+        refs[-1][0] = 0
 
     return pl.pallas_call(
         kernel,
         name="stamp",
-        in_specs=[ANY] * len(values),
-        out_specs=VMEM,
-        out_shape=shape((8, 128), F32),
+        in_specs=[VMEM] * len(values) + [ANY] * len(kept),
+        out_specs=SMEM,
+        out_shape=shape((1,), jnp.int32),
         compiler_params=pltpu.CompilerParams(vmem_limit_bytes=16 << 20),
         cost_estimate=pl.CostEstimate(flops=0, bytes_accessed=0, transcendentals=0),
-    )(*values)
+    )(*values, *[in_hbm(value) for value in kept])
 
 
 def zero_after(after):
@@ -799,7 +802,7 @@
 attn_forward = call(
     attn_kernel,
     "attention",
-    RAW + ["v", "a", "a"],
+    RAW + ["v", "r", "a"],
     PARTS
     + [
         ("h", shape((SEQ, 768))),
@@ -826,7 +829,7 @@
 feed_forward = call(
     feed_kernel,
     "feed",
-    RAW + ["a"] * 5,
+    RAW + ["r", "r", "a", "r", "a"],
     PARTS + [("h", WHOLE)] * 3 + [("h", BLOCKS)] * 2,
     [scratch((4, 16, WIDE)), scratch((8, WIDE), F32), DMA((5,)), FOUR],
 )
@@ -1081,19 +1084,19 @@
         vec_zero = attn_zero[0][0, 128:144]
         middle, low, kept_attn_zero = attn_half(share_in, whole_in, attn_zero, vec_zero)
         spread = gather(low)
-        up_zero = hold(up_zero, low)
+        up_zero = hold(up_zero, kept_attn_zero[4])
         down_zero = hold(down_zero, stamp(*spread[1:]))
         feed_zero = (attn_zero[0], up_zero, swap_core(up_zero), down_zero, swap_core(down_zero))
         first, kept_feed_zero = feed_half(middle, spread, feed_zero, vec_zero)
 
         whole = gather(first)
-        attn_one = hold(attn_one, first)
+        attn_one = hold(attn_one, kept_feed_zero[3])
         vec_one = attn_one[0, 128:144]
         attn_one = (attn_one, swap_core(attn_one))
         middle, low, kept_attn_one = attn_half(first, whole, attn_one, vec_one)
         spread = gather(low)
-        up_one = hold(up_one, low)
-        down_one = hold(down_one, low)
+        up_one = hold(up_one, kept_attn_one[4])
+        down_one = hold(down_one, stamp(*spread[1:]))
         feed_one = (attn_one[0], up_one, swap_core(up_one), down_one, swap_core(down_one))
         grad_which = which ^ zero_after(kept_attn_zero[1])
         share_grad = place_in(lax.dynamic_index_in_dim(cotangent, grad_which, 0, False))
@@ -1127,8 +1130,8 @@
         )
         (section_outputs,) = finish_tokens(place, *outputs)
         grads = gather(low)
-        halves = feed_sum(core_sum_feed, halves, low)
-        ready = stamp(*grads[1:], in_hbm(halves[0]))
+        halves = feed_sum(core_sum_feed, halves, total)
+        ready = stamp(*grads[1:], kept=[halves[0]])
         parts, d_rows, grads = attn_half_back(grads, kept_attn_one, ready)
         parts = scatter(parts)
         up_grad_one, down_grad_one = [scatter_mp(hold(part, ready)) for part in halves]
@@ -1136,9 +1139,9 @@
             d_rows, kept_attn_one[3], kept_attn_one[0], grads, vec_first, vec_two, feed_bias
         )
         total, low, vec_two, grad_one = norm_two_back_sum(
-            *parts, vec_zero, total, kept_feed_zero[3], kept_feed_zero[4], own
-        )
-        (attn_grad_one,) = core_sum_attn(own, swap_core(hold(other, low)))
+            *parts, vec_zero, total, kept_feed_zero[3], kept_feed_zero[4], own, section_outputs
+        )
+        (attn_grad_one,) = core_sum_attn(own, swap_core(hold(other, total)))
         parts, halves, d_hidden = feed_half_back(
             low, kept_feed_zero, attn_grad_one, up_grad_one
         )
@@ -1155,8 +1158,8 @@
         grads = gather(low)
         attn_grad_one = scatter_mp(attn_grad_one)
         up, up_other, down, down_other, feed_bias = halves
-        (up,) = core_sum_up(up, swap_core(hold(up_other, low)))
-        ready = stamp(*grads[1:], in_hbm(up))
+        (up,) = core_sum_up(up, swap_core(hold(up_other, total)))
+        ready = stamp(*grads[1:], kept=[up])
         parts, d_rows, grads = attn_half_back(grads, kept_attn_zero, ready, attn_grad_one)
         up_grad_zero = scatter_mp(hold(up, ready))
         own, other = attn_weights(
@@ -1169,19 +1172,18 @@
             feed_bias,
         )
         attn_parts = split_attn(place, own, swap_core(other))
-        down_parts = split_down(place, down, swap_core(hold(down_other, low)))
-        parts = scatter(parts[:1] + [hold(part, attn_parts[1]) for part in parts[1:]])
+        down_parts = split_down(place, down, swap_core(hold(down_other, total)))
+        parts = scatter(parts[:1] + [hold(part, own) for part in parts[1:]])
 
         def scatter_direct(parts, *after):
             moved = [move(hold(part, *after)) for move, part in zip(swap_z, parts[1:])]
             total = sum((part.astype(F32) for part in moved), parts[0].astype(F32))
             return total.astype(BF16), stamp(*moved)
 
-        down_grad_zero, down_there = scatter_direct(down_parts, up_grad_zero)
-        attn_grad_zero, attn_there = scatter_direct(attn_parts, down_there)
         (grad_zero,) = last_sum(*parts, total)
-
-        def exchange(zero, one, *after):
+        down_grad_zero, _ = scatter_direct(down_parts, up_grad_zero)
+        attn_grad_zero, attn_there = scatter_direct(attn_parts, up_grad_zero)
+        def exchange(zero, one, *after, last=False):
             if replicas > 4:
                 groups = [[low + 4 * high for high in range(replicas // 4)] for low in range(4)]
                 zero, one = lax.psum((zero, one), "dp", axis_index_groups=groups)
@@ -1190,16 +1192,17 @@
             if after:
                 mine, theirs = hold(mine, *after), hold(theirs, *after)
             pieces = [mine, swap_y(theirs), swap_x(mine), swap_xy(theirs)]
-            return pieces + [swap_core(piece) for piece in pieces]
-
-        moved = to_layers(hold(grad_zero, attn_there), grad_one)
-        (section_input_grads,) = finish_grads(place, *moved)
+            own = hold(mine, stamp(pieces[1])) if last else mine
+            return pieces + [swap_core(piece) for piece in [own] + pieces[1:]]
+
         ups = exchange(up_grad_zero, up_grad_one, grad_zero)
         (g_up,) = finish_up(place, *ups)
         downs = exchange(down_grad_zero, down_grad_one)
         (g_down,) = finish_down(place, *downs)
-        attns = exchange(attn_grad_zero, attn_grad_one)
+        attns = exchange(attn_grad_zero, attn_grad_one, last=True)
         g_query, g_key, g_value, g_out, g_b_query, g_b_value, g_b_up, *vectors = finish_attn(place, *attns)
+        moved = to_layers(hold(grad_zero, attn_there), grad_one)
+        (section_input_grads,) = finish_grads(place, *moved, g_query)
         return (
             section_outputs,
             section_input_grads,

time: 552 us -> 535 us (0.969)
  the two profiles are of different devices: /device:TPU:5 before, /device:TPU:0 now
where the time goes in v5:
time: 535 us; the launch traced here: 526 us
  waiting for transfers between devices  198 us (37%)
  Pallas kernels  150 us (28%)
  starting transfers between devices  139 us (26%)
  between operations  16.1 us (3%)
  local copies, waits for them, and re-layouts  14.7 us (3%)
  other arithmetic  7.19 us (1%)
    ppermute x99, waiting for transfers between devices, move(): return lax.ppermute(values, AXES, pairs)  194 us
    pallas_call x35, Pallas kernels, run(): pl.pallas_call(partial(body, after), name=name, in_specs=in_specs + [ANY...  142 us
    ppermute x99, starting transfers between devices, move(): return lax.ppermute(values, AXES, pairs)  139 us
    unnamed x95, local copies, waits for them, and re-layouts  11.5 us
  transfers between devices with their start and end apart: 108, of which 52 were waited for; matrix products, arithmetic and copies ran while one was open for 2% of the time, Pallas kernels for 25%

profile of v5, /device:TPU:0, one launch (start us, length us, event | category | flops | bytes accessed | tf_op | source)
XLA Modules:
  0.0 526.1 jit_solution(14246205359665464816)
XLA Ops:
  14.4 6.3 %collective-permute-start.4 = (s32[2,1,512]{2,1,0:T(1,128)S(1)}, s32[2,1,512]{2,1,0:T(1,128)S(1)}, u32[]{:S(2)}, u32[]{:S(2)}) collective-permute-start(s32[2,1,512]{2,1,0:T(1,128)S(1)} %copy-done.46), channel_id=1, source_target_pairs={{0,16},{1,17},{2,18},{3,19},{4,20},{5,21},{6,22},{7,23},{8,24},{9,... | collective-permute-start | bytes 12296 | tf_op jit(solution)/shard_map/ppermute | solution.py:932
  25.5 7.1 %collective-permute-start.1 = (bf16[128,1024]{1,0:T(8,128)(2,1)}, bf16[128,1024]{1,0:T(8,128)(2,1)S(1)}, u32[]{:S(2)}, u32[]{:S(2)}) collective-permute-start(bf16[128,1024]{1,0:T(8,128)(2,1)} %copy-done.2), channel_id=1, source_target_pairs={{0,4},{1,5},{2,6},{3,7},{4,0},{5,1},{6,2},{7,3},{8,12},{9,13},{10,... | collective-permute-start | bytes 786440 | tf_op jit(solution)/shard_map/ppermute | solution.py:932
  50.7 10.4 %collective-permute-done.13 = bf16[256,1024]{1,0:T(8,128)(2,1)S(1)} collective-permute-done((bf16[256,1024]{1,0:T(8,128)(2,1)}, bf16[256,1024]{1,0:T(8,128)(2,1)S(1)}, u32[]{:S(2)}, u32[]{:S(2)}) %collective-permute-start.13) | collective-permute-done | bytes 524320 | tf_op jit(solution)/shard_map/ppermute | solution.py:932
  68.1 8.4 %attention.2 = (f32[128,1024]{1,0:T(8,128)S(1)}, bf16[128,1024]{1,0:T(8,128)(2,1)S(1)}, bf16[128,1024]{1,0:T(8,128)(2,1)S(1)}, bf16[128,1024]{1,0:T(8,128)(2,1)S...) custom-call(bf16[128,1024]{1,0:T(8,128)(2,1)S(1)} %copy-done.3, ...), custom_call_target="tpu_custom_call" | custom-call | tf_op jit(solution)/shard_map/attention/pallas_call | solution.py:172
  95.7 8.4 %collective-permute-done.15.refs_2_ = bf16[128,1024]{1,0:T(8,128)(2,1)S(1)} collective-permute-done((bf16[128,1024]{1,0:T(8,128)(2,1)S(1)}, bf16[128,1024]{1,0:T(8,128)(2,1)S(1)}, u32[]{:S(2)}, u32[]{:S(2)}) %collective-permute-start.15) | collective-permute-done | bytes 262176 | tf_op jit(solution)/shard_map/ppermute | solution.py:932
  117.6 6.3 %feed.2 = (f32[128,1024]{1,0:T(8,128)S(1)}, bf16[128,1024]{1,0:T(8,128)(2,1)S(1)}, bf16[128,1024]{1,0:T(8,128)(2,1)S(1)}, bf16[128,1024]{1,0:T(8,128)(2,1)S(1)},...) custom-call(bf16[128,1024]{1,0:T(8,128)(2,1)} %get-tuple-element.151, ...), custom_call_target="tpu_custom_call" | custom-call | tf_op jit(solution)/shard_map/feed/pallas_call | solution.py:172
  145.1 5.2 collective-permute-done.22.refs_1_
  157.1 8.4 %attention.3 = (f32[128,1024]{1,0:T(8,128)S(1)}, bf16[128,1024]{1,0:T(8,128)(2,1)S(1)}, bf16[128,1024]{1,0:T(8,128)(2,1)S(1)}, bf16[128,1024]{1,0:T(8,128)(2,1)S...) custom-call(bf16[128,1024]{1,0:T(8,128)(2,1)S(1)} %get-tuple-element, ...), custom_call_target="tpu_custom_call" | custom-call | tf_op jit(solution)/shard_map/attention/pallas_call | solution.py:172
  199.7 6.2 %feed.3 = (f32[128,1024]{1,0:T(8,128)S(1)}, bf16[128,1024]{1,0:T(8,128)(2,1)S(1)}, bf16[128,1024]{1,0:T(8,128)(2,1)S(1)}, bf16[128,1024]{1,0:T(8,128)(2,1)S(1)},...) custom-call(bf16[128,1024]{1,0:T(8,128)(2,1)S(1)} %copy-done.26, ...), custom_call_target="tpu_custom_call" | custom-call | tf_op jit(solution)/shard_map/feed/pallas_call | solution.py:172
  214.3 6.8 %collective-permute-done.35.refs_2_ = bf16[128,1024]{1,0:T(8,128)(2,1)S(1)} collective-permute-done((bf16[128,1024]{1,0:T(8,128)(2,1)S(1)}, bf16[128,1024]{1,0:T(8,128)(2,1)S(1)}, u32[]{:S(2)}, u32[]{:S(2)}) %collective-permute-start.35) | collective-permute-done | bytes 262176 | tf_op jit(solution)/shard_map/ppermute | solution.py:932
  234.5 10.7 %collective-permute-start.38 = (bf16[128,1024]{1,0:T(8,128)(2,1)S(1)}, bf16[128,1024]{1,0:T(8,128)(2,1)S(1)}, u32[]{:S(2)}, u32[]{:S(2)}) collective-permute-start(bf16[128,1024]{1,0:T(8,128)(2,1)S(1)} %get-tuple-element.283), channel_id=1, source_target_pairs={{0,4},{1,21},{2,2},{3,19},{4,5},{5,22},{6,3},{7,16},{8,12},{9,29},... | collective-permute-start | bytes 786440 | tf_op jit(solution)/shard_map/ppermute | solution.py:932
  245.2 6.0 %feed_back.2 = (f32[128,1024]{1,0:T(8,128)S(1)}, bf16[128,1024]{1,0:T(8,128)(2,1)S(1)}, bf16[128,1024]{1,0:T(8,128)(2,1)S(1)}, bf16[128,1024]{1,0:T(8,128)(2,1)S...) custom-call(bf16[128,1024]{1,0:T(8,128)(2,1)S(1)} %get-tuple-element.177.refs_0_, ...), custom_call_target="tpu_custom_call" | custom-call | tf_op jit(solution)/shard_map/feed_back/pallas_call | solution.py:172
  251.3 10.6 %collective-permute-start.43 = (bf16[128,1024]{1,0:T(8,128)(2,1)S(1)}, bf16[128,1024]{1,0:T(8,128)(2,1)S(1)}, u32[]{:S(2)}, u32[]{:S(2)}) collective-permute-start(bf16[128,1024]{1,0:T(8,128)(2,1)S(1)} %get-tuple-element.182), channel_id=1, source_target_pairs={{0,4},{1,5},{2,6},{3,7},{4,0},{5,1},{6,2},{7,3},{8,12},{9,13},{10,... | collective-permute-start | bytes 786440 | tf_op jit(solution)/shard_map/ppermute | solution.py:932
  265.3 6.4 %feed_weights.2 = (bf16[4,128,1024]{2,1,0:T(8,128)(2,1)}, bf16[4,128,1024]{2,1,0:T(8,128)(2,1)}, bf16[4,128,1024]{2,1,0:T(8,128)(2,1)}, bf16[4,128,1024]{2,1,0:T(8,128)(2,1)}, f32[8,1024]{1,0:T(8,128)}) custom-call(bf16[512,1024]{1,0:T(8,128)(2,1)} %get-tuple-element.187.refs_0_, bf16[512,1024]{1,0:T(8,128)(2,1)} %get-tuple-element.188.refs_1_, ...), custom_call_target="tpu_custom_call" | custom-call | tf_op jit(solution)/shard_map/feed_weights/pallas_call | solution.py:172
  295.1 9.8 %attention_back.2 = (f32[128,1024]{1,0:T(8,128)S(1)}, bf16[128,1024]{1,0:T(8,128)(2,1)S(1)}, bf16[128,1024]{1,0:T(8,128)(2,1)S(1)}, bf16[128,1024]{1,0:T(8,128)(...) custom-call(bf16[128,1024]{1,0:T(8,128)(2,1)S(1)} %get-tuple-element.192.refs_0_, ...), custom_call_target="tpu_custom_call" | custom-call | tf_op jit(solution)/shard_map/attention_back/pallas_call | solution.py:172
  337.1 6.1 %feed_back.3 = (f32[128,1024]{1,0:T(8,128)S(1)}, bf16[128,1024]{1,0:T(8,128)(2,1)S(1)}, bf16[128,1024]{1,0:T(8,128)(2,1)S(1)}, bf16[128,1024]{1,0:T(8,128)(2,1)S...) custom-call(bf16[128,1024]{1,0:T(8,128)(2,1)S(1)} %get-tuple-element.214.refs_0_, ...), custom_call_target="tpu_custom_call" | custom-call | tf_op jit(solution)/shard_map/feed_back/pallas_call | solution.py:172
  346.8 6.3 %feed_weights.3 = (bf16[4,128,1024]{2,1,0:T(8,128)(2,1)}, bf16[4,128,1024]{2,1,0:T(8,128)(2,1)}, bf16[4,128,1024]{2,1,0:T(8,128)(2,1)}, bf16[4,128,1024]{2,1,0:T(8,128)(2,1)}, f32[8,1024]{1,0:T(8,128)}) custom-call(bf16[512,1024]{1,0:T(8,128)(2,1)} %get-tuple-element.225.refs_0_.refs_1_, bf16[512,1024]{1,0:T(8,128)(2,1)} %get-tuple-element.226.refs_1_, ...), custom_call_target="tpu_custom_call" | custom-call | tf_op jit(solution)/shard_map/feed_weights/pallas_call | solution.py:172
  370.7 5.1 collective-permute-done.63.refs_2_.refs_3_
  381.5 9.7 %attention_back.3 = (f32[128,1024]{1,0:T(8,128)S(1)}, bf16[128,1024]{1,0:T(8,128)(2,1)S(1)}, bf16[128,1024]{1,0:T(8,128)(2,1)S(1)}, bf16[128,1024]{1,0:T(8,128)(...) custom-call(bf16[128,1024]{1,0:T(8,128)(2,1)S(1)} %get-tuple-element.231.refs_0_, ...), custom_call_target="tpu_custom_call" | custom-call | tf_op jit(solution)/shard_map/attention_back/pallas_call | solution.py:172
  406.6 5.3 %collective-permute-done.66.refs_2_ = bf16[128,1024]{1,0:T(8,128)(2,1)} collective-permute-done((bf16[128,1024]{1,0:T(8,128)(2,1)}, bf16[128,1024]{1,0:T(8,128)(2,1)}, u32[]{:S(2)}, u32[]{:S(2)}) %collective-permute-start.66) | collective-permute-done | bytes 262176 | tf_op jit(solution)/shard_map/ppermute | solution.py:932
  430.6 7.0 %collective-permute-done.90 = bf16[128,1024]{1,0:T(8,128)(2,1)} collective-permute-done((bf16[128,1024]{1,0:T(8,128)(2,1)}, bf16[128,1024]{1,0:T(8,128)(2,1)}, u32[]{:S(2)}, u32[]{:S(2)}) %collective-permute-start.90) | collective-permute-done | bytes 262176 | tf_op jit(solution)/shard_map/ppermute | solution.py:932
  449.9 17.9 %collective-permute-done.70.refs_1_ = bf16[144,1024]{1,0:T(8,128)(2,1)S(1)} collective-permute-done((bf16[144,1024]{1,0:T(8,128)(2,1)}, bf16[144,1024]{1,0:T(8,128)(2,1)S(1)}, u32[]{:S(2)}, u32[]{:S(2)}) %collective-permute-start.70) | collective-permute-done | bytes 294944 | tf_op jit(solution)/shard_map/ppermute | solution.py:932
  489.0 5.7 %collective-permute-start.73 = (bf16[128,1024]{1,0:T(8,128)(2,1)S(1)}, bf16[128,1024]{1,0:T(8,128)(2,1)S(1)}, u32[]{:S(2)}, u32[]{:S(2)}) collective-permute-start(bf16[128,1024]{1,0:T(8,128)(2,1)S(1)} %get-tuple-element.281), channel_id=1, source_target_pairs={{0,4},{1,21},{2,2},{3,19},{4,5},{5,22},{6,3},{7,16},{8,12},{9,29},... | collective-permute-start | bytes 786440 | tf_op jit(solution)/shard_map/ppermute | solution.py:932
  510.8 6.9 %collective-permute-done.73.refs_2_ = bf16[128,1024]{1,0:T(8,128)(2,1)S(1)} collective-permute-done((bf16[128,1024]{1,0:T(8,128)(2,1)S(1)}, bf16[128,1024]{1,0:T(8,128)(2,1)S(1)}, u32[]{:S(2)}, u32[]{:S(2)}) %collective-permute-start.73) | collective-permute-done | bytes 262176 | tf_op jit(solution)/shard_map/ppermute | solution.py:932
  (385 shorter events, 322.8 us)
Async XLA Ops:
  7.2 57.8 %all-gather.11.cloned.1.call-start = ((), (), s32[]{:S(2)}) async-start(), calls=%async_computation.8 | async-start | bytes 1474560 | tf_op jit(solution)/shard_map/all_gather | solution.py:983
  25.5 87.7 %all-gather.13.cloned.1.call-start = ((), (), s32[]{:S(2)}) async-start(), calls=%async_computation.9 | async-start | bytes 1310720 | tf_op jit(solution)/shard_map/all_gather | solution.py:983
  63.8 77.4 %all-gather.15.cloned.1.call-start = ((), (), s32[]{:S(2)}) async-start(), calls=%async_computation.10 | async-start | bytes 1474560 | tf_op jit(solution)/shard_map/all_gather | solution.py:983
  64.9 120.6 %all-gather.17.cloned.1.call-start = ((), (), s32[]{:S(2)}) async-start(), calls=%async_computation.11 | async-start | bytes 1310720 | tf_op jit(solution)/shard_map/all_gather | solution.py:983
  80.1 23.9 %collective-permute-start.15 = (bf16[128,1024]{1,0:T(8,128)(2,1)S(1)}, bf16[128,1024]{1,0:T(8,128)(2,1)S(1)}, u32[]{:S(2)}, u32[]{:S(2)}) collective-permute-start(bf16[128,1024]{1,0:T(8,128)(2,1)S(1)} %get-tuple-element.287.refs_1_), channel_id=1, source_target_pairs={{0,1},{1,0},{2,3},{3,2},{4,5},{5,4},{6,7},{7,6},{8,9},{9,8},{10,11... | collective-permute-start | bytes 786440 | tf_op jit(solution)/shard_map/ppermute | solution.py:932
  80.1 27.2 %collective-permute-start.16 = (bf16[128,1024]{1,0:T(8,128)(2,1)S(1)}, bf16[128,1024]{1,0:T(8,128)(2,1)S(1)}, u32[]{:S(2)}, u32[]{:S(2)}) collective-permute-start(bf16[128,1024]{1,0:T(8,128)(2,1)S(1)} %get-tuple-element.287.refs_1_), channel_id=1, source_target_pairs={{0,2},{1,3},{2,0},{3,1},{4,6},{5,7},{6,4},{7,5},{8,10},{9,11},{10,... | collective-permute-start | bytes 786440 | tf_op jit(solution)/shard_map/ppermute | solution.py:932
  85.8 25.8 %collective-permute-start.17 = (bf16[128,1024]{1,0:T(8,128)(2,1)S(1)}, bf16[128,1024]{1,0:T(8,128)(2,1)S(1)}, u32[]{:S(2)}, u32[]{:S(2)}) collective-permute-start(bf16[128,1024]{1,0:T(8,128)(2,1)S(1)} %get-tuple-element.287.refs_1_), channel_id=1, source_target_pairs={{0,3},{1,2},{2,1},{3,0},{4,7},{5,6},{6,5},{7,4},{8,11},{9,10},{10,... | collective-permute-start | bytes 786440 | tf_op jit(solution)/shard_map/ppermute | solution.py:932
  107.3 88.8 %all-gather.19.cloned.1.call-start = ((), (), s32[]{:S(2)}) async-start(), calls=%async_computation.12 | async-start | bytes 1310720 | tf_op jit(solution)/shard_map/all_gather | solution.py:983
  141.3 195.8 %reduce-scatter.5.cloned.1.call-start = ((), (), s32[]{:S(2)}) async-start(), calls=%async_computation.4 | async-start | bytes 1310720 | tf_op jit(solution)/shard_map/reduce_scatter | solution.py:986
  233.8 38.0 %collective-permute-start.37 = (bf16[128,1024]{1,0:T(8,128)(2,1)S(1)}, bf16[128,1024]{1,0:T(8,128)(2,1)S(1)}, u32[]{:S(2)}, u32[]{:S(2)}) collective-permute-start(bf16[128,1024]{1,0:T(8,128)(2,1)S(1)} %get-tuple-element.284), channel_id=1, source_target_pairs={{0,0},{1,17},{2,6},{3,23},{4,1},{5,18},{6,7},{7,20},{8,8},{9,25},{... | collective-permute-start | bytes 786440 | tf_op jit(solution)/shard_map/ppermute | solution.py:932
  234.5 37.3 %collective-permute-start.38 = (bf16[128,1024]{1,0:T(8,128)(2,1)S(1)}, bf16[128,1024]{1,0:T(8,128)(2,1)S(1)}, u32[]{:S(2)}, u32[]{:S(2)}) collective-permute-start(bf16[128,1024]{1,0:T(8,128)(2,1)S(1)} %get-tuple-element.283), channel_id=1, source_target_pairs={{0,4},{1,21},{2,2},{3,19},{4,5},{5,22},{6,3},{7,16},{8,12},{9,29},... | collective-permute-start | bytes 786440 | tf_op jit(solution)/shard_map/ppermute | solution.py:932
  294.2 59.0 %reduce-scatter.7.cloned.1.call-start = ((), (), s32[]{:S(2)}) async-start(), calls=%async_computation.5 | async-start | bytes 1310720 | tf_op jit(solution)/shard_map/reduce_scatter | solution.py:986
  295.0 86.5 %reduce-scatter.9.cloned.1.call-start = ((), (), s32[]{:S(2)}) async-start(), calls=%async_computation.6 | async-start | bytes 1474560 | tf_op jit(solution)/shard_map/reduce_scatter | solution.py:986
  343.2 71.5 %reduce-scatter.11.cloned.1.call-start = ((), (), s32[]{:S(2)}) async-start(), calls=%async_computation.7 | async-start | bytes 1310720 | tf_op jit(solution)/shard_map/reduce_scatter | solution.py:986
  377.1 22.8 %collective-permute-start.88 = (bf16[4,128,1024]{2,1,0:T(8,128)(2,1)}, bf16[4,128,1024]{2,1,0:T(8,128)(2,1)S(1)}, u32[]{:S(2)}, u32[]{:S(2)}) collective-permute-start(bf16[4,128,1024]{2,1,0:T(8,128)(2,1)} %hold.50), channel_id=1, source_target_pairs={{0,8},{1,9},{2,10},{3,11},{4,12},{5,13},{6,14},{7,15},{8,0},{9,1},... | collective-permute-start | bytes 3145736 | tf_op jit(solution)/shard_map/ppermute | solution.py:932
  396.2 25.4 %collective-permute-start.68 = (bf16[4,144,1024]{2,1,0:T(8,128)(2,1)}, bf16[4,144,1024]{2,1,0:T(8,128)(2,1)S(1)}, u32[]{:S(2)}, u32[]{:S(2)}) collective-permute-start(bf16[4,144,1024]{2,1,0:T(8,128)(2,1)} %get-tuple-element.248), channel_id=1, source_target_pairs={{0,8},{1,9},{2,10},{3,11},{4,12},{5,13},{6,14},{7,15},{8,0},{9,1},... | collective-permute-start | bytes 3538952 | tf_op jit(solution)/shard_map/ppermute | solution.py:932
  416.0 21.7 %collective-permute-start.90 = (bf16[128,1024]{1,0:T(8,128)(2,1)}, bf16[128,1024]{1,0:T(8,128)(2,1)}, u32[]{:S(2)}, u32[]{:S(2)}) collective-permute-start(bf16[128,1024]{1,0:T(8,128)(2,1)} %hold.52), channel_id=1, source_target_pairs={{0,2},{1,3},{2,0},{3,1},{4,6},{5,7},{6,4},{7,5},{8,10},{9,11},{10,... | collective-permute-start | bytes 786440 | tf_op jit(solution)/shard_map/ppermute | solution.py:932
  421.6 22.5 %collective-permute-start.81 = (bf16[128,1024]{1,0:T(8,128)(2,1)}, bf16[128,1024]{1,0:T(8,128)(2,1)S(1)}, u32[]{:S(2)}, u32[]{:S(2)}) collective-permute-start(bf16[128,1024]{1,0:T(8,128)(2,1)} %hold.49), channel_id=1, source_target_pairs={{0,4},{1,5},{2,6},{3,7},{4,0},{5,1},{6,2},{7,3},{8,12},{9,13},{10,... | collective-permute-start | bytes 786440 | tf_op jit(solution)/shard_map/ppermute | solution.py:932
  439.2 28.6 %collective-permute-start.70 = (bf16[144,1024]{1,0:T(8,128)(2,1)}, bf16[144,1024]{1,0:T(8,128)(2,1)S(1)}, u32[]{:S(2)}, u32[]{:S(2)}) collective-permute-start(bf16[144,1024]{1,0:T(8,128)(2,1)} %hold.44), channel_id=1, source_target_pairs={{0,2},{1,3},{2,0},{3,1},{4,6},{5,7},{6,4},{7,5},{8,10},{9,11},{10,... | collective-permute-start | bytes 884744 | tf_op jit(solution)/shard_map/ppermute | solution.py:932
  444.1 23.8 %collective-permute-start.69 = (bf16[144,1024]{1,0:T(8,128)(2,1)}, bf16[144,1024]{1,0:T(8,128)(2,1)S(1)}, u32[]{:S(2)}, u32[]{:S(2)}) collective-permute-start(bf16[144,1024]{1,0:T(8,128)(2,1)} %hold.43), channel_id=1, source_target_pairs={{0,1},{1,0},{2,3},{3,2},{4,5},{5,4},{6,7},{7,6},{8,9},{9,8},{10,11... | collective-permute-start | bytes 884744 | tf_op jit(solution)/shard_map/ppermute | solution.py:932
  445.6 24.5 %collective-permute-start.92 = (bf16[128,1024]{1,0:T(8,128)(2,1)S(1)}, bf16[128,1024]{1,0:T(8,128)(2,1)}, u32[]{:S(2)}, u32[]{:S(2)}) collective-permute-start(bf16[128,1024]{1,0:T(8,128)(2,1)S(1)} %get-tuple-element.273), channel_id=1, source_target_pairs={{0,4},{1,5},{2,6},{3,7},{4,0},{5,1},{6,2},{7,3},{8,12},{9,13},{10,... | collective-permute-start | bytes 786440 | tf_op jit(solution)/shard_map/ppermute | solution.py:932
  446.3 23.9 %collective-permute-start.94 = (bf16[128,1024]{1,0:T(8,128)(2,1)S(1)}, bf16[128,1024]{1,0:T(8,128)(2,1)}, u32[]{:S(2)}, u32[]{:S(2)}) collective-permute-start(bf16[128,1024]{1,0:T(8,128)(2,1)S(1)} %get-tuple-element.273), channel_id=1, source_target_pairs={{0,20},{1,21},{2,22},{3,23},{4,16},{5,17},{6,18},{7,19},{8,28},{9,... | collective-permute-start | bytes 786440 | tf_op jit(solution)/shard_map/ppermute | solution.py:932
  488.4 22.5 %collective-permute-start.72 = (bf16[128,1024]{1,0:T(8,128)(2,1)S(1)}, bf16[128,1024]{1,0:T(8,128)(2,1)S(1)}, u32[]{:S(2)}, u32[]{:S(2)}) collective-permute-start(bf16[128,1024]{1,0:T(8,128)(2,1)S(1)} %get-tuple-element.282), channel_id=1, source_target_pairs={{0,0},{1,17},{2,6},{3,23},{4,1},{5,18},{6,7},{7,20},{8,8},{9,25},{... | collective-permute-start | bytes 786440 | tf_op jit(solution)/shard_map/ppermute | solution.py:932
  489.0 28.7 %collective-permute-start.73 = (bf16[128,1024]{1,0:T(8,128)(2,1)S(1)}, bf16[128,1024]{1,0:T(8,128)(2,1)S(1)}, u32[]{:S(2)}, u32[]{:S(2)}) collective-permute-start(bf16[128,1024]{1,0:T(8,128)(2,1)S(1)} %get-tuple-element.281), channel_id=1, source_target_pairs={{0,4},{1,21},{2,2},{3,19},{4,5},{5,22},{6,3},{7,16},{8,12},{9,29},... | collective-permute-start | bytes 786440 | tf_op jit(solution)/shard_map/ppermute | solution.py:932
  (131 other events, 1256.2 us)
Sparse Core Ops, SparseCore 0:
  25.6 38.3 all-gather.10
  65.5 38.3 all-gather.12
  105.4 30.0 all-gather.14
  136.9 26.9 all-gather.16
  165.3 27.4 all-gather.18
  294.4 28.7 reduce-scatter.4
  325.5 25.7 reduce-scatter.6
  353.7 27.7 reduce-scatter.8
  384.4 25.8 reduce-scatter.10

commit v6 on v5

--- a/solution.py
+++ b/solution.py
@@ -358,9 +358,18 @@
     vectors[...] = sums(rounded.astype(F32), grad * flat, grad)
 
 
-def norm_two_back_kernel(upstream, vec, normed, inverse, total, low, vectors):
-    (gain,) = rows_of(vec, 5)
-    norm_back(upstream[...].astype(F32), gain, normed, inverse, total, low, vectors)
+def norm_two_both_kernel(own, r1, r2, r3, residual, upstream, vec, low, total, low_grad, vectors):
+    bias, gain, offset = rows_of(vec, 4, 5, 6)
+    hidden = residual[...].astype(F32) + received(own, r1, r2, r3) + bias
+    result, flat, scale = norm_forward(hidden, gain, offset)
+    low[...] = result.astype(BF16)
+    grad = upstream[...].astype(F32)
+    value = norm_backward(grad, flat, scale, gain)
+    rounded = value.astype(BF16)
+    low_grad[...] = rounded
+    total[...] = value
+    total.send()
+    vectors[...] = sums(rounded.astype(F32), grad * flat, grad)
 
 
 def norm_two_back_sum_kernel(
@@ -781,8 +790,8 @@
     for first, name in ((True, "norm_one"), (False, "norm_two"))
 )
 BACKS = [("h", WIDE_TOKEN), ("v", TOKEN), ("h", VECTORS)]
-norm_two_back = call(
-    norm_two_back_kernel, "norm_two_back", ["v", "v", TOKEN, ONE], BACKS
+norm_two_both = call(
+    norm_two_both_kernel, "norm_two_both", ["v"] * 7, [("v", TOKEN)] + BACKS
 )
 norm_two_back_sum = call(
     norm_two_back_sum_kernel,
@@ -1075,11 +1084,9 @@
             middle, low, normed, inverse = norm_one(*parts, share, vec)
             return middle, low, (whole, qkv, probs, mixed, normed, inverse, weights)
 
-        def feed_half(middle, spread, weights, vec):
-            *parts, active, slope, spread, up, down = feed_forward(*spread, *weights)
-            parts = scatter(parts)
-            _, result, normed, inverse = norm_two(*parts, middle, vec)
-            return result, (spread, active, slope, normed, inverse, up, down)
+        def feed_half(middle, spread, weights, vec, *after):
+            *parts, active, slope, spread, up, down = feed_forward(*spread, *weights, *after)
+            return scatter(parts), (spread, active, slope, up, down)
 
         vec_zero = attn_zero[0][0, 128:144]
         middle, low, kept_attn_zero = attn_half(share_in, whole_in, attn_zero, vec_zero)
@@ -1087,10 +1094,11 @@
         up_zero = hold(up_zero, kept_attn_zero[4])
         down_zero = hold(down_zero, stamp(*spread[1:]))
         feed_zero = (attn_zero[0], up_zero, swap_core(up_zero), down_zero, swap_core(down_zero))
-        first, kept_feed_zero = feed_half(middle, spread, feed_zero, vec_zero)
+        parts, kept_feed_zero = feed_half(middle, spread, feed_zero, vec_zero)
+        _, first, *kept_norm_zero = norm_two(*parts, middle, vec_zero)
 
         whole = gather(first)
-        attn_one = hold(attn_one, kept_feed_zero[3])
+        attn_one = hold(attn_one, kept_norm_zero[0])
         vec_one = attn_one[0, 128:144]
         attn_one = (attn_one, swap_core(attn_one))
         middle, low, kept_attn_one = attn_half(first, whole, attn_one, vec_one)
@@ -1100,10 +1108,11 @@
         feed_one = (attn_one[0], up_one, swap_core(up_one), down_one, swap_core(down_one))
         grad_which = which ^ zero_after(kept_attn_zero[1])
         share_grad = place_in(lax.dynamic_index_in_dim(cotangent, grad_which, 0, False))
-        second, kept_feed_one = feed_half(middle, spread, feed_one, vec_one)
+        parts, kept_feed_one = feed_half(middle, spread, feed_one, vec_one)
+        second, total, low, vec_two = norm_two_both(*parts, middle, share_grad, vec_one)
 
         def feed_half_back(low, kept, *after):
-            spread, active, slope, _, _, up, down = kept
+            spread, active, slope, up, down = kept
             grads = gather(low)
             *parts, d_hidden, grads = feed_backward(*grads, down, slope, up, *after)
             parts = scatter(parts)
@@ -1119,9 +1128,6 @@
             received = [swap_core(hold(other, start)) for other in (up_other, down_other)]
             return total(place, up, down, *received, *after)
 
-        total, low, vec_two = norm_two_back(
-            share_grad, vec_one, kept_feed_one[3], kept_feed_one[4]
-        )
         parts, halves, _ = feed_half_back(low, kept_feed_one)
         feed_bias = halves[4]
         outputs = to_layers(first, second)
@@ -1139,7 +1145,7 @@
             d_rows, kept_attn_one[3], kept_attn_one[0], grads, vec_first, vec_two, feed_bias
         )
         total, low, vec_two, grad_one = norm_two_back_sum(
-            *parts, vec_zero, total, kept_feed_zero[3], kept_feed_zero[4], own, section_outputs
+            *parts, vec_zero, total, *kept_norm_zero, own, section_outputs
         )
         (attn_grad_one,) = core_sum_attn(own, swap_core(hold(other, total)))
         parts, halves, d_hidden = feed_half_back(

time: 535 us -> 533 us (level)
    pallas_call x35 -> x34, Pallas kernels: 142 us -> 139 us  [run(): pl.pallas_call(partial(body, after), name=name, in_specs=in_specs + [ANY...]
    unnamed x95 -> x93, local copies, waits for them, and re-layouts: 11.5 us -> 11.5 us
  transfers between devices with their start and end apart: 108 -> 108, of which waited for: 52 -> 51; matrix products, arithmetic and copies ran while one was open for 2% -> 2% of each run, Pallas kernels for 25% -> 26%
where the time goes in v6:
time: 533 us; the launch traced here: 525 us
  waiting for transfers between devices  195 us (37%)
  Pallas kernels  148 us (28%)
  starting transfers between devices  143 us (27%)
  between operations  16.1 us (3%)
  local copies, waits for them, and re-layouts  15.6 us (3%)
  other arithmetic  7.21 us (1%)
    ppermute x99, waiting for transfers between devices, move(): return lax.ppermute(values, AXES, pairs)  191 us
    ppermute x99, starting transfers between devices, move(): return lax.ppermute(values, AXES, pairs)  142 us
    pallas_call x34, Pallas kernels, run(): pl.pallas_call(partial(body, after), name=name, in_specs=in_specs + [ANY...  139 us
    unnamed x93, local copies, waits for them, and re-layouts  11.5 us
  transfers between devices with their start and end apart: 108, of which 51 were waited for; matrix products, arithmetic and copies ran while one was open for 2% of the time, Pallas kernels for 26%

profile of v6, /device:TPU:0, one launch (start us, length us, event | category | flops | bytes accessed | tf_op | source)
XLA Modules:
  0.0 524.6 jit_solution(16807913760102468192)
XLA Ops:
  14.4 6.3 %collective-permute-start.4 = (s32[2,1,512]{2,1,0:T(1,128)S(1)}, s32[2,1,512]{2,1,0:T(1,128)S(1)}, u32[]{:S(2)}, u32[]{:S(2)}) collective-permute-start(s32[2,1,512]{2,1,0:T(1,128)S(1)} %copy-done.45), channel_id=1, source_target_pairs={{0,16},{1,17},{2,18},{3,19},{4,20},{5,21},{6,22},{7,23},{8,24},{9,... | collective-permute-start | bytes 12296 | tf_op jit(solution)/shard_map/ppermute | solution.py:941
  25.5 7.1 %collective-permute-start.1 = (bf16[128,1024]{1,0:T(8,128)(2,1)}, bf16[128,1024]{1,0:T(8,128)(2,1)S(1)}, u32[]{:S(2)}, u32[]{:S(2)}) collective-permute-start(bf16[128,1024]{1,0:T(8,128)(2,1)} %copy-done.2), channel_id=1, source_target_pairs={{0,4},{1,5},{2,6},{3,7},{4,0},{5,1},{6,2},{7,3},{8,12},{9,13},{10,... | collective-permute-start | bytes 786440 | tf_op jit(solution)/shard_map/ppermute | solution.py:941
  50.7 10.4 %collective-permute-done.13 = bf16[256,1024]{1,0:T(8,128)(2,1)S(1)} collective-permute-done((bf16[256,1024]{1,0:T(8,128)(2,1)}, bf16[256,1024]{1,0:T(8,128)(2,1)S(1)}, u32[]{:S(2)}, u32[]{:S(2)}) %collective-permute-start.13) | collective-permute-done | bytes 524320 | tf_op jit(solution)/shard_map/ppermute | solution.py:941
  68.1 8.4 %attention.2 = (f32[128,1024]{1,0:T(8,128)S(1)}, bf16[128,1024]{1,0:T(8,128)(2,1)S(1)}, bf16[128,1024]{1,0:T(8,128)(2,1)S(1)}, bf16[128,1024]{1,0:T(8,128)(2,1)S...) custom-call(bf16[128,1024]{1,0:T(8,128)(2,1)S(1)} %copy-done.3, ...), custom_call_target="tpu_custom_call" | custom-call | tf_op jit(solution)/shard_map/attention/pallas_call | solution.py:172
  95.7 8.3 %collective-permute-done.15.refs_2_ = bf16[128,1024]{1,0:T(8,128)(2,1)S(1)} collective-permute-done((bf16[128,1024]{1,0:T(8,128)(2,1)S(1)}, bf16[128,1024]{1,0:T(8,128)(2,1)S(1)}, u32[]{:S(2)}, u32[]{:S(2)}) %collective-permute-start.15) | collective-permute-done | bytes 262176 | tf_op jit(solution)/shard_map/ppermute | solution.py:941
  117.6 6.3 %feed.2 = (f32[128,1024]{1,0:T(8,128)S(1)}, bf16[128,1024]{1,0:T(8,128)(2,1)S(1)}, bf16[128,1024]{1,0:T(8,128)(2,1)S(1)}, bf16[128,1024]{1,0:T(8,128)(2,1)S(1)},...) custom-call(bf16[128,1024]{1,0:T(8,128)(2,1)} %get-tuple-element.149, ...), custom_call_target="tpu_custom_call" | custom-call | tf_op jit(solution)/shard_map/feed/pallas_call | solution.py:172
  157.1 8.4 %attention.3 = (f32[128,1024]{1,0:T(8,128)S(1)}, bf16[128,1024]{1,0:T(8,128)(2,1)S(1)}, bf16[128,1024]{1,0:T(8,128)(2,1)S(1)}, bf16[128,1024]{1,0:T(8,128)(2,1)S...) custom-call(bf16[128,1024]{1,0:T(8,128)(2,1)S(1)} %get-tuple-element, ...), custom_call_target="tpu_custom_call" | custom-call | tf_op jit(solution)/shard_map/attention/pallas_call | solution.py:172
  199.7 6.2 %feed.3 = (f32[128,1024]{1,0:T(8,128)S(1)}, bf16[128,1024]{1,0:T(8,128)(2,1)S(1)}, bf16[128,1024]{1,0:T(8,128)(2,1)S(1)}, bf16[128,1024]{1,0:T(8,128)(2,1)S(1)},...) custom-call(bf16[128,1024]{1,0:T(8,128)(2,1)S(1)} %copy-done.26, ...), custom_call_target="tpu_custom_call" | custom-call | tf_op jit(solution)/shard_map/feed/pallas_call | solution.py:172
  206.0 9.6 %collective-permute-start.34 = (bf16[128,1024]{1,0:T(8,128)(2,1)S(1)}, bf16[128,1024]{1,0:T(8,128)(2,1)S(1)}, u32[]{:S(2)}, u32[]{:S(2)}) collective-permute-start(bf16[128,1024]{1,0:T(8,128)(2,1)S(1)} %get-tuple-element.167), channel_id=1, source_target_pairs={{0,4},{1,5},{2,6},{3,7},{4,0},{5,1},{6,2},{7,3},{8,12},{9,13},{10,... | collective-permute-start | bytes 786440 | tf_op jit(solution)/shard_map/ppermute | solution.py:941
  234.8 6.5 %collective-permute-start.39 = (bf16[128,1024]{1,0:T(8,128)(2,1)S(1)}, bf16[128,1024]{1,0:T(8,128)(2,1)S(1)}, u32[]{:S(2)}, u32[]{:S(2)}) collective-permute-start(bf16[128,1024]{1,0:T(8,128)(2,1)S(1)} %get-tuple-element.279), channel_id=1, source_target_pairs={{0,4},{1,21},{2,2},{3,19},{4,5},{5,22},{6,3},{7,16},{8,12},{9,29},... | collective-permute-start | bytes 786440 | tf_op jit(solution)/shard_map/ppermute | solution.py:941
  245.0 6.0 %feed_back.2 = (f32[128,1024]{1,0:T(8,128)S(1)}, bf16[128,1024]{1,0:T(8,128)(2,1)S(1)}, bf16[128,1024]{1,0:T(8,128)(2,1)S(1)}, bf16[128,1024]{1,0:T(8,128)(2,1)S...) custom-call(bf16[128,1024]{1,0:T(8,128)(2,1)S(1)} %get-tuple-element.173.refs_0_, ...), custom_call_target="tpu_custom_call" | custom-call | tf_op jit(solution)/shard_map/feed_back/pallas_call | solution.py:172
  251.0 9.6 %collective-permute-start.43 = (bf16[128,1024]{1,0:T(8,128)(2,1)S(1)}, bf16[128,1024]{1,0:T(8,128)(2,1)S(1)}, u32[]{:S(2)}, u32[]{:S(2)}) collective-permute-start(bf16[128,1024]{1,0:T(8,128)(2,1)S(1)} %get-tuple-element.178), channel_id=1, source_target_pairs={{0,4},{1,5},{2,6},{3,7},{4,0},{5,1},{6,2},{7,3},{8,12},{9,13},{10,... | collective-permute-start | bytes 786440 | tf_op jit(solution)/shard_map/ppermute | solution.py:941
  264.1 6.4 %feed_weights.2 = (bf16[4,128,1024]{2,1,0:T(8,128)(2,1)}, bf16[4,128,1024]{2,1,0:T(8,128)(2,1)}, bf16[4,128,1024]{2,1,0:T(8,128)(2,1)}, bf16[4,128,1024]{2,1,0:T(8,128)(2,1)}, f32[8,1024]{1,0:T(8,128)}) custom-call(bf16[512,1024]{1,0:T(8,128)(2,1)} %get-tuple-element.183.refs_0_, bf16[512,1024]{1,0:T(8,128)(2,1)} %get-tuple-element.184.refs_1_, ...), custom_call_target="tpu_custom_call" | custom-call | tf_op jit(solution)/shard_map/feed_weights/pallas_call | solution.py:172
  286.5 5.5 %collective-permute-done.48.refs_2_.refs_3_ = bf16[128,1024]{1,0:T(8,128)(2,1)S(1)} collective-permute-done((bf16[128,1024]{1,0:T(8,128)(2,1)S(1)}, bf16[128,1024]{1,0:T(8,128)(2,1)S(1)}, u32[]{:S(2)}, u32[]{:S(2)}) %collective-permute-start.48) | collective-permute-done | bytes 262176 | tf_op jit(solution)/shard_map/ppermute | solution.py:941
  294.1 9.8 %attention_back.2 = (f32[128,1024]{1,0:T(8,128)S(1)}, bf16[128,1024]{1,0:T(8,128)(2,1)S(1)}, bf16[128,1024]{1,0:T(8,128)(2,1)S(1)}, bf16[128,1024]{1,0:T(8,128)(...) custom-call(bf16[128,1024]{1,0:T(8,128)(2,1)S(1)} %get-tuple-element.188.refs_0_, ...), custom_call_target="tpu_custom_call" | custom-call | tf_op jit(solution)/shard_map/attention_back/pallas_call | solution.py:172
  330.2 6.0 %collective-permute-done.56.refs_3_ = bf16[128,1024]{1,0:T(8,128)(2,1)S(1)} collective-permute-done((bf16[128,1024]{1,0:T(8,128)(2,1)S(1)}, bf16[128,1024]{1,0:T(8,128)(2,1)S(1)}, u32[]{:S(2)}, u32[]{:S(2)}) %collective-permute-start.56) | collective-permute-done | bytes 262176 | tf_op jit(solution)/shard_map/ppermute | solution.py:941
  336.2 6.1 %feed_back.3 = (f32[128,1024]{1,0:T(8,128)S(1)}, bf16[128,1024]{1,0:T(8,128)(2,1)S(1)}, bf16[128,1024]{1,0:T(8,128)(2,1)S(1)}, bf16[128,1024]{1,0:T(8,128)(2,1)S...) custom-call(bf16[128,1024]{1,0:T(8,128)(2,1)S(1)} %get-tuple-element.210.refs_0_, ...), custom_call_target="tpu_custom_call" | custom-call | tf_op jit(solution)/shard_map/feed_back/pallas_call | solution.py:172
  345.9 6.3 %feed_weights.3 = (bf16[4,128,1024]{2,1,0:T(8,128)(2,1)}, bf16[4,128,1024]{2,1,0:T(8,128)(2,1)}, bf16[4,128,1024]{2,1,0:T(8,128)(2,1)}, bf16[4,128,1024]{2,1,0:T(8,128)(2,1)}, f32[8,1024]{1,0:T(8,128)}) custom-call(bf16[512,1024]{1,0:T(8,128)(2,1)} %get-tuple-element.221.refs_0_.refs_1_, bf16[512,1024]{1,0:T(8,128)(2,1)} %get-tuple-element.222.refs_1_, ...), custom_call_target="tpu_custom_call" | custom-call | tf_op jit(solution)/shard_map/feed_weights/pallas_call | solution.py:172
  368.8 6.0 %collective-permute-done.63.refs_2_.refs_3_ = bf16[128,1024]{1,0:T(8,128)(2,1)S(1)} collective-permute-done((bf16[128,1024]{1,0:T(8,128)(2,1)S(1)}, bf16[128,1024]{1,0:T(8,128)(2,1)S(1)}, u32[]{:S(2)}, u32[]{:S(2)}) %collective-permute-start.63) | collective-permute-done | bytes 262176 | tf_op jit(solution)/shard_map/ppermute | solution.py:941
  380.4 9.7 %attention_back.3 = (f32[128,1024]{1,0:T(8,128)S(1)}, bf16[128,1024]{1,0:T(8,128)(2,1)S(1)}, bf16[128,1024]{1,0:T(8,128)(2,1)S(1)}, bf16[128,1024]{1,0:T(8,128)(...) custom-call(bf16[128,1024]{1,0:T(8,128)(2,1)S(1)} %get-tuple-element.227.refs_0_, ...), custom_call_target="tpu_custom_call" | custom-call | tf_op jit(solution)/shard_map/attention_back/pallas_call | solution.py:172
  429.5 6.0 %collective-permute-done.90 = bf16[128,1024]{1,0:T(8,128)(2,1)} collective-permute-done((bf16[128,1024]{1,0:T(8,128)(2,1)}, bf16[128,1024]{1,0:T(8,128)(2,1)}, u32[]{:S(2)}, u32[]{:S(2)}) %collective-permute-start.90) | collective-permute-done | bytes 262176 | tf_op jit(solution)/shard_map/ppermute | solution.py:941
  448.8 16.9 %collective-permute-done.70.refs_1_ = bf16[144,1024]{1,0:T(8,128)(2,1)S(1)} collective-permute-done((bf16[144,1024]{1,0:T(8,128)(2,1)}, bf16[144,1024]{1,0:T(8,128)(2,1)S(1)}, u32[]{:S(2)}, u32[]{:S(2)}) %collective-permute-start.70) | collective-permute-done | bytes 294944 | tf_op jit(solution)/shard_map/ppermute | solution.py:941
  486.9 5.7 %collective-permute-start.73 = (bf16[128,1024]{1,0:T(8,128)(2,1)S(1)}, bf16[128,1024]{1,0:T(8,128)(2,1)S(1)}, u32[]{:S(2)}, u32[]{:S(2)}) collective-permute-start(bf16[128,1024]{1,0:T(8,128)(2,1)S(1)} %get-tuple-element.277), channel_id=1, source_target_pairs={{0,4},{1,21},{2,2},{3,19},{4,5},{5,22},{6,3},{7,16},{8,12},{9,29},... | collective-permute-start | bytes 786440 | tf_op jit(solution)/shard_map/ppermute | solution.py:941
  508.7 7.5 %collective-permute-done.73.refs_2_ = bf16[128,1024]{1,0:T(8,128)(2,1)S(1)} collective-permute-done((bf16[128,1024]{1,0:T(8,128)(2,1)S(1)}, bf16[128,1024]{1,0:T(8,128)(2,1)S(1)}, u32[]{:S(2)}, u32[]{:S(2)}) %collective-permute-start.73) | collective-permute-done | bytes 262176 | tf_op jit(solution)/shard_map/ppermute | solution.py:941
  (382 shorter events, 323.2 us)
Async XLA Ops:
  7.2 57.8 %all-gather.11.cloned.1.call-start = ((), (), s32[]{:S(2)}) async-start(), calls=%async_computation.8 | async-start | bytes 1474560 | tf_op jit(solution)/shard_map/all_gather | solution.py:992
  25.5 87.7 %all-gather.13.cloned.1.call-start = ((), (), s32[]{:S(2)}) async-start(), calls=%async_computation.9 | async-start | bytes 1310720 | tf_op jit(solution)/shard_map/all_gather | solution.py:992
  63.8 77.3 %all-gather.15.cloned.1.call-start = ((), (), s32[]{:S(2)}) async-start(), calls=%async_computation.10 | async-start | bytes 1474560 | tf_op jit(solution)/shard_map/all_gather | solution.py:992
  64.9 120.6 %all-gather.17.cloned.1.call-start = ((), (), s32[]{:S(2)}) async-start(), calls=%async_computation.11 | async-start | bytes 1310720 | tf_op jit(solution)/shard_map/all_gather | solution.py:992
  80.1 23.9 %collective-permute-start.15 = (bf16[128,1024]{1,0:T(8,128)(2,1)S(1)}, bf16[128,1024]{1,0:T(8,128)(2,1)S(1)}, u32[]{:S(2)}, u32[]{:S(2)}) collective-permute-start(bf16[128,1024]{1,0:T(8,128)(2,1)S(1)} %get-tuple-element.283.refs_1_), channel_id=1, source_target_pairs={{0,1},{1,0},{2,3},{3,2},{4,5},{5,4},{6,7},{7,6},{8,9},{9,8},{10,11... | collective-permute-start | bytes 786440 | tf_op jit(solution)/shard_map/ppermute | solution.py:941
  80.1 27.2 %collective-permute-start.16 = (bf16[128,1024]{1,0:T(8,128)(2,1)S(1)}, bf16[128,1024]{1,0:T(8,128)(2,1)S(1)}, u32[]{:S(2)}, u32[]{:S(2)}) collective-permute-start(bf16[128,1024]{1,0:T(8,128)(2,1)S(1)} %get-tuple-element.283.refs_1_), channel_id=1, source_target_pairs={{0,2},{1,3},{2,0},{3,1},{4,6},{5,7},{6,4},{7,5},{8,10},{9,11},{10,... | collective-permute-start | bytes 786440 | tf_op jit(solution)/shard_map/ppermute | solution.py:941
  85.7 25.8 %collective-permute-start.17 = (bf16[128,1024]{1,0:T(8,128)(2,1)S(1)}, bf16[128,1024]{1,0:T(8,128)(2,1)S(1)}, u32[]{:S(2)}, u32[]{:S(2)}) collective-permute-start(bf16[128,1024]{1,0:T(8,128)(2,1)S(1)} %get-tuple-element.283.refs_1_), channel_id=1, source_target_pairs={{0,3},{1,2},{2,1},{3,0},{4,7},{5,6},{6,5},{7,4},{8,11},{9,10},{10,... | collective-permute-start | bytes 786440 | tf_op jit(solution)/shard_map/ppermute | solution.py:941
  107.3 88.7 %all-gather.19.cloned.1.call-start = ((), (), s32[]{:S(2)}) async-start(), calls=%async_computation.12 | async-start | bytes 1310720 | tf_op jit(solution)/shard_map/all_gather | solution.py:992
  141.2 194.9 %reduce-scatter.5.cloned.1.call-start = ((), (), s32[]{:S(2)}) async-start(), calls=%async_computation.4 | async-start | bytes 1310720 | tf_op jit(solution)/shard_map/reduce_scatter | solution.py:995
  234.1 36.4 %collective-permute-start.38 = (bf16[128,1024]{1,0:T(8,128)(2,1)S(1)}, bf16[128,1024]{1,0:T(8,128)(2,1)S(1)}, u32[]{:S(2)}, u32[]{:S(2)}) collective-permute-start(bf16[128,1024]{1,0:T(8,128)(2,1)S(1)} %get-tuple-element.280), channel_id=1, source_target_pairs={{0,0},{1,17},{2,6},{3,23},{4,1},{5,18},{6,7},{7,20},{8,8},{9,25},{... | collective-permute-start | bytes 786440 | tf_op jit(solution)/shard_map/ppermute | solution.py:941
  234.8 35.7 %collective-permute-start.39 = (bf16[128,1024]{1,0:T(8,128)(2,1)S(1)}, bf16[128,1024]{1,0:T(8,128)(2,1)S(1)}, u32[]{:S(2)}, u32[]{:S(2)}) collective-permute-start(bf16[128,1024]{1,0:T(8,128)(2,1)S(1)} %get-tuple-element.279), channel_id=1, source_target_pairs={{0,4},{1,21},{2,2},{3,19},{4,5},{5,22},{6,3},{7,16},{8,12},{9,29},... | collective-permute-start | bytes 786440 | tf_op jit(solution)/shard_map/ppermute | solution.py:941
  293.3 58.9 %reduce-scatter.7.cloned.1.call-start = ((), (), s32[]{:S(2)}) async-start(), calls=%async_computation.5 | async-start | bytes 1310720 | tf_op jit(solution)/shard_map/reduce_scatter | solution.py:995
  294.0 86.4 %reduce-scatter.9.cloned.1.call-start = ((), (), s32[]{:S(2)}) async-start(), calls=%async_computation.6 | async-start | bytes 1474560 | tf_op jit(solution)/shard_map/reduce_scatter | solution.py:995
  342.3 71.4 %reduce-scatter.11.cloned.1.call-start = ((), (), s32[]{:S(2)}) async-start(), calls=%async_computation.7 | async-start | bytes 1310720 | tf_op jit(solution)/shard_map/reduce_scatter | solution.py:995
  376.0 22.7 %collective-permute-start.88 = (bf16[4,128,1024]{2,1,0:T(8,128)(2,1)}, bf16[4,128,1024]{2,1,0:T(8,128)(2,1)S(1)}, u32[]{:S(2)}, u32[]{:S(2)}) collective-permute-start(bf16[4,128,1024]{2,1,0:T(8,128)(2,1)} %hold.50), channel_id=1, source_target_pairs={{0,8},{1,9},{2,10},{3,11},{4,12},{5,13},{6,14},{7,15},{8,0},{9,1},... | collective-permute-start | bytes 3145736 | tf_op jit(solution)/shard_map/ppermute | solution.py:941
  395.1 25.4 %collective-permute-start.68 = (bf16[4,144,1024]{2,1,0:T(8,128)(2,1)}, bf16[4,144,1024]{2,1,0:T(8,128)(2,1)S(1)}, u32[]{:S(2)}, u32[]{:S(2)}) collective-permute-start(bf16[4,144,1024]{2,1,0:T(8,128)(2,1)} %get-tuple-element.244), channel_id=1, source_target_pairs={{0,8},{1,9},{2,10},{3,11},{4,12},{5,13},{6,14},{7,15},{8,0},{9,1},... | collective-permute-start | bytes 3538952 | tf_op jit(solution)/shard_map/ppermute | solution.py:941
  413.8 21.7 %collective-permute-start.90 = (bf16[128,1024]{1,0:T(8,128)(2,1)}, bf16[128,1024]{1,0:T(8,128)(2,1)}, u32[]{:S(2)}, u32[]{:S(2)}) collective-permute-start(bf16[128,1024]{1,0:T(8,128)(2,1)} %hold.52), channel_id=1, source_target_pairs={{0,2},{1,3},{2,0},{3,1},{4,6},{5,7},{6,4},{7,5},{8,10},{9,11},{10,... | collective-permute-start | bytes 786440 | tf_op jit(solution)/shard_map/ppermute | solution.py:941
  420.5 21.7 %collective-permute-start.81 = (bf16[128,1024]{1,0:T(8,128)(2,1)}, bf16[128,1024]{1,0:T(8,128)(2,1)S(1)}, u32[]{:S(2)}, u32[]{:S(2)}) collective-permute-start(bf16[128,1024]{1,0:T(8,128)(2,1)} %hold.49), channel_id=1, source_target_pairs={{0,4},{1,5},{2,6},{3,7},{4,0},{5,1},{6,2},{7,3},{8,12},{9,13},{10,... | collective-permute-start | bytes 786440 | tf_op jit(solution)/shard_map/ppermute | solution.py:941
  438.1 27.6 %collective-permute-start.70 = (bf16[144,1024]{1,0:T(8,128)(2,1)}, bf16[144,1024]{1,0:T(8,128)(2,1)S(1)}, u32[]{:S(2)}, u32[]{:S(2)}) collective-permute-start(bf16[144,1024]{1,0:T(8,128)(2,1)} %hold.44), channel_id=1, source_target_pairs={{0,2},{1,3},{2,0},{3,1},{4,6},{5,7},{6,4},{7,5},{8,10},{9,11},{10,... | collective-permute-start | bytes 884744 | tf_op jit(solution)/shard_map/ppermute | solution.py:941
  442.2 23.6 %collective-permute-start.69 = (bf16[144,1024]{1,0:T(8,128)(2,1)}, bf16[144,1024]{1,0:T(8,128)(2,1)S(1)}, u32[]{:S(2)}, u32[]{:S(2)}) collective-permute-start(bf16[144,1024]{1,0:T(8,128)(2,1)} %hold.43), channel_id=1, source_target_pairs={{0,1},{1,0},{2,3},{3,2},{4,5},{5,4},{6,7},{7,6},{8,9},{9,8},{10,11... | collective-permute-start | bytes 884744 | tf_op jit(solution)/shard_map/ppermute | solution.py:941
  443.7 24.8 %collective-permute-start.92 = (bf16[128,1024]{1,0:T(8,128)(2,1)S(1)}, bf16[128,1024]{1,0:T(8,128)(2,1)}, u32[]{:S(2)}, u32[]{:S(2)}) collective-permute-start(bf16[128,1024]{1,0:T(8,128)(2,1)S(1)} %get-tuple-element.269), channel_id=1, source_target_pairs={{0,4},{1,5},{2,6},{3,7},{4,0},{5,1},{6,2},{7,3},{8,12},{9,13},{10,... | collective-permute-start | bytes 786440 | tf_op jit(solution)/shard_map/ppermute | solution.py:941
  445.2 23.4 %collective-permute-start.94 = (bf16[128,1024]{1,0:T(8,128)(2,1)S(1)}, bf16[128,1024]{1,0:T(8,128)(2,1)}, u32[]{:S(2)}, u32[]{:S(2)}) collective-permute-start(bf16[128,1024]{1,0:T(8,128)(2,1)S(1)} %get-tuple-element.269), channel_id=1, source_target_pairs={{0,20},{1,21},{2,22},{3,23},{4,16},{5,17},{6,18},{7,19},{8,28},{9,... | collective-permute-start | bytes 786440 | tf_op jit(solution)/shard_map/ppermute | solution.py:941
  486.2 22.5 %collective-permute-start.72 = (bf16[128,1024]{1,0:T(8,128)(2,1)S(1)}, bf16[128,1024]{1,0:T(8,128)(2,1)S(1)}, u32[]{:S(2)}, u32[]{:S(2)}) collective-permute-start(bf16[128,1024]{1,0:T(8,128)(2,1)S(1)} %get-tuple-element.278), channel_id=1, source_target_pairs={{0,0},{1,17},{2,6},{3,23},{4,1},{5,18},{6,7},{7,20},{8,8},{9,25},{... | collective-permute-start | bytes 786440 | tf_op jit(solution)/shard_map/ppermute | solution.py:941
  486.9 29.3 %collective-permute-start.73 = (bf16[128,1024]{1,0:T(8,128)(2,1)S(1)}, bf16[128,1024]{1,0:T(8,128)(2,1)S(1)}, u32[]{:S(2)}, u32[]{:S(2)}) collective-permute-start(bf16[128,1024]{1,0:T(8,128)(2,1)S(1)} %get-tuple-element.277), channel_id=1, source_target_pairs={{0,4},{1,21},{2,2},{3,19},{4,5},{5,22},{6,3},{7,16},{8,12},{9,29},... | collective-permute-start | bytes 786440 | tf_op jit(solution)/shard_map/ppermute | solution.py:941
  (130 other events, 1235.0 us)
Sparse Core Ops, SparseCore 0:
  25.6 38.3 all-gather.10
  65.5 38.3 all-gather.12
  105.4 30.0 all-gather.14
  137.0 26.8 all-gather.16
  165.3 27.4 all-gather.18
  293.4 28.5 reduce-scatter.4
  324.4 25.7 reduce-scatter.6
  352.5 27.8 reduce-scatter.8
  383.3 25.8 reduce-scatter.10

commit v7 on v6

--- a/solution.py
+++ b/solution.py
@@ -1206,9 +1206,11 @@
         downs = exchange(down_grad_zero, down_grad_one)
         (g_down,) = finish_down(place, *downs)
         attns = exchange(attn_grad_zero, attn_grad_one, last=True)
-        g_query, g_key, g_value, g_out, g_b_query, g_b_value, g_b_up, *vectors = finish_attn(place, *attns)
         moved = to_layers(hold(grad_zero, attn_there), grad_one)
-        (section_input_grads,) = finish_grads(place, *moved, g_query)
+        (section_input_grads,) = finish_grads(place, *moved)
+        g_query, g_key, g_value, g_out, g_b_query, g_b_value, g_b_up, *vectors = finish_attn(
+            place, *attns, section_input_grads
+        )
         return (
             section_outputs,
             section_input_grads,

time: 533 us -> 539 us (1.011)
  starting transfers between devices: 143 us -> 150 us
    ppermute x99, starting transfers between devices: 142 us -> 150 us  [move(): return lax.ppermute(values, AXES, pairs)]
  transfers between devices with their start and end apart: 108 -> 108, of which waited for: 51 -> 49; matrix products, arithmetic and copies ran while one was open for 2% -> 2% of each run, Pallas kernels for 26% -> 25%
where the time goes in v7:
time: 539 us; the launch traced here: 530 us
  waiting for transfers between devices  190 us (35%)
  starting transfers between devices  150 us (28%)
  Pallas kernels  146 us (27%)
  local copies, waits for them, and re-layouts  19.3 us (4%)
  between operations  16.1 us (3%)
  other arithmetic  8.5 us (2%)
    ppermute x99, waiting for transfers between devices, move(): return lax.ppermute(values, AXES, pairs)  186 us
    ppermute x99, starting transfers between devices, move(): return lax.ppermute(values, AXES, pairs)  150 us
    pallas_call x34, Pallas kernels, run(): pl.pallas_call(partial(body, after), name=name, in_specs=in_specs + [ANY...  138 us
    unnamed x93, local copies, waits for them, and re-layouts  15.2 us
  transfers between devices with their start and end apart: 108, of which 49 were waited for; matrix products, arithmetic and copies ran while one was open for 2% of the time, Pallas kernels for 25%

profile of v7, /device:TPU:0, one launch (start us, length us, event | category | flops | bytes accessed | tf_op | source)
XLA Modules:
  0.0 530.4 jit_solution(10487165916170405410)
XLA Ops:
  14.4 6.3 %collective-permute-start.4 = (s32[2,1,512]{2,1,0:T(1,128)S(1)}, s32[2,1,512]{2,1,0:T(1,128)S(1)}, u32[]{:S(2)}, u32[]{:S(2)}) collective-permute-start(s32[2,1,512]{2,1,0:T(1,128)S(1)} %copy-done.45), channel_id=1, source_target_pairs={{0,16},{1,17},{2,18},{3,19},{4,20},{5,21},{6,22},{7,23},{8,24},{9,... | collective-permute-start | bytes 12296 | tf_op jit(solution)/shard_map/ppermute | solution.py:941
  25.5 7.1 %collective-permute-start.1 = (bf16[128,1024]{1,0:T(8,128)(2,1)}, bf16[128,1024]{1,0:T(8,128)(2,1)S(1)}, u32[]{:S(2)}, u32[]{:S(2)}) collective-permute-start(bf16[128,1024]{1,0:T(8,128)(2,1)} %copy-done.2), channel_id=1, source_target_pairs={{0,4},{1,5},{2,6},{3,7},{4,0},{5,1},{6,2},{7,3},{8,12},{9,13},{10,... | collective-permute-start | bytes 786440 | tf_op jit(solution)/shard_map/ppermute | solution.py:941
  50.7 10.4 %collective-permute-done.13 = bf16[256,1024]{1,0:T(8,128)(2,1)S(1)} collective-permute-done((bf16[256,1024]{1,0:T(8,128)(2,1)}, bf16[256,1024]{1,0:T(8,128)(2,1)S(1)}, u32[]{:S(2)}, u32[]{:S(2)}) %collective-permute-start.13) | collective-permute-done | bytes 524320 | tf_op jit(solution)/shard_map/ppermute | solution.py:941
  68.1 8.4 %attention.2 = (f32[128,1024]{1,0:T(8,128)S(1)}, bf16[128,1024]{1,0:T(8,128)(2,1)S(1)}, bf16[128,1024]{1,0:T(8,128)(2,1)S(1)}, bf16[128,1024]{1,0:T(8,128)(2,1)S...) custom-call(bf16[128,1024]{1,0:T(8,128)(2,1)S(1)} %copy-done.3, ...), custom_call_target="tpu_custom_call" | custom-call | tf_op jit(solution)/shard_map/attention/pallas_call | solution.py:172
  94.9 9.1 %collective-permute-done.15.refs_2_ = bf16[128,1024]{1,0:T(8,128)(2,1)S(1)} collective-permute-done((bf16[128,1024]{1,0:T(8,128)(2,1)S(1)}, bf16[128,1024]{1,0:T(8,128)(2,1)S(1)}, u32[]{:S(2)}, u32[]{:S(2)}) %collective-permute-start.15) | collective-permute-done | bytes 262176 | tf_op jit(solution)/shard_map/ppermute | solution.py:941
  117.6 6.3 %feed.2 = (f32[128,1024]{1,0:T(8,128)S(1)}, bf16[128,1024]{1,0:T(8,128)(2,1)S(1)}, bf16[128,1024]{1,0:T(8,128)(2,1)S(1)}, bf16[128,1024]{1,0:T(8,128)(2,1)S(1)},...) custom-call(bf16[128,1024]{1,0:T(8,128)(2,1)S(1)} %get-tuple-element, ...), custom_call_target="tpu_custom_call" | custom-call | tf_op jit(solution)/shard_map/feed/pallas_call | solution.py:172
  157.1 8.4 %attention.3 = (f32[128,1024]{1,0:T(8,128)S(1)}, bf16[128,1024]{1,0:T(8,128)(2,1)S(1)}, bf16[128,1024]{1,0:T(8,128)(2,1)S(1)}, bf16[128,1024]{1,0:T(8,128)(2,1)S...) custom-call(bf16[128,1024]{1,0:T(8,128)(2,1)S(1)} %get-tuple-element, ...), custom_call_target="tpu_custom_call" | custom-call | tf_op jit(solution)/shard_map/attention/pallas_call | solution.py:172
  200.7 6.2 %feed.3 = (f32[128,1024]{1,0:T(8,128)S(1)}, bf16[128,1024]{1,0:T(8,128)(2,1)S(1)}, bf16[128,1024]{1,0:T(8,128)(2,1)S(1)}, bf16[128,1024]{1,0:T(8,128)(2,1)S(1)},...) custom-call(bf16[128,1024]{1,0:T(8,128)(2,1)S(1)} %copy-done.22, ...), custom_call_target="tpu_custom_call" | custom-call | tf_op jit(solution)/shard_map/feed/pallas_call | solution.py:172
  207.0 9.5 %collective-permute-start.34 = (bf16[128,1024]{1,0:T(8,128)(2,1)S(1)}, bf16[128,1024]{1,0:T(8,128)(2,1)S(1)}, u32[]{:S(2)}, u32[]{:S(2)}) collective-permute-start(bf16[128,1024]{1,0:T(8,128)(2,1)S(1)} %get-tuple-element.167), channel_id=1, source_target_pairs={{0,4},{1,5},{2,6},{3,7},{4,0},{5,1},{6,2},{7,3},{8,12},{9,13},{10,... | collective-permute-start | bytes 786440 | tf_op jit(solution)/shard_map/ppermute | solution.py:941
  235.7 6.5 %collective-permute-start.39 = (bf16[128,1024]{1,0:T(8,128)(2,1)S(1)}, bf16[128,1024]{1,0:T(8,128)(2,1)S(1)}, u32[]{:S(2)}, u32[]{:S(2)}) collective-permute-start(bf16[128,1024]{1,0:T(8,128)(2,1)S(1)} %get-tuple-element.279), channel_id=1, source_target_pairs={{0,4},{1,21},{2,2},{3,19},{4,5},{5,22},{6,3},{7,16},{8,12},{9,29},... | collective-permute-start | bytes 786440 | tf_op jit(solution)/shard_map/ppermute | solution.py:941
  245.9 6.0 %feed_back.2 = (f32[128,1024]{1,0:T(8,128)S(1)}, bf16[128,1024]{1,0:T(8,128)(2,1)S(1)}, bf16[128,1024]{1,0:T(8,128)(2,1)S(1)}, bf16[128,1024]{1,0:T(8,128)(2,1)S...) custom-call(bf16[128,1024]{1,0:T(8,128)(2,1)S(1)} %get-tuple-element.173.refs_0_, ...), custom_call_target="tpu_custom_call" | custom-call | tf_op jit(solution)/shard_map/feed_back/pallas_call | solution.py:172
  251.9 9.7 %collective-permute-start.43 = (bf16[128,1024]{1,0:T(8,128)(2,1)S(1)}, bf16[128,1024]{1,0:T(8,128)(2,1)S(1)}, u32[]{:S(2)}, u32[]{:S(2)}) collective-permute-start(bf16[128,1024]{1,0:T(8,128)(2,1)S(1)} %get-tuple-element.178), channel_id=1, source_target_pairs={{0,4},{1,5},{2,6},{3,7},{4,0},{5,1},{6,2},{7,3},{8,12},{9,13},{10,... | collective-permute-start | bytes 786440 | tf_op jit(solution)/shard_map/ppermute | solution.py:941
  264.9 6.4 %feed_weights.2 = (bf16[4,128,1024]{2,1,0:T(8,128)(2,1)}, bf16[4,128,1024]{2,1,0:T(8,128)(2,1)}, bf16[4,128,1024]{2,1,0:T(8,128)(2,1)}, bf16[4,128,1024]{2,1,0:T(8,128)(2,1)}, f32[8,1024]{1,0:T(8,128)}) custom-call(bf16[512,1024]{1,0:T(8,128)(2,1)} %get-tuple-element.183.refs_0_, bf16[512,1024]{1,0:T(8,128)(2,1)} %get-tuple-element.184.refs_1_, ...), custom_call_target="tpu_custom_call" | custom-call | tf_op jit(solution)/shard_map/feed_weights/pallas_call | solution.py:172
  287.5 5.5 %collective-permute-done.48.refs_2_.refs_3_ = bf16[128,1024]{1,0:T(8,128)(2,1)S(1)} collective-permute-done((bf16[128,1024]{1,0:T(8,128)(2,1)S(1)}, bf16[128,1024]{1,0:T(8,128)(2,1)S(1)}, u32[]{:S(2)}, u32[]{:S(2)}) %collective-permute-start.48) | collective-permute-done | bytes 262176 | tf_op jit(solution)/shard_map/ppermute | solution.py:941
  295.1 9.8 %attention_back.2 = (f32[128,1024]{1,0:T(8,128)S(1)}, bf16[128,1024]{1,0:T(8,128)(2,1)S(1)}, bf16[128,1024]{1,0:T(8,128)(2,1)S(1)}, bf16[128,1024]{1,0:T(8,128)(...) custom-call(bf16[128,1024]{1,0:T(8,128)(2,1)S(1)} %get-tuple-element.188.refs_0_, ...), custom_call_target="tpu_custom_call" | custom-call | tf_op jit(solution)/shard_map/attention_back/pallas_call | solution.py:172
  331.2 5.9 %collective-permute-done.56.refs_3_ = bf16[128,1024]{1,0:T(8,128)(2,1)S(1)} collective-permute-done((bf16[128,1024]{1,0:T(8,128)(2,1)S(1)}, bf16[128,1024]{1,0:T(8,128)(2,1)S(1)}, u32[]{:S(2)}, u32[]{:S(2)}) %collective-permute-start.56) | collective-permute-done | bytes 262176 | tf_op jit(solution)/shard_map/ppermute | solution.py:941
  337.2 6.1 %feed_back.3 = (f32[128,1024]{1,0:T(8,128)S(1)}, bf16[128,1024]{1,0:T(8,128)(2,1)S(1)}, bf16[128,1024]{1,0:T(8,128)(2,1)S(1)}, bf16[128,1024]{1,0:T(8,128)(2,1)S...) custom-call(bf16[128,1024]{1,0:T(8,128)(2,1)S(1)} %get-tuple-element.210.refs_0_, ...), custom_call_target="tpu_custom_call" | custom-call | tf_op jit(solution)/shard_map/feed_back/pallas_call | solution.py:172
  346.9 6.3 %feed_weights.3 = (bf16[4,128,1024]{2,1,0:T(8,128)(2,1)}, bf16[4,128,1024]{2,1,0:T(8,128)(2,1)}, bf16[4,128,1024]{2,1,0:T(8,128)(2,1)}, bf16[4,128,1024]{2,1,0:T(8,128)(2,1)}, f32[8,1024]{1,0:T(8,128)}) custom-call(bf16[512,1024]{1,0:T(8,128)(2,1)} %get-tuple-element.221.refs_0_.refs_1_, bf16[512,1024]{1,0:T(8,128)(2,1)} %get-tuple-element.222.refs_1_, ...), custom_call_target="tpu_custom_call" | custom-call | tf_op jit(solution)/shard_map/feed_weights/pallas_call | solution.py:172
  369.9 5.9 %collective-permute-done.63.refs_2_.refs_3_ = bf16[128,1024]{1,0:T(8,128)(2,1)S(1)} collective-permute-done((bf16[128,1024]{1,0:T(8,128)(2,1)S(1)}, bf16[128,1024]{1,0:T(8,128)(2,1)S(1)}, u32[]{:S(2)}, u32[]{:S(2)}) %collective-permute-start.63) | collective-permute-done | bytes 262176 | tf_op jit(solution)/shard_map/ppermute | solution.py:941
  380.8 9.7 %attention_back.3 = (f32[128,1024]{1,0:T(8,128)S(1)}, bf16[128,1024]{1,0:T(8,128)(2,1)S(1)}, bf16[128,1024]{1,0:T(8,128)(2,1)S(1)}, bf16[128,1024]{1,0:T(8,128)(...) custom-call(bf16[128,1024]{1,0:T(8,128)(2,1)S(1)} %get-tuple-element.227.refs_0_, ...), custom_call_target="tpu_custom_call" | custom-call | tf_op jit(solution)/shard_map/attention_back/pallas_call | solution.py:172
  430.8 9.2 %collective-permute-done.90 = bf16[128,1024]{1,0:T(8,128)(2,1)} collective-permute-done((bf16[128,1024]{1,0:T(8,128)(2,1)}, bf16[128,1024]{1,0:T(8,128)(2,1)}, u32[]{:S(2)}, u32[]{:S(2)}) %collective-permute-start.90) | collective-permute-done | bytes 262176 | tf_op jit(solution)/shard_map/ppermute | solution.py:941
  442.5 11.0 %collective-permute-start.70 = (bf16[144,1024]{1,0:T(8,128)(2,1)}, bf16[144,1024]{1,0:T(8,128)(2,1)S(1)}, u32[]{:S(2)}, u32[]{:S(2)}) collective-permute-start(bf16[144,1024]{1,0:T(8,128)(2,1)} %hold.44), channel_id=1, source_target_pairs={{0,2},{1,3},{2,0},{3,1},{4,6},{5,7},{6,4},{7,5},{8,10},{9,11},{10,... | collective-permute-start | bytes 884744 | tf_op jit(solution)/shard_map/ppermute | solution.py:941
  458.8 7.8 %collective-permute-done.70.refs_1_ = bf16[144,1024]{1,0:T(8,128)(2,1)S(1)} collective-permute-done((bf16[144,1024]{1,0:T(8,128)(2,1)}, bf16[144,1024]{1,0:T(8,128)(2,1)S(1)}, u32[]{:S(2)}, u32[]{:S(2)}) %collective-permute-start.70) | collective-permute-done | bytes 294944 | tf_op jit(solution)/shard_map/ppermute | solution.py:941
  491.6 14.9 %collective-permute-done.73.refs_2_ = bf16[128,1024]{1,0:T(8,128)(2,1)} collective-permute-done((bf16[128,1024]{1,0:T(8,128)(2,1)}, bf16[128,1024]{1,0:T(8,128)(2,1)}, u32[]{:S(2)}, u32[]{:S(2)}) %collective-permute-start.73) | collective-permute-done | bytes 262176 | tf_op jit(solution)/shard_map/ppermute | solution.py:941
  (382 shorter events, 321.7 us)
Async XLA Ops:
  7.2 57.8 %all-gather.11.cloned.1.call-start = ((), (), s32[]{:S(2)}) async-start(), calls=%async_computation.8 | async-start | bytes 1474560 | tf_op jit(solution)/shard_map/all_gather | solution.py:992
  25.5 87.7 %all-gather.13.cloned.1.call-start = ((), (), s32[]{:S(2)}) async-start(), calls=%async_computation.9 | async-start | bytes 1310720 | tf_op jit(solution)/shard_map/all_gather | solution.py:992
  63.8 77.4 %all-gather.15.cloned.1.call-start = ((), (), s32[]{:S(2)}) async-start(), calls=%async_computation.10 | async-start | bytes 1474560 | tf_op jit(solution)/shard_map/all_gather | solution.py:992
  64.9 120.6 %all-gather.17.cloned.1.call-start = ((), (), s32[]{:S(2)}) async-start(), calls=%async_computation.11 | async-start | bytes 1310720 | tf_op jit(solution)/shard_map/all_gather | solution.py:992
  80.1 23.9 %collective-permute-start.15 = (bf16[128,1024]{1,0:T(8,128)(2,1)S(1)}, bf16[128,1024]{1,0:T(8,128)(2,1)S(1)}, u32[]{:S(2)}, u32[]{:S(2)}) collective-permute-start(bf16[128,1024]{1,0:T(8,128)(2,1)S(1)} %get-tuple-element.283.refs_1_), channel_id=1, source_target_pairs={{0,1},{1,0},{2,3},{3,2},{4,5},{5,4},{6,7},{7,6},{8,9},{9,8},{10,11... | collective-permute-start | bytes 786440 | tf_op jit(solution)/shard_map/ppermute | solution.py:941
  80.1 27.2 %collective-permute-start.16 = (bf16[128,1024]{1,0:T(8,128)(2,1)S(1)}, bf16[128,1024]{1,0:T(8,128)(2,1)S(1)}, u32[]{:S(2)}, u32[]{:S(2)}) collective-permute-start(bf16[128,1024]{1,0:T(8,128)(2,1)S(1)} %get-tuple-element.283.refs_1_), channel_id=1, source_target_pairs={{0,2},{1,3},{2,0},{3,1},{4,6},{5,7},{6,4},{7,5},{8,10},{9,11},{10,... | collective-permute-start | bytes 786440 | tf_op jit(solution)/shard_map/ppermute | solution.py:941
  85.8 25.8 %collective-permute-start.17 = (bf16[128,1024]{1,0:T(8,128)(2,1)S(1)}, bf16[128,1024]{1,0:T(8,128)(2,1)S(1)}, u32[]{:S(2)}, u32[]{:S(2)}) collective-permute-start(bf16[128,1024]{1,0:T(8,128)(2,1)S(1)} %get-tuple-element.283.refs_1_), channel_id=1, source_target_pairs={{0,3},{1,2},{2,1},{3,0},{4,7},{5,6},{6,5},{7,4},{8,11},{9,10},{10,... | collective-permute-start | bytes 786440 | tf_op jit(solution)/shard_map/ppermute | solution.py:941
  107.3 88.8 %all-gather.19.cloned.1.call-start = ((), (), s32[]{:S(2)}) async-start(), calls=%async_computation.12 | async-start | bytes 1310720 | tf_op jit(solution)/shard_map/all_gather | solution.py:992
  141.3 195.9 %reduce-scatter.5.cloned.1.call-start = ((), (), s32[]{:S(2)}) async-start(), calls=%async_computation.4 | async-start | bytes 1310720 | tf_op jit(solution)/shard_map/reduce_scatter | solution.py:995
  235.0 36.4 %collective-permute-start.38 = (bf16[128,1024]{1,0:T(8,128)(2,1)S(1)}, bf16[128,1024]{1,0:T(8,128)(2,1)S(1)}, u32[]{:S(2)}, u32[]{:S(2)}) collective-permute-start(bf16[128,1024]{1,0:T(8,128)(2,1)S(1)} %get-tuple-element.280), channel_id=1, source_target_pairs={{0,0},{1,17},{2,6},{3,23},{4,1},{5,18},{6,7},{7,20},{8,8},{9,25},{... | collective-permute-start | bytes 786440 | tf_op jit(solution)/shard_map/ppermute | solution.py:941
  235.7 35.7 %collective-permute-start.39 = (bf16[128,1024]{1,0:T(8,128)(2,1)S(1)}, bf16[128,1024]{1,0:T(8,128)(2,1)S(1)}, u32[]{:S(2)}, u32[]{:S(2)}) collective-permute-start(bf16[128,1024]{1,0:T(8,128)(2,1)S(1)} %get-tuple-element.279), channel_id=1, source_target_pairs={{0,4},{1,21},{2,2},{3,19},{4,5},{5,22},{6,3},{7,16},{8,12},{9,29},... | collective-permute-start | bytes 786440 | tf_op jit(solution)/shard_map/ppermute | solution.py:941
  294.3 59.0 %reduce-scatter.7.cloned.1.call-start = ((), (), s32[]{:S(2)}) async-start(), calls=%async_computation.5 | async-start | bytes 1310720 | tf_op jit(solution)/shard_map/reduce_scatter | solution.py:995
  295.0 85.8 %reduce-scatter.9.cloned.1.call-start = ((), (), s32[]{:S(2)}) async-start(), calls=%async_computation.6 | async-start | bytes 1474560 | tf_op jit(solution)/shard_map/reduce_scatter | solution.py:995
  343.3 71.7 %reduce-scatter.11.cloned.1.call-start = ((), (), s32[]{:S(2)}) async-start(), calls=%async_computation.7 | async-start | bytes 1310720 | tf_op jit(solution)/shard_map/reduce_scatter | solution.py:995
  377.1 22.0 %collective-permute-start.88 = (bf16[4,128,1024]{2,1,0:T(8,128)(2,1)}, bf16[4,128,1024]{2,1,0:T(8,128)(2,1)S(1)}, u32[]{:S(2)}, u32[]{:S(2)}) collective-permute-start(bf16[4,128,1024]{2,1,0:T(8,128)(2,1)} %hold.50), channel_id=1, source_target_pairs={{0,8},{1,9},{2,10},{3,11},{4,12},{5,13},{6,14},{7,15},{8,0},{9,1},... | collective-permute-start | bytes 3145736 | tf_op jit(solution)/shard_map/ppermute | solution.py:941
  395.5 26.3 %collective-permute-start.68 = (bf16[4,144,1024]{2,1,0:T(8,128)(2,1)}, bf16[4,144,1024]{2,1,0:T(8,128)(2,1)S(1)}, u32[]{:S(2)}, u32[]{:S(2)}) collective-permute-start(bf16[4,144,1024]{2,1,0:T(8,128)(2,1)} %get-tuple-element.244), channel_id=1, source_target_pairs={{0,8},{1,9},{2,10},{3,11},{4,12},{5,13},{6,14},{7,15},{8,0},{9,1},... | collective-permute-start | bytes 3538952 | tf_op jit(solution)/shard_map/ppermute | solution.py:941
  415.1 24.9 %collective-permute-start.90 = (bf16[128,1024]{1,0:T(8,128)(2,1)}, bf16[128,1024]{1,0:T(8,128)(2,1)}, u32[]{:S(2)}, u32[]{:S(2)}) collective-permute-start(bf16[128,1024]{1,0:T(8,128)(2,1)} %hold.52), channel_id=1, source_target_pairs={{0,2},{1,3},{2,0},{3,1},{4,6},{5,7},{6,4},{7,5},{8,10},{9,11},{10,... | collective-permute-start | bytes 786440 | tf_op jit(solution)/shard_map/ppermute | solution.py:941
  416.9 25.7 %collective-permute-start.91 = (bf16[128,1024]{1,0:T(8,128)(2,1)}, bf16[128,1024]{1,0:T(8,128)(2,1)}, u32[]{:S(2)}, u32[]{:S(2)}) collective-permute-start(bf16[128,1024]{1,0:T(8,128)(2,1)} %hold.53), channel_id=1, source_target_pairs={{0,3},{1,2},{2,1},{3,0},{4,7},{5,6},{6,5},{7,4},{8,11},{9,10},{10,... | collective-permute-start | bytes 786440 | tf_op jit(solution)/shard_map/ppermute | solution.py:941
  420.3 33.2 %collective-permute-start.82 = (bf16[128,1024]{1,0:T(8,128)(2,1)}, bf16[128,1024]{1,0:T(8,128)(2,1)S(1)}, u32[]{:S(2)}, u32[]{:S(2)}) collective-permute-start(bf16[128,1024]{1,0:T(8,128)(2,1)} %hold.48.refs_1_), channel_id=1, source_target_pairs={{0,16},{1,17},{2,18},{3,19},{4,20},{5,21},{6,22},{7,23},{8,24},{9,... | collective-permute-start | bytes 786440 | tf_op jit(solution)/shard_map/ppermute | solution.py:941
  421.8 33.9 %collective-permute-start.81 = (bf16[128,1024]{1,0:T(8,128)(2,1)}, bf16[128,1024]{1,0:T(8,128)(2,1)S(1)}, u32[]{:S(2)}, u32[]{:S(2)}) collective-permute-start(bf16[128,1024]{1,0:T(8,128)(2,1)} %hold.49), channel_id=1, source_target_pairs={{0,4},{1,5},{2,6},{3,7},{4,0},{5,1},{6,2},{7,3},{8,12},{9,13},{10,... | collective-permute-start | bytes 786440 | tf_op jit(solution)/shard_map/ppermute | solution.py:941
  428.5 27.3 %collective-permute-start.83 = (bf16[128,1024]{1,0:T(8,128)(2,1)S(1)}, bf16[128,1024]{1,0:T(8,128)(2,1)S(1)}, u32[]{:S(2)}, u32[]{:S(2)}) collective-permute-start(bf16[128,1024]{1,0:T(8,128)(2,1)S(1)} %copy-done.40), channel_id=1, source_target_pairs={{0,20},{1,21},{2,22},{3,23},{4,16},{5,17},{6,18},{7,19},{8,28},{9,... | collective-permute-start | bytes 786440 | tf_op jit(solution)/shard_map/ppermute | solution.py:941
  442.5 24.1 %collective-permute-start.70 = (bf16[144,1024]{1,0:T(8,128)(2,1)}, bf16[144,1024]{1,0:T(8,128)(2,1)S(1)}, u32[]{:S(2)}, u32[]{:S(2)}) collective-permute-start(bf16[144,1024]{1,0:T(8,128)(2,1)} %hold.44), channel_id=1, source_target_pairs={{0,2},{1,3},{2,0},{3,1},{4,6},{5,7},{6,4},{7,5},{8,10},{9,11},{10,... | collective-permute-start | bytes 884744 | tf_op jit(solution)/shard_map/ppermute | solution.py:941
  479.2 27.4 %collective-permute-start.75 = (bf16[144,1024]{1,0:T(8,128)(2,1)S(1)}, bf16[144,1024]{1,0:T(8,128)(2,1)S(1)}, u32[]{:S(2)}, u32[]{:S(2)}) collective-permute-start(bf16[144,1024]{1,0:T(8,128)(2,1)S(1)} %broadcast_select_fusion.3.refs_1_), channel_id=1, source_target_pairs={{0,16},{1,17},{2,18},{3,19},{4,20},{5,21},{6,22},{7,23},{8,24},{9,... | collective-permute-start | bytes 884744 | tf_op jit(solution)/shard_map/ppermute | solution.py:941
  483.7 23.3 %collective-permute-start.76 = (bf16[144,1024]{1,0:T(8,128)(2,1)}, bf16[144,1024]{1,0:T(8,128)(2,1)S(1)}, u32[]{:S(2)}, u32[]{:S(2)}) collective-permute-start(bf16[144,1024]{1,0:T(8,128)(2,1)} %get-tuple-element.271), channel_id=1, source_target_pairs={{0,20},{1,21},{2,22},{3,23},{4,16},{5,17},{6,18},{7,19},{8,28},{9,... | collective-permute-start | bytes 884744 | tf_op jit(solution)/shard_map/ppermute | solution.py:941
  (130 other events, 1176.3 us)
Sparse Core Ops, SparseCore 0:
  25.6 38.3 all-gather.10
  65.5 38.3 all-gather.12
  105.5 30.0 all-gather.14
  137.0 26.8 all-gather.16
  165.3 27.4 all-gather.18
  294.4 27.9 reduce-scatter.4
  324.7 25.7 reduce-scatter.6
  352.9 27.8 reduce-scatter.8
  383.6 25.8 reduce-scatter.10
